TPU v7x, 128 devices: a whole 4x4x4 slice. The times are simulated.
128 devices in a mesh: fsdp: 16 (over y, x), tp: 8 (over z, core).
Axes of the slice: x: 4, y: 4, z: 4, core: 2. Of those that a mesh axis runs over, the one named last changes fastest.
Arguments:
- old_codes: bfloat16 [32768, 8192], P(('fsdp', 'tp')), may hold values from -448 to 448
- old_scales: bfloat16 [256, 64], P(('fsdp', 'tp')), may hold values from 4.9829483e-05 to 0.00049972534
- old_offsets: int32 [129], replicated, may hold values from 0 to 14336, as said below
- tokens: bfloat16 [4096, 8192], P('fsdp'), may hold values from -6 to 6
- cotangent: bfloat16 [4096, 14336], P('fsdp', 'tp'), may hold values from -0.1796875 to 0.1796875
Outputs:
- projected: bfloat16 [4096, 14336], P('fsdp', 'tp')
- grad: float32 [8192, 14336], P('fsdp', 'tp')
Inputs may be any that keep to these rules, and one draw needn't show every extreme that they name: old_offsets never falls, starts at 0, ends at 14336 and holds multiples of 128; owner o is the device at position o of fsdp+tp and holds saved rows old_offsets[o] to old_offsets[o + 1] - 1 in the first rows of its 256 rows of old_codes and its scales in the first rows of its 2 rows of old_scales; no owner holds more than 256 rows and some owner holds exactly 256; old_offsets[k * 16] = k * 1792 for every k.
All inputs are finite; a program needn't handle non-finite values.
Results may differ from a plain program's by a relative error of at most 0.0049.
Values may be sent and summed in bfloat16 or wider, within the bound.
No kernel may reach another device: no remote copies, remote signals or barrier semaphores. Data moves between devices by JAX's collectives and lax.ppermute only.
A program may use at most 192 MiB of HBM per device.

v0:
```python
import jax
import jax.numpy as jnp
from jax import lax
from jax.sharding import PartitionSpec as P


def on_device(old_codes, old_scales, old_offsets, tokens, cotangent):
    fsdp_count = lax.axis_size("fsdp")
    capacity = old_codes.shape[0]
    width = old_codes.shape[1]
    col_width = width // fsdp_count
    block_rows = old_scales.shape[0]
    block_size = capacity // block_rows
    col_blocks = col_width // block_size
    local_tokens = tokens.shape[0]
    local_hidden = cotangent.shape[1]
    outgoing = (
        old_codes.reshape(1, 1, capacity, fsdp_count, col_width),
        old_scales.reshape(1, 1, block_rows, fsdp_count, col_blocks),
    )
    codes_in, scales_in = (
        lax.all_to_all(
            lax.all_to_all(outgoing[0], "fsdp", split_axis=3, concat_axis=0, tiled=True),
            "tp",
            split_axis=0,
            concat_axis=1,
            tiled=True,
        ),
        lax.all_to_all(
            lax.all_to_all(outgoing[1], "fsdp", split_axis=3, concat_axis=0, tiled=True),
            "tp",
            split_axis=0,
            concat_axis=1,
            tiled=True,
        ),
    )
    codes_flat = codes_in.reshape(-1, col_width)
    scales_flat = scales_in.reshape(-1, col_blocks)
    tp_index = lax.axis_index("tp")
    row_ids = tp_index * local_hidden + jnp.arange(local_hidden, dtype=jnp.int32)
    starts = old_offsets[:-1]
    owner_ids = jnp.sum((starts[None, :] <= row_ids[:, None]).astype(jnp.int32), axis=1) - 1
    slot_ids = (owner_ids - tp_index * fsdp_count) * capacity + row_ids - old_offsets[owner_ids]
    picked = jnp.take(codes_flat, slot_ids, axis=0)
    picked_scales = jnp.take(scales_flat, slot_ids // block_size, axis=0)
    scaled = (
        picked.astype(jnp.float32).reshape(local_hidden, col_blocks, block_size)
        * picked_scales.astype(jnp.float32)[:, :, None]
    )
    weight = scaled.reshape(local_hidden, col_width).astype(jnp.bfloat16)
    exchanged = lax.all_to_all(
        tokens.reshape(local_tokens, fsdp_count, col_width),
        "fsdp",
        split_axis=1,
        concat_axis=0,
        tiled=True,
    )
    token_cols = exchanged.reshape(-1, col_width)
    token_part = tokens
    summed = lax.dot_general(
        token_part,
        lax.all_gather(weight, "fsdp", axis=1, tiled=True),
        (((1,), (1,)), ((), ())),
        preferred_element_type=jnp.float32,
    )
    projected = summed.astype(jnp.bfloat16)
    token_part = token_cols
    grad = lax.dot_general(
        token_part,
        lax.all_gather(cotangent, "fsdp", axis=0, tiled=True),
        (((0,), (0,)), ((), ())),
        preferred_element_type=jnp.float32,
    )
    return (projected, grad)


def solution(mesh):
    placed = (
        P(("fsdp", "tp"), None),
        P(("fsdp", "tp"), None),
        P(),
        P("fsdp", None),
        P("fsdp", "tp"),
    )
    return jax.shard_map(
        on_device,
        mesh=mesh,
        in_specs=placed,
        out_specs=(P("fsdp", "tp"), P("fsdp", "tp")),
        check_vma=False,
    )
```

profile of v0, /device:TPU:0, one launch (start us, length us, event | category | flops | bytes accessed | tf_op | source)
XLA Modules:
  0.0 453.0 jit_solution(12571463707577266851)
XLA Ops:
  7.2 0.0 all-gather.5.cloned.1.call-start
  7.2 0.7 all-gather.5.cloned.1.call-update
  7.9 0.7 reshape.186
  8.7 14.5 %all_to_all.81 = bf16[1,1,2,16,4]{4,2,1,0,3:T(2,128)(2,1)S(1)} all-to-all(bf16[1,1,2,16,4]{4,2,1,0,3:T(2,128)(2,1)S(1)} %copy.56), channel_id=1, replica_groups=mesh['fsdp'=16,'tp'=8] {'fsdp'}, dimensions={3} | all-to-all | bytes 512 | tf_op jit(solution)/shard_map/all_to_all | solution.py:30
  23.1 0.1 copy.57
  23.2 0.7 copy.58
  23.9 5.3 %all-to-all-start.3 = ((bf16[16,1,2,1,4]{4,2,3,1,0:T(2,128)(2,1)}), bf16[16,1,2,1,4]{4,2,3,1,0:T(2,128)(2,1)S(1)}, u32[]{:S(2)}, u32[]{:S(2)}) async-start(bf16[16,1,2,1,4]{4,2,3,1,0:T(2,128)(2,1)} %copy.58), calls=%async_computation.3 | async-start | bytes 16384 | tf_op jit(solution)/shard_map/all_to_all | solution.py:29
  29.3 6.4 %copy.51 = bf16[256,8192]{0,1:T(8,128)(2,1)} copy(bf16[256,8192]{1,0:T(8,128)(2,1)} %param.5) | data formatting | bytes 8388608 | tf_op args[0]
  35.7 0.0 all-to-all-done.3
  35.7 92.5 %all_to_all.82 = bf16[1,1,256,16,512]{2,4,1,0,3:T(8,128)(2,1)} all-to-all(bf16[1,1,256,16,512]{2,4,1,0,3:T(8,128)(2,1)} %bitcast.42), channel_id=1, replica_groups=mesh['fsdp'=16,'tp'=8] {'fsdp'}, dimensions={3} | all-to-all | bytes 8388608 | tf_op jit(solution)/shard_map/all_to_all | solution.py:23
  128.2 0.0 slice-start
  128.2 0.0 copy-start
  128.2 5.0 %all-to-all-start.1 = ((bf16[16,1,256,1,512]{2,4,3,1,0:T(8,128)(2,1)}), bf16[16,1,256,1,512]{2,4,3,1,0:T(8,128)(2,1)}, u32[]{:S(2)}, u32[]{:S(2)}) async-start(bf16[16,1,256,1,512]{2,4,3,1,0:T(8,128)(2,1)} %bitcast.41), calls=%async_computation.1 | async-start | bytes 8388608 | tf_op jit(solution)/shard_map/all_to_all | solution.py:22
  133.2 0.0 all-gather.3.cloned.1.call-start
  133.3 0.0 slice-done
  133.3 0.6 convert_reduce_fusion
  133.9 0.0 copy-done
  133.9 10.9 %gather_fusion = s32[1792]{0:T(1024)S(1)} fusion(s32[129]{0:T(256)S(1)} %copy-done, s32[2048]{0:T(1024)S(1)} %pad_clamp_fusion.2), kind=kCustom, calls=%fused_computation | custom fusion | bytes 21504 | tf_op jit(solution)/shard_map/gather | solution.py:43
  144.8 0.1 fusion.4
  145.0 3.7 gather_fusion.2
  148.8 0.3 select_convert_fusion
  149.1 33.9 %all-to-all-done.1 = bf16[16,1,256,1,512]{2,4,3,1,0:T(8,128)(2,1)} async-done(((bf16[16,1,256,1,512]{2,4,3,1,0:T(8,128)(2,1)}), bf16[16,1,256,1,512]{2,4,3,1,0:T(8,128)(2,1)}, u32[]{:S(2)}, u32[]{:S(2)}) %all-to-all-start.1) | async-done | bytes 4194336 | tf_op jit(solution)/shard_map/all_to_all | solution.py:22
  183.0 6.5 %copy.54 = bf16[16,1,256,1,512]{4,2,0,3,1:T(8,128)(2,1)} copy(bf16[16,1,256,1,512]{2,4,3,1,0:T(8,128)(2,1)} %all-to-all-done.1) | data formatting | bytes 8388608 | tf_op jit(solution)/shard_map/all_to_all | solution.py:22
  189.5 4.5 copy.55
  193.9 8.3 %gather_fusion.1 = bf16[1792,512]{1,0:T(8,128)(2,1)S(1)} fusion(bf16[4096,512]{1,0:T(8,128)(2,1)} %bitcast.40, s32[2048]{0:T(1024)S(1)} %get-tuple-element.21), kind=kCustom, calls=%fused_computation.1 | custom fusion | bytes 3677184 | tf_op jit(solution)/shard_map/jit(_take)/gather | solution.py:44
  202.3 2.2 mul.48
  204.4 2.3 fusion
  206.7 0.0 all-gather.3.cloned.1.call-update
  206.7 6.5 %copy.61 = bf16[256,8192]{0,1:T(8,128)(2,1)} copy(bf16[256,8192]{1,0:T(8,128)(2,1)} %param.8) | data formatting | bytes 8388608 | tf_op args[3]
  213.2 81.2 %all_to_all.83 = bf16[256,16,512]{0,2,1:T(8,128)(2,1)} all-to-all(bf16[256,16,512]{0,2,1:T(8,128)(2,1)} %bitcast.45), channel_id=1, replica_groups=mesh['fsdp'=16,'tp'=8] {'fsdp'}, dimensions={1} | all-to-all | bytes 8388608 | tf_op jit(solution)/shard_map/all_to_all | solution.py:51
  294.4 6.4 %copy.62 = bf16[16,256,1,512]{3,1,0,2:T(8,128)(2,1)} copy(bf16[16,256,1,512]{1,3,0,2:T(8,128)(2,1)} %bitcast.44) | data formatting | bytes 8388608 | tf_op jit(solution)/shard_map/all_to_all | solution.py:51
  300.8 0.0 all-gather.5.cloned.1.call-done
  300.8 14.7 %fusion.7 = f32[512,1792]{1,0:T(8,128)} fusion(bf16[4096,512]{1,0:T(8,128)(2,1)} %bitcast.47, bf16[4096,1792]{1,0:T(8,128)(2,1)} %all-gather.5.cloned.1.call-done), kind=kOutput, calls=%fused_computation.38 | convolution fusion | flops 7516192768 | bytes 22544384 | tf_op jit(solution)/shard_map/dot_general | solution.py:68
  315.5 114.7 %all-gather.3.cloned.1.call-done = bf16[1792,8192]{1,0:T(8,128)(2,1)} async-done(((bf16[1792,512]{1,0:T(8,128)(2,1)}), bf16[1792,8192]{1,0:T(8,128)(2,1)}) %all-gather.3.cloned.1.call-update) | async-done | bytes 29360144 | tf_op jit(solution)/shard_map/all_gather | solution.py:62
  430.2 14.5 %fusion.1 = bf16[256,1792]{0,1:T(8,128)(2,1)S(1)} fusion(bf16[1792,8192]{1,0:T(8,128)(2,1)} %all-gather.3.cloned.1.call-done, bf16[256,8192]{1,0:T(8,128)(2,1)} %param.8), kind=kOutput, calls=%fused_computation.6 | convolution fusion | flops 7516651520 | bytes 34471936 | tf_op jit(solution)/shard_map/dot_general | solution.py:60
  444.7 1.4 copy.63
  (9 shorter events, 0.1 us)
Async XLA Ops:
  7.2 293.6 %all-gather.5.cloned.1.call-start = ((), (), s32[]{:S(2)}) async-start(), calls=%async_computation.6 | async-start | bytes 15597568 | tf_op jit(solution)/shard_map/all_gather | solution.py:70
  23.9 11.7 %all-to-all-start.3 = ((bf16[16,1,2,1,4]{4,2,3,1,0:T(2,128)(2,1)}), bf16[16,1,2,1,4]{4,2,3,1,0:T(2,128)(2,1)S(1)}, u32[]{:S(2)}, u32[]{:S(2)}) async-start(bf16[16,1,2,1,4]{4,2,3,1,0:T(2,128)(2,1)} %copy.58), calls=%async_computation.3 | async-start | bytes 16384 | tf_op jit(solution)/shard_map/all_to_all | solution.py:29
  128.2 5.1 %slice-start = ((s32[129]{0:T(256)}), s32[128]{0:T(128)S(1)}, s32[]{:S(2)}) async-start(s32[129]{0:T(256)} %param.7), calls=%async_computation.7 | async-start | bytes 1024 | tf_op jit(solution)/shard_map/slice | solution.py:41
  128.2 5.7 %copy-start = (s32[129]{0:T(256)S(1)}, s32[129]{0:T(256)}, u32[]{:S(2)}) copy-start(s32[129]{0:T(256)} %param.7) | copy-start | bytes 1552
  128.2 54.8 %all-to-all-start.1 = ((bf16[16,1,256,1,512]{2,4,3,1,0:T(8,128)(2,1)}), bf16[16,1,256,1,512]{2,4,3,1,0:T(8,128)(2,1)}, u32[]{:S(2)}, u32[]{:S(2)}) async-start(bf16[16,1,256,1,512]{2,4,3,1,0:T(8,128)(2,1)} %bitcast.41), calls=%async_computation.1 | async-start | bytes 8388608 | tf_op jit(solution)/shard_map/all_to_all | solution.py:22
  133.2 297.0 %all-gather.3.cloned.1.call-start = ((), (), s32[]{:S(2)}) async-start(), calls=%async_computation.5 | async-start | bytes 31195136 | tf_op jit(solution)/shard_map/all_gather | solution.py:62
Sparse Core Ops, SparseCore 0:
  10.1 138.7 all-gather.4
  206.9 223.2 all-gather.2
where the time goes:
time: 454 us; the launch traced here: 453 us
  blocking collectives  188 us (41%)
  waiting for transfers between devices  149 us (33%)
  local copies, waits for them, and re-layouts  58.3 us (13%)
  matrix products  29.3 us (6%)
  between operations  14.2 us (3%)
  starting transfers between devices  10.4 us (2%)
    all_gather x1, waiting for transfers between devices, on_device(): lax.all_gather(weight, 'fsdp', axis=1, tiled=True)  115 us
    all_to_all x1, blocking collectives, on_device(): lax.all_to_all(outgoing[0], 'fsdp', split_axis=3, concat_axis=0, tiled=True)  92.5 us
    all_to_all x1, blocking collectives, on_device(): lax.all_to_all(tokens.reshape(local_tokens, fsdp_count, col_width), 'fsdp...  81.2 us
    all_to_all x1, waiting for transfers between devices, on_device(): lax.all_to_all(lax.all_to_all(outgoing[0], 'fsdp', split_axis=3, concat_a...  33.9 us
    dot_general x1, matrix products, on_device(): lax.dot_general(token_part, lax.all_gather(cotangent, 'fsdp', axis=0, til...  14.7 us
    dot_general x1, matrix products, on_device(): lax.dot_general(token_part, lax.all_gather(weight, 'fsdp', axis=1, tiled=...  14.5 us
    all_to_all x1, blocking collectives, on_device(): lax.all_to_all(outgoing[1], 'fsdp', split_axis=3, concat_axis=0, tiled=True)  14.5 us
    unnamed x5, local copies, waits for them, and re-layouts  14.3 us
  transfers between devices with their start and end apart: 4, of which 2 were waited for; matrix products, arithmetic and copies ran while one was open for 17% of the time, Pallas kernels for 0%

commit v1 on v0

v1 whole, which is shorter than its diff:
```python
import math

import jax
import jax.numpy as jnp
from jax import lax
from jax.experimental import pallas as pl
from jax.experimental.pallas import tpu as pltpu
from jax.sharding import Mesh, PartitionSpec as P

AXES = ("y", "x", "z", "c")
RING = 4
NEAR_LAST = (2, 1, 3)
PARAMS = pltpu.CompilerParams(vmem_limit_bytes=56 << 20)


def swap(array, axis, s):
    return lax.ppermute(array, axis, [(i, i ^ s) for i in range(RING)])


def exchange(parts, axis):
    got = [parts[0]] + [None] * (RING - 1)
    for s in NEAR_LAST:
        got[s] = swap(parts[s], axis, s)
    return got


def pick(array, index, axis=0):
    return lax.dynamic_index_in_dim(array, index, axis, keepdims=False)


def all_to_all(array, axis):
    return lax.all_to_all(array, axis, 0, 0, tiled=True)


def cut_kernel(place_ref, tokens_ref, out_ref):
    part = out_ref.shape[2]
    for x in range(RING):
        out_ref[x] = tokens_ref[:, x * part:(x + 1) * part]


def cut_tokens(tokens, c):
    rows, width = tokens.shape
    quarter = width // RING
    part = quarter // RING
    return pl.pallas_call(
        cut_kernel,
        grid_spec=pltpu.PrefetchScalarGridSpec(
            num_scalar_prefetch=1,
            grid=(RING,),
            in_specs=[pl.BlockSpec((rows // 2, quarter), lambda q, place: (place[0], q))],
            out_specs=pl.BlockSpec((RING, rows // 2, part), lambda q, place: (0, 0, q)),
        ),
        out_shape=jax.ShapeDtypeStruct((RING, rows // 2, quarter), tokens.dtype),
        compiler_params=PARAMS,
        name="cut_tokens",
    )(c[None], tokens)


def dequantize_kernel(place_ref, codes_ref, scales_ref, first_ref, *second_refs):
    step = pl.program_id(0)
    part = first_ref.shape[-1]
    block = first_ref.shape[-2]

    def values(slot, x):
        cols = slice(x * part, (x + 1) * part)
        codes = codes_ref[slot * block:(slot + 1) * block, cols].astype(jnp.float32)
        return (codes * scales_ref[slot:slot + 1, cols]).astype(jnp.bfloat16)

    for x in range(RING):
        first_ref[x, 0] = values(0, x)
    for s, ref in enumerate(second_refs):
        @pl.when(step == s)
        def _():
            for x in range(RING):
                ref[x] = values(1, x)


def dequantize(codes, scales, z):
    capacity, width = codes.shape
    slots, col_blocks = scales.shape
    block = capacity // slots
    quarter = width // RING
    part = quarter // RING
    spread = jnp.repeat(scales.astype(jnp.float32), width // col_blocks, axis=1)
    return pl.pallas_call(
        dequantize_kernel,
        grid_spec=pltpu.PrefetchScalarGridSpec(
            num_scalar_prefetch=1,
            grid=(RING,),
            in_specs=[
                pl.BlockSpec((capacity, quarter), lambda i, place: (0, place[0] ^ i)),
                pl.BlockSpec((slots, quarter), lambda i, place: (0, place[0] ^ i)),
            ],
            out_specs=[pl.BlockSpec((RING, 1, block, part), lambda i, place: (0, place[0] ^ i, 0, 0))]
            + [pl.BlockSpec((RING, block, part), lambda i, place: (0, 0, 0))] * RING,
        ),
        out_shape=[jax.ShapeDtypeStruct((RING, RING, block, part), jnp.bfloat16)]
        + [jax.ShapeDtypeStruct((RING, block, part), jnp.bfloat16)] * RING,
        compiler_params=PARAMS,
        name="dequantize",
    )(z[None], codes, spread)


def gather_kernel(kind_ref, index_ref, half_ref, *refs):
    sources, outs = refs[:6], refs[6:10]
    rows = math.gcd(outs[0].shape[0], sources[0].shape[1])
    count = outs[0].shape[0] // rows
    for s, out_ref in enumerate(outs):
        for i in range(count):
            n = s * count + i
            half = pl.ds(pl.multiple_of(half_ref[n] * rows, rows), rows)
            for kind, source in enumerate(sources):
                @pl.when(kind_ref[n] == kind)
                def _():
                    out_ref[i * rows:(i + 1) * rows, :] = source[index_ref[n], half, :]


def gather(kind, index, half, sources, hidden):
    part = sources[0].shape[-1]
    return pl.pallas_call(
        gather_kernel,
        grid_spec=pltpu.PrefetchScalarGridSpec(
            num_scalar_prefetch=3,
            grid=(1,),
            in_specs=[pl.BlockSpec(a.shape, lambda i, *_: (0, 0, 0)) for a in sources],
            out_specs=[pl.BlockSpec((hidden, part), lambda i, *_: (0, 0))] * RING,
        ),
        out_shape=[jax.ShapeDtypeStruct((hidden, part), sources[0].dtype)] * RING,
        compiler_params=PARAMS,
        name="gather_blocks",
    )(kind, index, half, *sources)


def weight_rows(old_codes, old_scales, old_offsets, local_hidden, cot):
    y, x, z, c = (lax.axis_index(a) for a in AXES)
    owners = RING * RING
    slots = old_scales.shape[0]
    block = old_codes.shape[0] // slots
    hidden = local_hidden // RING
    first, *second = dequantize(old_codes, old_scales, z)
    part = first.shape[-1]

    second = jnp.stack(exchange(second, "z"), axis=1)
    first = all_to_all(first, "x")
    firsts = exchange([pick(first, z ^ s, 1) for s in range(RING)], "z")
    second = all_to_all(second, "x")
    second, cot = lax.optimization_barrier((second, cot))
    give = [lax.dynamic_slice_in_dim(a, 2 * (1 - c), 2, 0) for a in firsts]
    give = give + [lax.dynamic_slice_in_dim(second, 2 * (1 - c), 2, 0).reshape(2 * RING, block, part)]
    other = lax.ppermute(jnp.concatenate(give), "c", [(0, 1), (1, 0)])

    group = 2 * y + c
    rows = math.gcd(hidden, block)
    count = hidden // rows
    n = jnp.arange(RING * count, dtype=jnp.int32)
    row = group * local_hidden + (z ^ (n // count)) * hidden + rows * (n % count)
    starts = old_offsets[:-1]
    before = (starts[None, :] <= row[:, None]).astype(jnp.int32)
    owner = jnp.sum(before, axis=1) - 1
    start = jnp.max(jnp.where(before == 1, starts[None, :], 0), axis=1)
    member = owner - group * owners
    low, zs, cs = member >> 3, (member >> 1) & 3, member & 1
    slot = (row - start) // block
    half = (row - start) % block // rows
    s = zs ^ z
    kind = jnp.where(cs != c, RING + 1, jnp.where(slot == 0, s, RING))
    index = jnp.where(
        cs != c,
        jnp.where(slot == 0, s * 2 + low, 2 * RING + low * RING + s),
        jnp.where(slot == 0, 2 * c + low, (2 * c + low) * RING + s),
    )
    sources = firsts + [second.reshape(owners, block, part), other]
    return gather(kind, index, half, sources, hidden), cot


def project_kernel(place_ref, tokens_ref, *refs):
    out_ref = refs[-1]
    pieces, hidden, share = out_ref.shape
    total = None
    for s, weight_ref in enumerate(refs[:-1]):
        part = weight_ref.shape[1]
        start = pl.multiple_of((place_ref[1] ^ s) * part, part)
        rows = tokens_ref[:, 0, :, pl.ds(start, part)].reshape(pieces * share, part)
        product = lax.dot_general(
            weight_ref[...], rows, (((1,), (1,)), ((), ())), preferred_element_type=jnp.float32
        )
        total = product if total is None else total + product
    for i in range(pieces):
        out_ref[i] = total[:, i * share:(i + 1) * share].astype(out_ref.dtype)


def project(tokens, weights, x, z):
    pieces, _, share, quarter = tokens.shape
    steps = 2
    hidden, part = weights[0].shape
    rows = pieces * share // RING
    return pl.pallas_call(
        project_kernel,
        grid_spec=pltpu.PrefetchScalarGridSpec(
            num_scalar_prefetch=1,
            grid=(steps,),
            in_specs=[
                pl.BlockSpec((pieces // steps, 1, share, quarter), lambda i, place: (i, place[0], 0, 0))
            ]
            + [pl.BlockSpec((hidden, part), lambda i, place: (0, 0))] * RING,
            out_specs=pl.BlockSpec((RING // steps, hidden, rows), lambda i, place: (i, 0, 0)),
        ),
        out_shape=jax.ShapeDtypeStruct((RING, hidden, rows), jnp.bfloat16),
        compiler_params=PARAMS,
        name="project",
    )(jnp.stack([x, z]), tokens, *weights)


def grad_kernel(place_ref, tokens_ref, *refs):
    cots, outs, total_ref, cot_ref = refs[:RING], refs[RING:2 * RING], refs[2 * RING], refs[2 * RING + 1]
    step = pl.program_id(0)
    rows = cots[0].shape[2]
    part = outs[0].shape[1]
    for s, ref in enumerate(cots):
        @pl.when(step == s)
        def _():
            for t in range(RING):
                start = pl.multiple_of((place_ref[0] ^ t) * rows, rows)
                cot_ref[:, pl.ds(start, rows)] = ref[t]
    product = lax.dot_general(
        cot_ref[...], tokens_ref[...].reshape(cot_ref.shape[1], tokens_ref.shape[-1]),
        (((1,), (0,)), ((), ())), preferred_element_type=jnp.float32,
    )

    @pl.when(step == 0)
    def _():
        total_ref[...] = product

    @pl.when(step > 0)
    def _():
        total_ref[...] += product

    @pl.when(step == pl.num_programs(0) - 1)
    def _():
        for s, ref in enumerate(outs):
            start = pl.multiple_of((place_ref[0] ^ s) * part, part)
            ref[...] = total_ref[:, pl.ds(start, part)].astype(ref.dtype)


def gradient(tokens, cots, y, x):
    pieces, _, share, quarter = tokens.shape
    part = quarter // RING
    _, hidden, rows = cots[0].shape
    return pl.pallas_call(
        grad_kernel,
        grid_spec=pltpu.PrefetchScalarGridSpec(
            num_scalar_prefetch=1,
            grid=(RING,),
            in_specs=[pl.BlockSpec((pieces, 1, share, quarter), lambda i, place: (0, place[1] ^ i, 0, 0))]
            + [pl.BlockSpec((RING, hidden, rows), lambda i, place: (0, 0, 0))] * RING,
            out_specs=[pl.BlockSpec((hidden, part), lambda i, place: (0, 0))] * RING,
            scratch_shapes=[
                pltpu.VMEM((hidden, quarter), jnp.float32),
                pltpu.VMEM((hidden, RING * rows), jnp.bfloat16),
            ],
        ),
        out_shape=[jax.ShapeDtypeStruct((hidden, part), jnp.bfloat16)] * RING,
        compiler_params=PARAMS,
        name="gradient",
    )(jnp.stack([y, x]), tokens, *cots)


def assemble_kernel(place_ref, *refs):
    pieces, out_ref, all_ref = refs[:RING], refs[RING], refs[RING + 1]
    hidden = pieces[0].shape[0]
    for s, ref in enumerate(pieces):
        start = pl.multiple_of((place_ref[0] ^ s) * hidden, hidden)
        all_ref[pl.ds(start, hidden), :] = ref[...].astype(jnp.float32)
    out_ref[...] = all_ref[...].T.astype(out_ref.dtype)


def assemble(pieces, me, dtype):
    hidden, rows = pieces[0].shape
    lanes = min(rows, 128)
    return pl.pallas_call(
        assemble_kernel,
        grid_spec=pltpu.PrefetchScalarGridSpec(
            num_scalar_prefetch=1,
            grid=(rows // lanes,),
            in_specs=[pl.BlockSpec((hidden, lanes), lambda i, place: (0, i))] * RING,
            out_specs=pl.BlockSpec((lanes, RING * hidden), lambda i, place: (i, 0)),
            scratch_shapes=[pltpu.VMEM((RING * hidden, lanes), jnp.float32)],
        ),
        out_shape=jax.ShapeDtypeStruct((rows, RING * hidden), dtype),
        compiler_params=PARAMS,
        name="assemble",
    )(me[None], *pieces)


def on_device(old_codes, old_scales, old_offsets, tokens, cotangent):
    y, x, z, c = (lax.axis_index(a) for a in AXES)
    local_tokens, width = tokens.shape
    local_hidden = cotangent.shape[1]
    hidden = local_hidden // RING

    with jax.named_scope("tokens"):
        every = lax.all_gather(all_to_all(cut_tokens(tokens, c), "x"), ("y", "c"))

    with jax.named_scope("cotangent"):
        cut = cotangent.T.reshape(RING, hidden, local_tokens)
        cot = jnp.stack(exchange([pick(cut, y ^ s) for s in range(RING)], "y"))

    with jax.named_scope("weight"):
        weights, cot = weight_rows(old_codes, old_scales, old_offsets, local_hidden, cot)
        weights = exchange(weights, "z")

    with jax.named_scope("grad"):
        cots = exchange([cot] * RING, "x")
        grad = assemble(exchange(gradient(every, cots, y, x), "y"), y, jnp.float32)

    with jax.named_scope("projected"):
        parts = [None] * RING
        for s in NEAR_LAST:
            parts[s] = swap(project(every, weights, x ^ s, z), "x", s)
        parts[0] = project(every, weights, x, z)
        total = sum(p.astype(jnp.float32) for p in parts).astype(jnp.bfloat16)
        done = []
        for s in range(RING):
            pairs = [(a * RING + b, (b ^ s) * RING + a) for a in range(RING) for b in range(RING)]
            done.append(lax.ppermute(pick(total, z ^ s), ("y", "z"), pairs))
        projected = assemble(done, y, jnp.bfloat16)
    return (projected, grad)


def solution(mesh):
    devices = mesh.devices.reshape(RING, RING, RING, 2)
    split = Mesh(devices, AXES)
    fsdp, tp = ("y", "x"), ("z", "c")
    placed = (P(fsdp + tp, None), P(fsdp + tp, None), P(), P(fsdp, None), P(fsdp, tp))
    return jax.shard_map(
        on_device,
        mesh=split,
        in_specs=placed,
        out_specs=(P(fsdp, tp), P(fsdp, tp)),
        check_vma=False,
    )
```

time: 454 us -> 289 us (0.64)
  blocking collectives: 188 us -> 30.9 us
  Pallas kernels: 0 us -> 61.5 us
  waiting for transfers between devices: 149 us -> 99.2 us
  starting transfers between devices: 10.4 us -> 53.1 us
  local copies, waits for them, and re-layouts: 58.3 us -> 20.9 us
  matrix products: 29.3 us -> 0 us
  other arithmetic: 3.31 us -> 8.29 us
    all_to_all x3 -> x1, blocking collectives: 188 us -> 30.9 us  [all_to_all(): return lax.all_to_all(array, axis, 0, 0, tiled=True)]
    all_gather x2 -> x1, waiting for transfers between devices: 115 us -> 0.01 us  [on_device(): every = lax.all_gather(all_to_all(cut_tokens(tokens, c), 'x'), ('y', 'c'))]
    ppermute x0 -> x26, waiting for transfers between devices: none -> 99.2 us  [the longest x21 98.4 us: swap(): return lax.ppermute(array, axis, [(i, i ^ s) for i in range(RING)])]
    pallas_call x0 -> x10, Pallas kernels: none -> 61.5 us  [the longest x4 23.4 us: project(): pl.pallas_call(project_kernel, grid_spec=pltpu.PrefetchScalarGridSpec(num...]
    ppermute x0 -> x26, starting transfers between devices: none -> 44.9 us  [the longest x21 38.2 us: swap(): return lax.ppermute(array, axis, [(i, i ^ s) for i in range(RING)])]
    all_to_all x2, waiting for transfers between devices: 33.9 us -> 0.01 us  [all_to_all(): return lax.all_to_all(array, axis, 0, 0, tiled=True)]
    dot_general x2 -> x0, matrix products: 29.3 us -> none  [the longest x1 14.7 us: on_device(): lax.dot_general(token_part, lax.all_gather(cotangent, 'fsdp', axis=0, til...]
    gather x3 -> x0, local copies, waits for them, and re-layouts: 23 us -> none  [the longest x1 10.9 us: on_device(): old_offsets[owner_ids]]
  transfers between devices with their start and end apart: 4 -> 29, of which waited for: 2 -> 12; matrix products, arithmetic and copies ran while one was open for 17% -> 8% of each run, Pallas kernels for 0% -> 19%
where the time goes in v1:
time: 289 us; the launch traced here: 288 us
  waiting for transfers between devices  99.2 us (34%)
  Pallas kernels  61.5 us (21%)
  starting transfers between devices  53.1 us (18%)
  blocking collectives  30.9 us (11%)
  local copies, waits for them, and re-layouts  20.9 us (7%)
  between operations  14.3 us (5%)
  other arithmetic  8.29 us (3%)
    ppermute x21, waiting for transfers between devices, swap(): return lax.ppermute(array, axis, [(i, i ^ s) for i in range(RING)])  98.4 us
    ppermute x21, starting transfers between devices, swap(): return lax.ppermute(array, axis, [(i, i ^ s) for i in range(RING)])  38.2 us
    all_to_all x1, blocking collectives, all_to_all(): return lax.all_to_all(array, axis, 0, 0, tiled=True)  30.9 us
    pallas_call x4, Pallas kernels, project(): pl.pallas_call(project_kernel, grid_spec=pltpu.PrefetchScalarGridSpec(num...  23.4 us
    pallas_call x1, Pallas kernels, gradient(): pl.pallas_call(grad_kernel, grid_spec=pltpu.PrefetchScalarGridSpec(num_sc...  15.6 us
    unnamed x48, local copies, waits for them, and re-layouts  12.7 us
    all_to_all x2, starting transfers between devices, all_to_all(): return lax.all_to_all(array, axis, 0, 0, tiled=True)  8.13 us
    pallas_call x2, Pallas kernels, assemble(): pl.pallas_call(assemble_kernel, grid_spec=pltpu.PrefetchScalarGridSpec(nu...  7.21 us
  transfers between devices with their start and end apart: 29, of which 12 were waited for; matrix products, arithmetic and copies ran while one was open for 8% of the time, Pallas kernels for 19%

profile of v1, /device:TPU:0, one launch (start us, length us, event | category | flops | bytes accessed | tf_op | source)
XLA Modules:
  0.0 288.1 jit_solution(4247894132905964225)
XLA Ops:
  7.2 3.8 %cut_tokens.1 = bf16[4,128,2048]{2,1,0:T(8,128)(2,1)} custom-call(s32[1]{0:T(128)} %bitcast.3.place_ref, bf16[256,8192]{1,0:T(8,128)(2,1)} %tokens_ref.1), custom_call_target="tpu_custom_call" | custom-call | tf_op jit(solution)/shard_map/tokens/cut_tokens/pallas_call | solution.py:45
  11.0 30.9 %all_to_all.15 = bf16[4,128,2048]{2,1,0:T(8,128)(2,1)} all-to-all(bf16[4,128,2048]{2,1,0:T(8,128)(2,1)} %cut_tokens.1), channel_id=1, replica_groups=mesh['y'=4,'x'=4,'z'=4,'c'=2] {'x'}, dimensions={0} | all-to-all | bytes 4194304 | tf_op jit(solution)/shard_map/tokens/all_to_all | solution.py:32
  42.0 0.6 copy-done.20
  42.7 0.7 copy.16
  43.3 5.2 %dequantize.1 = (bf16[4,4,128,512]{3,2,1,0:T(8,128)(2,1)}, bf16[4,128,512]{2,1,0:T(8,128)(2,1)}, bf16[4,128,512]{2,1,0:T(8,128)(2,1)}, bf16[4,128,512]{2,1,0:T(8,128)(2,1)}, bf16[4,128,512]{2,1,0:T(8,128)(2,1)}) custom-call(s32[1]{0:T(128)} %bitcast.2.place_ref, bf16[256,8192]{1,0:T(8,128)(2,1)} %codes_ref.1, f32[2,8192]{1,0:T(2,128)} %bitcast.61), custom_call_target="tpu_custom_call" | custom-call | tf_op jit(solution)/shard_map/weight/dequantize/pallas_call | solution.py:85
  48.5 3.8 %all-to-all-start.1 = ((bf16[4,4,128,512]{3,2,1,0:T(8,128)(2,1)}), bf16[4,4,128,512]{3,2,1,0:T(8,128)(2,1)S(1)}, u32[]{:S(2)}, u32[]{:S(2)}) async-start(bf16[4,4,128,512]{3,2,1,0:T(8,128)(2,1)} %get-tuple-element.17), calls=%async_computation.1 | async-start | bytes 4194304 | tf_op jit(solution)/shard_map/weight/all_to_all | solution.py:32
  52.4 4.4 %collective-permute-start.5 = (bf16[4,128,512]{2,1,0:T(8,128)(2,1)}, bf16[4,128,512]{2,1,0:T(8,128)(2,1)S(1)}, u32[]{:S(2)}, u32[]{:S(2)}) collective-permute-start(bf16[4,128,512]{2,1,0:T(8,128)(2,1)} %get-tuple-element.21), channel_id=1, source_target_pairs={{0,6},{2,4},{4,2},{6,0},{1,7},{3,5},{5,3},{7,1},{8,14},{10,12},{12... | collective-permute-start | bytes 1572872 | tf_op jit(solution)/shard_map/weight/ppermute | solution.py:17
  56.7 0.9 collective-permute-start.3
  57.7 21.2 %collective-permute-done.5 = bf16[4,128,512]{2,1,0:T(8,128)(2,1)S(1)} collective-permute-done((bf16[4,128,512]{2,1,0:T(8,128)(2,1)}, bf16[4,128,512]{2,1,0:T(8,128)(2,1)S(1)}, u32[]{:S(2)}, u32[]{:S(2)}) %collective-permute-start.5) | collective-permute-done | bytes 524320 | tf_op jit(solution)/shard_map/weight/ppermute | solution.py:17
  78.9 0.7 collective-permute-done.3
  79.8 1.6 copy.12
  81.4 1.3 copy-done.1
  82.7 4.3 %all-to-all-start.2 = ((bf16[4,4,128,512]{3,2,1,0:T(8,128)(2,1)}), bf16[4,4,128,512]{3,2,1,0:T(8,128)(2,1)S(1)}, u32[]{:S(2)}, u32[]{:S(2)}) async-start(bf16[4,4,128,512]{3,2,1,0:T(8,128)(2,1)} %copy.12), calls=%async_computation.2 | async-start | bytes 4194304 | tf_op jit(solution)/shard_map/weight/all_to_all | solution.py:32
  87.0 1.6 copy.13
  88.7 3.0 %dynamic-slice_bitcast_fusion = (bf16[4,128,512]{2,1,0:T(8,128)(2,1)}, bf16[4,128,512]{2,1,0:T(8,128)(2,1)}, bf16[4,128,512]{2,1,0:T(8,128)(2,1)}, bf16[4,128,512]{2,1,0:T(8,128)(2,1)}) fusion(bf16[4,4,128,512]{3,2,1,0:T(8,128)(2,1)} %copy-done.1, s32[]{:T(128)S(6)} %select_n.106, s32[]{:T(128)S(6)} %select_n.105, s32[]{:T(128)S(6)} %select_n.104, ...), kind=kLoop, calls=%fused_computation.3 | loop fusion | bytes 4194320 | tf_op jit(solution)/shard_map/weight/jit(dynamic_index_in_dim)/squeeze | solution.py:28
  91.6 1.0 collective-permute-start
  92.7 0.9 constant_dynamic-slice_fusion.1
  93.5 3.1 %collective-permute-start.8 = (bf16[448,256]{1,0:T(8,128)(2,1)S(1)}, bf16[448,256]{1,0:T(8,128)(2,1)S(1)}, u32[]{:S(2)}, u32[]{:S(2)}) collective-permute-start(bf16[448,256]{1,0:T(8,128)(2,1)S(1)} %get-tuple-element.47), channel_id=1, source_target_pairs={{0,96},{32,64},{64,32},{96,0},{1,97},{33,65},{65,33},{97,1},{2,98}... | collective-permute-start | bytes 688136 | tf_op jit(solution)/shard_map/cotangent/ppermute | solution.py:17
  97.6 3.4 %collective-permute-start.1 = (bf16[4,128,512]{2,1,0:T(8,128)(2,1)}, bf16[4,128,512]{2,1,0:T(8,128)(2,1)}, u32[]{:S(2)}, u32[]{:S(2)}) collective-permute-start(bf16[4,128,512]{2,1,0:T(8,128)(2,1)} %get-tuple-element.39), channel_id=1, source_target_pairs={{0,4},{2,6},{4,0},{6,2},{1,5},{3,7},{5,1},{7,3},{8,12},{10,14},{12... | collective-permute-start | bytes 1572872 | tf_op jit(solution)/shard_map/weight/ppermute | solution.py:17
  101.0 10.6 %collective-permute-done.8 = bf16[448,256]{1,0:T(8,128)(2,1)S(1)} collective-permute-done((bf16[448,256]{1,0:T(8,128)(2,1)S(1)}, bf16[448,256]{1,0:T(8,128)(2,1)S(1)}, u32[]{:S(2)}, u32[]{:S(2)}) %collective-permute-start.8) | collective-permute-done | bytes 229408 | tf_op jit(solution)/shard_map/cotangent/ppermute | solution.py:17
  111.6 2.8 collective-permute-start.2
  114.4 3.2 %collective-permute-done.6 = bf16[448,256]{1,0:T(8,128)(2,1)S(1)} collective-permute-done((bf16[448,256]{1,0:T(8,128)(2,1)}, bf16[448,256]{1,0:T(8,128)(2,1)S(1)}, u32[]{:S(2)}, u32[]{:S(2)}) %collective-permute-start.6) | collective-permute-done | bytes 229408 | tf_op jit(solution)/shard_map/cotangent/ppermute | solution.py:17
  117.6 0.7 copy-done.13
  118.3 1.4 pad_maximum_fusion.1.refs_0_
  119.7 1.9 bitcast_dynamic-update-slice_fusion
  121.6 0.8 dynamic-slice_dynamic-update-slice_fusion.2
  122.4 1.8 dynamic-slice_dynamic-update-slice_fusion.1
  124.3 5.1 %collective-permute-done.2.refs_3_ = bf16[4,128,512]{2,1,0:T(8,128)(2,1)} collective-permute-done((bf16[4,128,512]{2,1,0:T(8,128)(2,1)}, bf16[4,128,512]{2,1,0:T(8,128)(2,1)}, u32[]{:S(2)}, u32[]{:S(2)}) %collective-permute-start.2) | collective-permute-done | bytes 524320 | tf_op jit(solution)/shard_map/weight/ppermute | solution.py:17
  129.4 1.7 dynamic-slice_dynamic-update-slice_fusion
  131.1 1.1 constant_dynamic-update-slice_fusion
  132.4 1.8 collective-permute-start.20
  136.0 0.7 collective-permute-done.9.refs_5_
  136.7 6.3 %gather_blocks.1 = (bf16[448,512]{1,0:T(8,128)(2,1)}, bf16[448,512]{1,0:T(8,128)(2,1)}, bf16[448,512]{1,0:T(8,128)(2,1)}, bf16[448,512]{1,0:T(8,128)(2,1)}) custom-call(s32[28]{0:T(128)} %compare_select_fusion.7.kind_ref, s32[28]{0:T(128)} %get-tuple-element.36.index_ref, s32[28]{0:T(128)} %get-tuple-element.34.half_ref, ...), custom_call_target="tpu_custom_call" | custom-call | tf_op jit(solution)/shard_map/weight/gather_blocks/pallas_call | solution.py:120
  143.2 1.0 collective-permute-start.11
  144.2 3.5 %collective-permute-start.12 = (bf16[448,512]{1,0:T(8,128)(2,1)}, bf16[448,512]{1,0:T(8,128)(2,1)S(1)}, u32[]{:S(2)}, u32[]{:S(2)}) collective-permute-start(bf16[448,512]{1,0:T(8,128)(2,1)} %get-tuple-element.26), channel_id=1, source_target_pairs={{0,6},{2,4},{4,2},{6,0},{1,7},{3,5},{5,3},{7,1},{8,14},{10,12},{12... | collective-permute-start | bytes 1376264 | tf_op jit(solution)/shard_map/weight/ppermute | solution.py:17
  148.3 0.7 pad_add_fusion.2.place_ref
  149.5 3.2 %collective-permute-start.21 = (bf16[4,448,256]{2,1,0:T(8,128)(2,1)S(1)}, bf16[4,448,256]{2,1,0:T(8,128)(2,1)}, u32[]{:S(2)}, u32[]{:S(2)}) collective-permute-start(bf16[4,448,256]{2,1,0:T(8,128)(2,1)S(1)} %pad_maximum_fusion.1.refs_0_), channel_id=1, source_target_pairs={{0,16},{8,24},{16,0},{24,8},{1,17},{9,25},{17,1},{25,9},{2,18},{10... | collective-permute-start | bytes 2752520 | tf_op jit(solution)/shard_map/grad/ppermute | solution.py:17
  152.8 3.8 %collective-permute-done.10.refs_1_ = bf16[448,512]{1,0:T(8,128)(2,1)S(1)} collective-permute-done((bf16[448,512]{1,0:T(8,128)(2,1)}, bf16[448,512]{1,0:T(8,128)(2,1)S(1)}, u32[]{:S(2)}, u32[]{:S(2)}) %collective-permute-start.10) | collective-permute-done | bytes 458784 | tf_op jit(solution)/shard_map/weight/ppermute | solution.py:17
  156.6 3.0 %collective-permute-start.22 = (bf16[4,448,256]{2,1,0:T(8,128)(2,1)S(1)}, bf16[4,448,256]{2,1,0:T(8,128)(2,1)}, u32[]{:S(2)}, u32[]{:S(2)}) collective-permute-start(bf16[4,448,256]{2,1,0:T(8,128)(2,1)S(1)} %pad_maximum_fusion.1.refs_0_), channel_id=1, source_target_pairs={{0,24},{8,16},{16,8},{24,0},{1,25},{9,17},{17,9},{25,1},{2,26},{10... | collective-permute-start | bytes 2752520 | tf_op jit(solution)/shard_map/grad/ppermute | solution.py:17
  159.5 5.5 %collective-permute-done.11.refs_2_ = bf16[448,512]{1,0:T(8,128)(2,1)S(1)} collective-permute-done((bf16[448,512]{1,0:T(8,128)(2,1)}, bf16[448,512]{1,0:T(8,128)(2,1)S(1)}, u32[]{:S(2)}, u32[]{:S(2)}) %collective-permute-start.11) | collective-permute-done | bytes 458784 | tf_op jit(solution)/shard_map/weight/ppermute | solution.py:17
  165.0 3.0 %collective-permute-done.12.refs_3_ = bf16[448,512]{1,0:T(8,128)(2,1)S(1)} collective-permute-done((bf16[448,512]{1,0:T(8,128)(2,1)}, bf16[448,512]{1,0:T(8,128)(2,1)S(1)}, u32[]{:S(2)}, u32[]{:S(2)}) %collective-permute-start.12) | collective-permute-done | bytes 458784 | tf_op jit(solution)/shard_map/weight/ppermute | solution.py:17
  168.0 0.8 copy-done.4
  168.8 5.9 %project.7 = bf16[4,448,256]{2,1,0:T(8,128)(2,1)} custom-call(s32[2]{0:T(128)} %pad_add_fusion.3.place_ref, bf16[8,4,128,2048]{3,2,1,0:T(8,128)(2,1)} %bitcast.48, bf16[448,512]{1,0:T(8,128)(2,1)} %get-tuple-element.23.refs_0_, bf16[448,512]{1,0:T(8,128)(2,1)} %copy-done.2, bf16[448,512]{1,0:T(8,128)(2,1)} %copy-done.3, bf16[448,512]{1,0:T(8,128)(2,1)} %copy-done.4), custom_call_target="tpu_custom_call" | custom-call | tf_op jit(solution)/shard_map/projected/project/pallas_call | solution.py:197
  174.7 2.9 %collective-permute-start.15 = (bf16[4,448,256]{2,1,0:T(8,128)(2,1)}, bf16[4,448,256]{2,1,0:T(8,128)(2,1)S(1)}, u32[]{:S(2)}, u32[]{:S(2)}) collective-permute-start(bf16[4,448,256]{2,1,0:T(8,128)(2,1)} %project.7), channel_id=1, source_target_pairs={{0,24},{8,16},{16,8},{24,0},{1,25},{9,17},{17,9},{25,1},{2,26},{10... | collective-permute-start | bytes 2752520 | tf_op jit(solution)/shard_map/projected/ppermute | solution.py:17
  177.6 5.9 %project.6 = bf16[4,448,256]{2,1,0:T(8,128)(2,1)} custom-call(s32[2]{0:T(128)} %pad_add_fusion.2.place_ref, bf16[8,4,128,2048]{3,2,1,0:T(8,128)(2,1)} %bitcast.49, bf16[448,512]{1,0:T(8,128)(2,1)} %get-tuple-element.23.refs_0_, bf16[448,512]{1,0:T(8,128)(2,1)} %copy-done.2, bf16[448,512]{1,0:T(8,128)(2,1)} %copy-done.3, bf16[448,512]{1,0:T(8,128)(2,1)} %copy-done.4), custom_call_target="tpu_custom_call" | custom-call | tf_op jit(solution)/shard_map/projected/project/pallas_call | solution.py:197
  183.5 0.9 collective-permute-start.14
  184.3 5.9 %project.5 = bf16[4,448,256]{2,1,0:T(8,128)(2,1)} custom-call(s32[2]{0:T(128)} %pad_add_fusion.1.place_ref, bf16[8,4,128,2048]{3,2,1,0:T(8,128)(2,1)} %bitcast.50, bf16[448,512]{1,0:T(8,128)(2,1)} %get-tuple-element.23.refs_0_, bf16[448,512]{1,0:T(8,128)(2,1)} %copy-done.2, bf16[448,512]{1,0:T(8,128)(2,1)} %copy-done.3, bf16[448,512]{1,0:T(8,128)(2,1)} %copy-done.4), custom_call_target="tpu_custom_call" | custom-call | tf_op jit(solution)/shard_map/projected/project/pallas_call | solution.py:197
  191.1 0.7 pad_add_fusion.4.place_ref
  191.7 25.1 %collective-permute-done.22.refs_3_ = bf16[4,448,256]{2,1,0:T(8,128)(2,1)} collective-permute-done((bf16[4,448,256]{2,1,0:T(8,128)(2,1)S(1)}, bf16[4,448,256]{2,1,0:T(8,128)(2,1)}, u32[]{:S(2)}, u32[]{:S(2)}) %collective-permute-start.22) | collective-permute-done | bytes 917536 | tf_op jit(solution)/shard_map/grad/ppermute | solution.py:17
  216.8 15.6 %gradient.1 = (bf16[448,512]{1,0:T(8,128)(2,1)}, bf16[448,512]{1,0:T(8,128)(2,1)}, bf16[448,512]{1,0:T(8,128)(2,1)}, bf16[448,512]{1,0:T(8,128)(2,1)}) custom-call(s32[2]{0:T(128)} %pad_add_fusion.4.place_ref, bf16[8,4,128,2048]{3,2,1,0:T(8,128)(2,1)} %bitcast.51, bf16[4,448,256]{2,1,0:T(8,128)(2,1)} %copy-done.5, ...), custom_call_target="tpu_custom_call" | custom-call | tf_op jit(solution)/shard_map/grad/gradient/pallas_call | solution.py:249
  232.4 1.5 collective-permute-start.23
  233.9 3.0 %collective-permute-start.24 = (bf16[448,512]{1,0:T(8,128)(2,1)}, bf16[448,512]{1,0:T(8,128)(2,1)S(1)}, u32[]{:S(2)}, u32[]{:S(2)}) collective-permute-start(bf16[448,512]{1,0:T(8,128)(2,1)} %get-tuple-element.30), channel_id=1, source_target_pairs={{0,64},{32,96},{64,0},{96,32},{1,65},{33,97},{65,1},{97,33},{2,66}... | collective-permute-start | bytes 1376264 | tf_op jit(solution)/shard_map/grad/ppermute | solution.py:17
  236.9 5.8 %project.4 = bf16[4,448,256]{2,1,0:T(8,128)(2,1)} custom-call(s32[2]{0:T(128)} %pad_add_fusion.place_ref, bf16[8,4,128,2048]{3,2,1,0:T(8,128)(2,1)} %bitcast.52, bf16[448,512]{1,0:T(8,128)(2,1)} %get-tuple-element.23.refs_0_, bf16[448,512]{1,0:T(8,128)(2,1)} %copy-done.2, bf16[448,512]{1,0:T(8,128)(2,1)} %copy-done.3, bf16[448,512]{1,0:T(8,128)(2,1)} %copy-done.4), custom_call_target="tpu_custom_call" | custom-call | tf_op jit(solution)/shard_map/projected/project/pallas_call | solution.py:197
  243.1 1.6 add_convert_fusion
  244.8 0.7 collective-permute-start.16
  245.5 2.4 collective-permute-start.17
  247.9 3.5 %collective-permute-start.18 = (bf16[448,256]{1,0:T(8,128)(2,1)S(1)}, bf16[448,256]{1,0:T(8,128)(2,1)S(1)}, u32[]{:S(2)}, u32[]{:S(2)}) collective-permute-start(bf16[448,256]{1,0:T(8,128)(2,1)S(1)} %get-tuple-element.43), channel_id=1, source_target_pairs={{0,64},{2,96},{4,0},{6,32},{32,66},{34,98},{36,2},{38,34},{64,68},... | collective-permute-start | bytes 688136 | tf_op jit(solution)/shard_map/projected/ppermute | solution.py:325
  251.4 7.1 %collective-permute-done.24.refs_2_ = bf16[448,512]{1,0:T(8,128)(2,1)S(1)} collective-permute-done((bf16[448,512]{1,0:T(8,128)(2,1)}, bf16[448,512]{1,0:T(8,128)(2,1)S(1)}, u32[]{:S(2)}, u32[]{:S(2)}) %collective-permute-start.24) | collective-permute-done | bytes 458784 | tf_op jit(solution)/shard_map/grad/ppermute | solution.py:17
  258.6 13.1 %collective-permute-done.25.refs_3_ = bf16[448,512]{1,0:T(8,128)(2,1)S(1)} collective-permute-done((bf16[448,512]{1,0:T(8,128)(2,1)S(1)}, bf16[448,512]{1,0:T(8,128)(2,1)S(1)}, u32[]{:S(2)}, u32[]{:S(2)}) %collective-permute-start.25) | collective-permute-done | bytes 458784 | tf_op jit(solution)/shard_map/grad/ppermute | solution.py:17
  271.7 0.8 copy-done.10
  272.5 4.8 %assemble.3 = f32[512,1792]{1,0:T(8,128)} custom-call(s32[1]{0:T(128)} %bitcast.place_ref, bf16[448,512]{1,0:T(8,128)(2,1)} %get-tuple-element.28.refs_0_, bf16[448,512]{1,0:T(8,128)(2,1)} %copy-done.8, bf16[448,512]{1,0:T(8,128)(2,1)} %copy-done.9, bf16[448,512]{1,0:T(8,128)(2,1)} %copy-done.10), custom_call_target="tpu_custom_call" | custom-call | tf_op jit(solution)/shard_map/grad/assemble/pallas_call | solution.py:280
  277.3 0.6 copy-done.14
  278.1 0.7 copy-done.17
  278.8 2.4 assemble.2
  (77 shorter events, 6.5 us)
Async XLA Ops:
  7.2 160.9 %all-gather.3.cloned.1.call-start = ((), (), s32[]{:S(2)}) async-start(), calls=%async_computation.3 | async-start | bytes 18874368 | tf_op jit(solution)/shard_map/tokens/all_gather | solution.py:302
  41.9 0.7 copy-start.20
  48.5 8.2 %copy-start.18 = (bf16[4,128,512]{2,1,0:T(8,128)(2,1)S(1)}, bf16[4,128,512]{2,1,0:T(8,128)(2,1)}, u32[]{:S(2)}) copy-start(bf16[4,128,512]{2,1,0:T(8,128)(2,1)} %get-tuple-element.19) | copy-start | bytes 1572868
  48.5 31.0 %copy-start.7 = (bf16[4,128,512]{2,1,0:T(8,128)(2,1)S(1)}, bf16[4,128,512]{2,1,0:T(8,128)(2,1)}, u32[]{:S(2)}) copy-start(bf16[4,128,512]{2,1,0:T(8,128)(2,1)} %get-tuple-element.18) | copy-start | bytes 1572868
  48.5 32.9 %all-to-all-start.1 = ((bf16[4,4,128,512]{3,2,1,0:T(8,128)(2,1)}), bf16[4,4,128,512]{3,2,1,0:T(8,128)(2,1)S(1)}, u32[]{:S(2)}, u32[]{:S(2)}) async-start(bf16[4,4,128,512]{3,2,1,0:T(8,128)(2,1)} %get-tuple-element.17), calls=%async_computation.1 | async-start | bytes 4194304 | tf_op jit(solution)/shard_map/weight/all_to_all | solution.py:32
  52.4 26.5 %collective-permute-start.5 = (bf16[4,128,512]{2,1,0:T(8,128)(2,1)}, bf16[4,128,512]{2,1,0:T(8,128)(2,1)S(1)}, u32[]{:S(2)}, u32[]{:S(2)}) collective-permute-start(bf16[4,128,512]{2,1,0:T(8,128)(2,1)} %get-tuple-element.21), channel_id=1, source_target_pairs={{0,6},{2,4},{4,2},{6,0},{1,7},{3,5},{5,3},{7,1},{8,14},{10,12},{12... | collective-permute-start | bytes 1572872 | tf_op jit(solution)/shard_map/weight/ppermute | solution.py:17
  56.7 22.1 %collective-permute-start.4 = (bf16[4,128,512]{2,1,0:T(8,128)(2,1)}, bf16[4,128,512]{2,1,0:T(8,128)(2,1)S(1)}, u32[]{:S(2)}, u32[]{:S(2)}) collective-permute-start(bf16[4,128,512]{2,1,0:T(8,128)(2,1)} %get-tuple-element.20), channel_id=1, source_target_pairs={{0,4},{2,6},{4,0},{6,2},{1,5},{3,7},{5,1},{7,3},{8,12},{10,14},{12... | collective-permute-start | bytes 1572872 | tf_op jit(solution)/shard_map/weight/ppermute | solution.py:17
  56.7 22.8 %collective-permute-start.3 = (bf16[4,128,512]{2,1,0:T(8,128)(2,1)S(1)}, bf16[4,128,512]{2,1,0:T(8,128)(2,1)S(1)}, u32[]{:S(2)}, u32[]{:S(2)}) collective-permute-start(bf16[4,128,512]{2,1,0:T(8,128)(2,1)S(1)} %copy-done.18), channel_id=1, source_target_pairs={{0,2},{2,0},{4,6},{6,4},{1,3},{3,1},{5,7},{7,5},{8,10},{10,8},{12,... | collective-permute-start | bytes 1572872 | tf_op jit(solution)/shard_map/weight/ppermute | solution.py:17
  81.4 1.3 copy-start.1
  82.7 38.9 %all-to-all-start.2 = ((bf16[4,4,128,512]{3,2,1,0:T(8,128)(2,1)}), bf16[4,4,128,512]{3,2,1,0:T(8,128)(2,1)S(1)}, u32[]{:S(2)}, u32[]{:S(2)}) async-start(bf16[4,4,128,512]{3,2,1,0:T(8,128)(2,1)} %copy.12), calls=%async_computation.2 | async-start | bytes 4194304 | tf_op jit(solution)/shard_map/weight/all_to_all | solution.py:32
  91.6 30.0 %collective-permute-start = (bf16[4,128,512]{2,1,0:T(8,128)(2,1)}, bf16[4,128,512]{2,1,0:T(8,128)(2,1)S(1)}, u32[]{:S(2)}, u32[]{:S(2)}) collective-permute-start(bf16[4,128,512]{2,1,0:T(8,128)(2,1)} %get-tuple-element.40), channel_id=1, source_target_pairs={{0,2},{2,0},{4,6},{6,4},{1,3},{3,1},{5,7},{7,5},{8,10},{10,8},{12,... | collective-permute-start | bytes 1572872 | tf_op jit(solution)/shard_map/weight/ppermute | solution.py:17
  93.5 18.1 %collective-permute-start.8 = (bf16[448,256]{1,0:T(8,128)(2,1)S(1)}, bf16[448,256]{1,0:T(8,128)(2,1)S(1)}, u32[]{:S(2)}, u32[]{:S(2)}) collective-permute-start(bf16[448,256]{1,0:T(8,128)(2,1)S(1)} %get-tuple-element.47), channel_id=1, source_target_pairs={{0,96},{32,64},{64,32},{96,0},{1,97},{33,65},{65,33},{97,1},{2,98}... | collective-permute-start | bytes 688136 | tf_op jit(solution)/shard_map/cotangent/ppermute | solution.py:17
  96.6 17.8 %collective-permute-start.7 = (bf16[448,256]{1,0:T(8,128)(2,1)}, bf16[448,256]{1,0:T(8,128)(2,1)S(1)}, u32[]{:S(2)}, u32[]{:S(2)}) collective-permute-start(bf16[448,256]{1,0:T(8,128)(2,1)} %get-tuple-element.48), channel_id=1, source_target_pairs={{0,64},{32,96},{64,0},{96,32},{1,65},{33,97},{65,1},{97,33},{2,66}... | collective-permute-start | bytes 688136 | tf_op jit(solution)/shard_map/cotangent/ppermute | solution.py:17
  97.2 20.5 %collective-permute-start.6 = (bf16[448,256]{1,0:T(8,128)(2,1)}, bf16[448,256]{1,0:T(8,128)(2,1)S(1)}, u32[]{:S(2)}, u32[]{:S(2)}) collective-permute-start(bf16[448,256]{1,0:T(8,128)(2,1)} %get-tuple-element.49), channel_id=1, source_target_pairs={{0,32},{32,0},{64,96},{96,64},{1,33},{33,1},{65,97},{97,65},{2,34}... | collective-permute-start | bytes 688136 | tf_op jit(solution)/shard_map/cotangent/ppermute | solution.py:17
  97.6 24.8 %collective-permute-start.1 = (bf16[4,128,512]{2,1,0:T(8,128)(2,1)}, bf16[4,128,512]{2,1,0:T(8,128)(2,1)}, u32[]{:S(2)}, u32[]{:S(2)}) collective-permute-start(bf16[4,128,512]{2,1,0:T(8,128)(2,1)} %get-tuple-element.39), channel_id=1, source_target_pairs={{0,4},{2,6},{4,0},{6,2},{1,5},{3,7},{5,1},{7,3},{8,12},{10,14},{12... | collective-permute-start | bytes 1572872 | tf_op jit(solution)/shard_map/weight/ppermute | solution.py:17
  111.6 6.1 %copy-start.11 = (bf16[448,256]{1,0:T(8,128)(2,1)}, bf16[448,256]{1,0:T(8,128)(2,1)S(1)}, u32[]{:S(2)}) copy-start(bf16[448,256]{1,0:T(8,128)(2,1)S(1)} %collective-permute-done.8) | copy-start | bytes 688132
  111.6 17.8 %collective-permute-start.2 = (bf16[4,128,512]{2,1,0:T(8,128)(2,1)}, bf16[4,128,512]{2,1,0:T(8,128)(2,1)}, u32[]{:S(2)}, u32[]{:S(2)}) collective-permute-start(bf16[4,128,512]{2,1,0:T(8,128)(2,1)} %get-tuple-element.38), channel_id=1, source_target_pairs={{0,6},{2,4},{4,2},{6,0},{1,7},{3,5},{5,3},{7,1},{8,14},{10,12},{12... | collective-permute-start | bytes 1572872 | tf_op jit(solution)/shard_map/weight/ppermute | solution.py:17
  114.4 3.3 %copy-start.12 = (bf16[448,256]{1,0:T(8,128)(2,1)}, bf16[448,256]{1,0:T(8,128)(2,1)S(1)}, u32[]{:S(2)}) copy-start(bf16[448,256]{1,0:T(8,128)(2,1)S(1)} %collective-permute-done.7) | copy-start | bytes 688132
  117.6 0.7 copy-start.13
  119.7 36.9 %copy-start.5 = (bf16[4,448,256]{2,1,0:T(8,128)(2,1)}, bf16[4,448,256]{2,1,0:T(8,128)(2,1)S(1)}, u32[]{:S(2)}) copy-start(bf16[4,448,256]{2,1,0:T(8,128)(2,1)S(1)} %pad_maximum_fusion.1.refs_0_) | copy-start | bytes 2752516
  121.6 10.6 %copy-start = (bf16[4,4,128,512]{3,2,1,0:T(8,128)(2,1)}, bf16[4,4,128,512]{3,2,1,0:T(8,128)(2,1)S(1)}, u32[]{:S(2)}) copy-start(bf16[4,4,128,512]{3,2,1,0:T(8,128)(2,1)S(1)} %all-to-all-done.2) | copy-start | bytes 6291460
  121.6 10.6 %copy-start.6 = (bf16[4,128,512]{2,1,0:T(8,128)(2,1)}, bf16[4,128,512]{2,1,0:T(8,128)(2,1)S(1)}, u32[]{:S(2)}) copy-start(bf16[4,128,512]{2,1,0:T(8,128)(2,1)S(1)} %collective-permute-done.refs_1_) | copy-start | bytes 1572868
  131.0 1.2 slice-start
  132.2 4.5 %collective-permute-start.9 = (bf16[16,128,512]{2,1,0:T(8,128)(2,1)}, bf16[16,128,512]{2,1,0:T(8,128)(2,1)}, u32[]{:S(2)}, u32[]{:S(2)}) collective-permute-start(bf16[16,128,512]{2,1,0:T(8,128)(2,1)} %constant_dynamic-update-slice_fusion), channel_id=1, source_target_pairs={{0,1},{1,0},{2,3},{3,2},{4,5},{5,4},{6,7},{7,6},{8,9},{9,8},{10,11... | collective-permute-start | bytes 6291464 | tf_op jit(solution)/shard_map/weight/ppermute | solution.py:150
  132.4 57.8 %collective-permute-start.20 = (bf16[4,448,256]{2,1,0:T(8,128)(2,1)S(1)}, bf16[4,448,256]{2,1,0:T(8,128)(2,1)}, u32[]{:S(2)}, u32[]{:S(2)}) collective-permute-start(bf16[4,448,256]{2,1,0:T(8,128)(2,1)S(1)} %pad_maximum_fusion.1.refs_0_), channel_id=1, source_target_pairs={{0,8},{8,0},{16,24},{24,16},{1,9},{9,1},{17,25},{25,17},{2,10},{10... | collective-permute-start | bytes 2752520 | tf_op jit(solution)/shard_map/grad/ppermute | solution.py:17
  143.0 13.6 %collective-permute-start.10 = (bf16[448,512]{1,0:T(8,128)(2,1)}, bf16[448,512]{1,0:T(8,128)(2,1)S(1)}, u32[]{:S(2)}, u32[]{:S(2)}) collective-permute-start(bf16[448,512]{1,0:T(8,128)(2,1)} %get-tuple-element.24), channel_id=1, source_target_pairs={{0,2},{2,0},{4,6},{6,4},{1,3},{3,1},{5,7},{7,5},{8,10},{10,8},{12,... | collective-permute-start | bytes 1376264 | tf_op jit(solution)/shard_map/weight/ppermute | solution.py:17
  143.2 21.8 %collective-permute-start.11 = (bf16[448,512]{1,0:T(8,128)(2,1)}, bf16[448,512]{1,0:T(8,128)(2,1)S(1)}, u32[]{:S(2)}, u32[]{:S(2)}) collective-permute-start(bf16[448,512]{1,0:T(8,128)(2,1)} %get-tuple-element.25), channel_id=1, source_target_pairs={{0,4},{2,6},{4,0},{6,2},{1,5},{3,7},{5,1},{7,3},{8,12},{10,14},{12... | collective-permute-start | bytes 1376264 | tf_op jit(solution)/shard_map/weight/ppermute | solution.py:17
  144.2 23.8 %collective-permute-start.12 = (bf16[448,512]{1,0:T(8,128)(2,1)}, bf16[448,512]{1,0:T(8,128)(2,1)S(1)}, u32[]{:S(2)}, u32[]{:S(2)}) collective-permute-start(bf16[448,512]{1,0:T(8,128)(2,1)} %get-tuple-element.26), channel_id=1, source_target_pairs={{0,6},{2,4},{4,2},{6,0},{1,7},{3,5},{5,3},{7,1},{8,14},{10,12},{12... | collective-permute-start | bytes 1376264 | tf_op jit(solution)/shard_map/weight/ppermute | solution.py:17
  149.5 42.2 %collective-permute-start.21 = (bf16[4,448,256]{2,1,0:T(8,128)(2,1)S(1)}, bf16[4,448,256]{2,1,0:T(8,128)(2,1)}, u32[]{:S(2)}, u32[]{:S(2)}) collective-permute-start(bf16[4,448,256]{2,1,0:T(8,128)(2,1)S(1)} %pad_maximum_fusion.1.refs_0_), channel_id=1, source_target_pairs={{0,16},{8,24},{16,0},{24,8},{1,17},{9,25},{17,1},{25,9},{2,18},{10... | collective-permute-start | bytes 2752520 | tf_op jit(solution)/shard_map/grad/ppermute | solution.py:17
  156.6 11.5 %copy-start.2 = (bf16[448,512]{1,0:T(8,128)(2,1)}, bf16[448,512]{1,0:T(8,128)(2,1)S(1)}, u32[]{:S(2)}) copy-start(bf16[448,512]{1,0:T(8,128)(2,1)S(1)} %collective-permute-done.10.refs_1_) | copy-start | bytes 1376260
  156.6 60.3 %collective-permute-start.22 = (bf16[4,448,256]{2,1,0:T(8,128)(2,1)S(1)}, bf16[4,448,256]{2,1,0:T(8,128)(2,1)}, u32[]{:S(2)}, u32[]{:S(2)}) collective-permute-start(bf16[4,448,256]{2,1,0:T(8,128)(2,1)S(1)} %pad_maximum_fusion.1.refs_0_), channel_id=1, source_target_pairs={{0,24},{8,16},{16,8},{24,0},{1,25},{9,17},{17,9},{25,1},{2,26},{10... | collective-permute-start | bytes 2752520 | tf_op jit(solution)/shard_map/grad/ppermute | solution.py:17
  165.0 3.1 %copy-start.3 = (bf16[448,512]{1,0:T(8,128)(2,1)}, bf16[448,512]{1,0:T(8,128)(2,1)S(1)}, u32[]{:S(2)}) copy-start(bf16[448,512]{1,0:T(8,128)(2,1)S(1)} %collective-permute-done.11.refs_2_) | copy-start | bytes 1376260
  168.0 0.8 copy-start.4
  174.7 68.1 %collective-permute-start.15 = (bf16[4,448,256]{2,1,0:T(8,128)(2,1)}, bf16[4,448,256]{2,1,0:T(8,128)(2,1)S(1)}, u32[]{:S(2)}, u32[]{:S(2)}) collective-permute-start(bf16[4,448,256]{2,1,0:T(8,128)(2,1)} %project.7), channel_id=1, source_target_pairs={{0,24},{8,16},{16,8},{24,0},{1,25},{9,17},{17,9},{25,1},{2,26},{10... | collective-permute-start | bytes 2752520 | tf_op jit(solution)/shard_map/projected/ppermute | solution.py:17
  183.5 59.6 %collective-permute-start.14 = (bf16[4,448,256]{2,1,0:T(8,128)(2,1)}, bf16[4,448,256]{2,1,0:T(8,128)(2,1)S(1)}, u32[]{:S(2)}, u32[]{:S(2)}) collective-permute-start(bf16[4,448,256]{2,1,0:T(8,128)(2,1)} %project.6), channel_id=1, source_target_pairs={{0,16},{8,24},{16,0},{24,8},{1,17},{9,25},{17,1},{25,9},{2,18},{10... | collective-permute-start | bytes 2752520 | tf_op jit(solution)/shard_map/projected/ppermute | solution.py:17
  190.2 52.9 %collective-permute-start.13 = (bf16[4,448,256]{2,1,0:T(8,128)(2,1)}, bf16[4,448,256]{2,1,0:T(8,128)(2,1)S(1)}, u32[]{:S(2)}, u32[]{:S(2)}) collective-permute-start(bf16[4,448,256]{2,1,0:T(8,128)(2,1)} %project.5), channel_id=1, source_target_pairs={{0,8},{8,0},{16,24},{24,16},{1,9},{9,1},{17,25},{25,17},{2,10},{10... | collective-permute-start | bytes 2752520 | tf_op jit(solution)/shard_map/projected/ppermute | solution.py:17
  232.4 15.5 %collective-permute-start.23 = (bf16[448,512]{1,0:T(8,128)(2,1)}, bf16[448,512]{1,0:T(8,128)(2,1)S(1)}, u32[]{:S(2)}, u32[]{:S(2)}) collective-permute-start(bf16[448,512]{1,0:T(8,128)(2,1)} %get-tuple-element.29), channel_id=1, source_target_pairs={{0,32},{32,0},{64,96},{96,64},{1,33},{33,1},{65,97},{97,65},{2,34}... | collective-permute-start | bytes 1376264 | tf_op jit(solution)/shard_map/grad/ppermute | solution.py:17
  233.9 8.9 %copy-start.19 = (bf16[448,512]{1,0:T(8,128)(2,1)S(1)}, bf16[448,512]{1,0:T(8,128)(2,1)}, u32[]{:S(2)}) copy-start(bf16[448,512]{1,0:T(8,128)(2,1)} %get-tuple-element.31) | copy-start | bytes 1376260
  233.9 24.5 %collective-permute-start.24 = (bf16[448,512]{1,0:T(8,128)(2,1)}, bf16[448,512]{1,0:T(8,128)(2,1)S(1)}, u32[]{:S(2)}, u32[]{:S(2)}) collective-permute-start(bf16[448,512]{1,0:T(8,128)(2,1)} %get-tuple-element.30), channel_id=1, source_target_pairs={{0,64},{32,96},{64,0},{96,32},{1,65},{33,97},{65,1},{97,33},{2,66}... | collective-permute-start | bytes 1376264 | tf_op jit(solution)/shard_map/grad/ppermute | solution.py:17
  242.8 28.9 %collective-permute-start.25 = (bf16[448,512]{1,0:T(8,128)(2,1)S(1)}, bf16[448,512]{1,0:T(8,128)(2,1)S(1)}, u32[]{:S(2)}, u32[]{:S(2)}) collective-permute-start(bf16[448,512]{1,0:T(8,128)(2,1)S(1)} %copy-done.19), channel_id=1, source_target_pairs={{0,96},{32,64},{64,32},{96,0},{1,97},{33,65},{65,33},{97,1},{2,98}... | collective-permute-start | bytes 1376264 | tf_op jit(solution)/shard_map/grad/ppermute | solution.py:17
  244.8 32.5 %collective-permute-start.16 = (bf16[448,256]{1,0:T(8,128)(2,1)S(1)}, bf16[448,256]{1,0:T(8,128)(2,1)S(1)}, u32[]{:S(2)}, u32[]{:S(2)}) collective-permute-start(bf16[448,256]{1,0:T(8,128)(2,1)S(1)} %get-tuple-element.45), channel_id=1, source_target_pairs={{0,0},{2,32},{4,64},{6,96},{32,2},{34,34},{36,66},{38,98},{64,4},{... | collective-permute-start | bytes 688136 | tf_op jit(solution)/shard_map/projected/ppermute | solution.py:325
  245.5 31.8 %collective-permute-start.17 = (bf16[448,256]{1,0:T(8,128)(2,1)S(1)}, bf16[448,256]{1,0:T(8,128)(2,1)S(1)}, u32[]{:S(2)}, u32[]{:S(2)}) collective-permute-start(bf16[448,256]{1,0:T(8,128)(2,1)S(1)} %get-tuple-element.44), channel_id=1, source_target_pairs={{0,32},{2,0},{4,96},{6,64},{32,34},{34,2},{36,98},{38,66},{64,36},... | collective-permute-start | bytes 688136 | tf_op jit(solution)/shard_map/projected/ppermute | solution.py:325
  247.9 23.8 %copy-start.8 = (bf16[448,512]{1,0:T(8,128)(2,1)}, bf16[448,512]{1,0:T(8,128)(2,1)S(1)}, u32[]{:S(2)}) copy-start(bf16[448,512]{1,0:T(8,128)(2,1)S(1)} %collective-permute-done.23.refs_1_) | copy-start | bytes 1376260
  247.9 29.4 %collective-permute-start.18 = (bf16[448,256]{1,0:T(8,128)(2,1)S(1)}, bf16[448,256]{1,0:T(8,128)(2,1)S(1)}, u32[]{:S(2)}, u32[]{:S(2)}) collective-permute-start(bf16[448,256]{1,0:T(8,128)(2,1)S(1)} %get-tuple-element.43), channel_id=1, source_target_pairs={{0,64},{2,96},{4,0},{6,32},{32,66},{34,98},{36,2},{38,34},{64,68},... | collective-permute-start | bytes 688136 | tf_op jit(solution)/shard_map/projected/ppermute | solution.py:325
  258.5 13.2 %copy-start.9 = (bf16[448,512]{1,0:T(8,128)(2,1)}, bf16[448,512]{1,0:T(8,128)(2,1)S(1)}, u32[]{:S(2)}) copy-start(bf16[448,512]{1,0:T(8,128)(2,1)S(1)} %collective-permute-done.24.refs_2_) | copy-start | bytes 1376260
  258.5 18.9 %collective-permute-start.19 = (bf16[448,256]{1,0:T(8,128)(2,1)S(1)}, bf16[448,256]{1,0:T(8,128)(2,1)S(1)}, u32[]{:S(2)}, u32[]{:S(2)}) collective-permute-start(bf16[448,256]{1,0:T(8,128)(2,1)S(1)} %get-tuple-element.42), channel_id=1, source_target_pairs={{0,96},{2,64},{4,32},{6,0},{32,98},{34,66},{36,34},{38,2},{64,100}... | collective-permute-start | bytes 688136 | tf_op jit(solution)/shard_map/projected/ppermute | solution.py:325
  271.7 0.8 copy-start.10
  277.3 0.7 copy-start.14
  277.3 0.8 copy-start.15
  277.3 0.8 copy-start.16
  278.1 0.7 copy-start.17
Sparse Core Ops, SparseCore 0:
  42.1 95.5 all-gather.2

commit v2 on v1

--- a/solution.py
+++ b/solution.py
@@ -38,8 +38,8 @@
         out_ref[x] = tokens_ref[:, x * part:(x + 1) * part]
 
 
-def cut_tokens(tokens, c):
-    rows, width = tokens.shape
+def cut_tokens(tokens, place, rows):
+    width = tokens.shape[1]
     quarter = width // RING
     part = quarter // RING
     return pl.pallas_call(
@@ -47,13 +47,13 @@
         grid_spec=pltpu.PrefetchScalarGridSpec(
             num_scalar_prefetch=1,
             grid=(RING,),
-            in_specs=[pl.BlockSpec((rows // 2, quarter), lambda q, place: (place[0], q))],
-            out_specs=pl.BlockSpec((RING, rows // 2, part), lambda q, place: (0, 0, q)),
-        ),
-        out_shape=jax.ShapeDtypeStruct((RING, rows // 2, quarter), tokens.dtype),
+            in_specs=[pl.BlockSpec((rows, quarter), lambda q, place: (place[0], q))],
+            out_specs=pl.BlockSpec((RING, rows, part), lambda q, place: (0, 0, q)),
+        ),
+        out_shape=jax.ShapeDtypeStruct((RING, rows, quarter), tokens.dtype),
         compiler_params=PARAMS,
         name="cut_tokens",
-    )(c[None], tokens)
+    )(place[None], tokens)
 
 
 def dequantize_kernel(place_ref, codes_ref, scales_ref, first_ref, *second_refs):
@@ -131,20 +131,34 @@
     )(kind, index, half, *sources)
 
 
-def weight_rows(old_codes, old_scales, old_offsets, local_hidden, cot):
+def together(*values):
+    return lax.optimization_barrier(values)
+
+
+def move(old_codes, old_scales, tokens, cotangent):
+    y, x, z, c = (lax.axis_index(a) for a in AXES)
+    first, *second = dequantize(old_codes, old_scales, z)
+    tokens, *second = together(tokens, *second)
+    tokens = all_to_all(cut_tokens(tokens, c, tokens.shape[0] // 2), "x")
+    second = exchange(second, "z")
+    first, tokens, cotangent, *second = together(first, tokens, cotangent, *second)
+    first = all_to_all(first, "x")
+    cot = jnp.stack(exchange([pick(cotangent, y ^ s) for s in range(RING)], "y"))
+    second = jnp.stack(second, axis=1)
+    first, second, cot = together(first, second, cot)
+    firsts = exchange([pick(first, z ^ s, 1) for s in range(RING)], "z")
+    second = all_to_all(second, "x")
+    second, cot = together(second, cot)
+    return lax.all_gather(tokens, ("y", "c")), firsts, second, cot
+
+
+def weight_rows(firsts, second, old_offsets, local_hidden):
     y, x, z, c = (lax.axis_index(a) for a in AXES)
     owners = RING * RING
-    slots = old_scales.shape[0]
-    block = old_codes.shape[0] // slots
+    slots = 2
+    block, part = second.shape[-2:]
     hidden = local_hidden // RING
-    first, *second = dequantize(old_codes, old_scales, z)
-    part = first.shape[-1]
-
-    second = jnp.stack(exchange(second, "z"), axis=1)
-    first = all_to_all(first, "x")
-    firsts = exchange([pick(first, z ^ s, 1) for s in range(RING)], "z")
-    second = all_to_all(second, "x")
-    second, cot = lax.optimization_barrier((second, cot))
+
     give = [lax.dynamic_slice_in_dim(a, 2 * (1 - c), 2, 0) for a in firsts]
     give = give + [lax.dynamic_slice_in_dim(second, 2 * (1 - c), 2, 0).reshape(2 * RING, block, part)]
     other = lax.ppermute(jnp.concatenate(give), "c", [(0, 1), (1, 0)])
@@ -170,45 +184,52 @@
         jnp.where(slot == 0, 2 * c + low, (2 * c + low) * RING + s),
     )
     sources = firsts + [second.reshape(owners, block, part), other]
-    return gather(kind, index, half, sources, hidden), cot
+    return gather(kind, index, half, sources, hidden)
 
 
 def project_kernel(place_ref, tokens_ref, *refs):
-    out_ref = refs[-1]
-    pieces, hidden, share = out_ref.shape
-    total = None
-    for s, weight_ref in enumerate(refs[:-1]):
-        part = weight_ref.shape[1]
-        start = pl.multiple_of((place_ref[1] ^ s) * part, part)
-        rows = tokens_ref[:, 0, :, pl.ds(start, part)].reshape(pieces * share, part)
-        product = lax.dot_general(
-            weight_ref[...], rows, (((1,), (1,)), ((), ())), preferred_element_type=jnp.float32
-        )
-        total = product if total is None else total + product
-    for i in range(pieces):
-        out_ref[i] = total[:, i * share:(i + 1) * share].astype(out_ref.dtype)
-
-
-def project(tokens, weights, x, z):
+    weights, outs, all_ref = refs[:RING], refs[RING:-1], refs[-1]
+    step = pl.program_id(0)
+    part = weights[0].shape[1]
+    rows = outs[0].shape[2]
+
+    @pl.when(step == 0)
+    def _():
+        for s, ref in enumerate(weights):
+            all_ref[:, pl.ds(pl.multiple_of((place_ref[0] ^ s) * part, part), part)] = ref[...]
+
+    product = lax.dot_general(
+        all_ref[...], tokens_ref[...].reshape(RING * rows, RING * part),
+        (((1,), (1,)), ((), ())), preferred_element_type=jnp.float32,
+    ).astype(jnp.bfloat16)
+    for n, ref in enumerate(outs):
+        @pl.when(step == n)
+        def _():
+            for i in range(RING):
+                ref[i] = product[:, i * rows:(i + 1) * rows]
+
+
+def project(tokens, weights, positions, z):
     pieces, _, share, quarter = tokens.shape
-    steps = 2
     hidden, part = weights[0].shape
     rows = pieces * share // RING
+    count = len(positions)
     return pl.pallas_call(
         project_kernel,
         grid_spec=pltpu.PrefetchScalarGridSpec(
             num_scalar_prefetch=1,
-            grid=(steps,),
+            grid=(count,),
             in_specs=[
-                pl.BlockSpec((pieces // steps, 1, share, quarter), lambda i, place: (i, place[0], 0, 0))
+                pl.BlockSpec((pieces, 1, share, quarter), lambda i, place: (0, place[1 + i], 0, 0))
             ]
             + [pl.BlockSpec((hidden, part), lambda i, place: (0, 0))] * RING,
-            out_specs=pl.BlockSpec((RING // steps, hidden, rows), lambda i, place: (i, 0, 0)),
-        ),
-        out_shape=jax.ShapeDtypeStruct((RING, hidden, rows), jnp.bfloat16),
+            out_specs=[pl.BlockSpec((RING, hidden, rows), lambda i, place: (0, 0, 0))] * count,
+            scratch_shapes=[pltpu.VMEM((hidden, quarter), jnp.bfloat16)],
+        ),
+        out_shape=[jax.ShapeDtypeStruct((RING, hidden, rows), jnp.bfloat16)] * count,
         compiler_params=PARAMS,
         name="project",
-    )(jnp.stack([x, z]), tokens, *weights)
+    )(jnp.stack([z, *positions]), tokens, *weights)
 
 
 def grad_kernel(place_ref, tokens_ref, *refs):
@@ -298,33 +319,31 @@
     local_hidden = cotangent.shape[1]
     hidden = local_hidden // RING
 
-    with jax.named_scope("tokens"):
-        every = lax.all_gather(all_to_all(cut_tokens(tokens, c), "x"), ("y", "c"))
-
-    with jax.named_scope("cotangent"):
+    with jax.named_scope("move"):
         cut = cotangent.T.reshape(RING, hidden, local_tokens)
-        cot = jnp.stack(exchange([pick(cut, y ^ s) for s in range(RING)], "y"))
+        every, firsts, second, cot = move(old_codes, old_scales, tokens, cut)
 
     with jax.named_scope("weight"):
-        weights, cot = weight_rows(old_codes, old_scales, old_offsets, local_hidden, cot)
-        weights = exchange(weights, "z")
+        weights = exchange(weight_rows(firsts, second, old_offsets, local_hidden), "z")
+
+    cots = exchange([cot] * RING, "x")
+    sides = together(*weights, *cots)
+    weights, cots = sides[:RING], sides[RING:]
+
+    with jax.named_scope("projected"):
+        far, right = project(every, weights, [x ^ 2, x ^ 1], z)
+        left, own = project(every, weights, [x ^ 3, x], z)
+        parts = [own, swap(far, "x", 2), swap(right, "x", 1), swap(left, "x", 3)]
+        total = sum(p.astype(jnp.float32) for p in parts).astype(jnp.bfloat16)
 
     with jax.named_scope("grad"):
-        cots = exchange([cot] * RING, "x")
-        grad = assemble(exchange(gradient(every, cots, y, x), "y"), y, jnp.float32)
-
-    with jax.named_scope("projected"):
-        parts = [None] * RING
-        for s in NEAR_LAST:
-            parts[s] = swap(project(every, weights, x ^ s, z), "x", s)
-        parts[0] = project(every, weights, x, z)
-        total = sum(p.astype(jnp.float32) for p in parts).astype(jnp.bfloat16)
-        done = []
-        for s in range(RING):
-            pairs = [(a * RING + b, (b ^ s) * RING + a) for a in range(RING) for b in range(RING)]
-            done.append(lax.ppermute(pick(total, z ^ s), ("y", "z"), pairs))
-        projected = assemble(done, y, jnp.bfloat16)
-    return (projected, grad)
+        grads = exchange(gradient(every, cots, y, x), "y")
+
+    done = []
+    for s in range(RING):
+        pairs = [(a * RING + b, (b ^ s) * RING + a) for a in range(RING) for b in range(RING)]
+        done.append(lax.ppermute(pick(total, z ^ s), ("y", "z"), pairs))
+    return assemble(done, y, jnp.bfloat16), assemble(grads, y, jnp.float32)
 
 
 def solution(mesh):

time: 289 us -> 260 us (0.90)
  blocking collectives: 30.9 us -> 0 us
  Pallas kernels: 61.5 us -> 56.7 us
  waiting for transfers between devices: 99.2 us -> 104 us
    all_to_all x1 -> x0, blocking collectives: 30.9 us -> none  [all_to_all(): return lax.all_to_all(array, axis, 0, 0, tiled=True)]
    pallas_call x4 -> x2, Pallas kernels: 23.4 us -> 18.3 us  [project(): pl.pallas_call(project_kernel, grid_spec=pltpu.PrefetchScalarGridSpec(num...]
    all_to_all x2 -> x3, waiting for transfers between devices: 0.01 us -> 4.77 us  [all_to_all(): return lax.all_to_all(array, axis, 0, 0, tiled=True)]
    all_to_all x2 -> x3, starting transfers between devices: 8.13 us -> 12.6 us  [all_to_all(): return lax.all_to_all(array, axis, 0, 0, tiled=True)]
    optimization_barrier x0 -> x1, local copies, waits for them, and re-layouts: none -> 3.88 us  [together(): return lax.optimization_barrier(values)]
    ppermute x21, starting transfers between devices: 38.2 us -> 34.8 us  [swap(): return lax.ppermute(array, axis, [(i, i ^ s) for i in range(RING)])]
    unnamed x48 -> x46, local copies, waits for them, and re-layouts: 12.7 us -> 12.7 us
  transfers between devices with their start and end apart: 29 -> 30, of which waited for: 12 -> 16; matrix products, arithmetic and copies ran while one was open for 8% -> 9% of each run, Pallas kernels for 19% -> 14%
where the time goes in v2:
time: 260 us; the launch traced here: 259 us
  waiting for transfers between devices  104 us (40%)
  Pallas kernels  56.7 us (22%)
  starting transfers between devices  54.7 us (21%)
  local copies, waits for them, and re-layouts  22.4 us (9%)
  between operations  14.3 us (6%)
  other arithmetic  7.44 us (3%)
    ppermute x21, waiting for transfers between devices, swap(): return lax.ppermute(array, axis, [(i, i ^ s) for i in range(RING)])  99.1 us
    ppermute x21, starting transfers between devices, swap(): return lax.ppermute(array, axis, [(i, i ^ s) for i in range(RING)])  34.8 us
    pallas_call x2, Pallas kernels, project(): pl.pallas_call(project_kernel, grid_spec=pltpu.PrefetchScalarGridSpec(num...  18.3 us
    pallas_call x1, Pallas kernels, gradient(): pl.pallas_call(grad_kernel, grid_spec=pltpu.PrefetchScalarGridSpec(num_sc...  15.7 us
    unnamed x46, local copies, waits for them, and re-layouts  12.7 us
    all_to_all x3, starting transfers between devices, all_to_all(): return lax.all_to_all(array, axis, 0, 0, tiled=True)  12.6 us
    ppermute x4, starting transfers between devices, on_device(): done.append(lax.ppermute(pick(total, z ^ s), ('y', 'z'), pairs))  7.3 us
    pallas_call x2, Pallas kernels, assemble(): pl.pallas_call(assemble_kernel, grid_spec=pltpu.PrefetchScalarGridSpec(nu...  7.21 us
  transfers between devices with their start and end apart: 30, of which 16 were waited for; matrix products, arithmetic and copies ran while one was open for 9% of the time, Pallas kernels for 14%

profile of v2, /device:TPU:0, one launch (start us, length us, event | category | flops | bytes accessed | tf_op | source)
XLA Modules:
  0.0 259.3 jit_solution(10153717803145465007)
XLA Ops:
  7.2 0.7 convert_element_type.21
  7.9 0.7 copy.16
  8.6 5.2 %dequantize.1 = (bf16[4,4,128,512]{3,2,1,0:T(8,128)(2,1)}, bf16[4,128,512]{2,1,0:T(8,128)(2,1)}, bf16[4,128,512]{2,1,0:T(8,128)(2,1)}, bf16[4,128,512]{2,1,0:T(8,128)(2,1)}, bf16[4,128,512]{2,1,0:T(8,128)(2,1)}) custom-call(s32[1]{0:T(128)} %bitcast.1.place_ref, bf16[256,8192]{1,0:T(8,128)(2,1)} %codes_ref.1, f32[2,8192]{1,0:T(2,128)} %bitcast.57), custom_call_target="tpu_custom_call" | custom-call | tf_op jit(solution)/shard_map/move/dequantize/pallas_call | solution.py:85
  13.8 3.8 %cut_tokens.1 = bf16[4,128,2048]{2,1,0:T(8,128)(2,1)} custom-call(s32[1]{0:T(128)} %bitcast.4.place_ref, bf16[256,8192]{1,0:T(8,128)(2,1)} %tokens_ref), custom_call_target="tpu_custom_call" | custom-call | tf_op jit(solution)/shard_map/move/cut_tokens/pallas_call | solution.py:45
  17.6 4.4 %all-to-all-start = ((bf16[4,128,2048]{2,1,0:T(8,128)(2,1)}), bf16[4,128,2048]{2,1,0:T(8,128)(2,1)S(1)}, u32[]{:S(2)}, u32[]{:S(2)}) async-start(bf16[4,128,2048]{2,1,0:T(8,128)(2,1)} %cut_tokens.1), calls=%async_computation | async-start | bytes 4194304 | tf_op jit(solution)/shard_map/move/all_to_all | solution.py:32
  21.9 1.9 collective-permute-start
  23.9 3.6 %collective-permute-start.1 = (bf16[4,128,512]{2,1,0:T(8,128)(2,1)}, bf16[4,128,512]{2,1,0:T(8,128)(2,1)}, u32[]{:S(2)}, u32[]{:S(2)}) collective-permute-start(bf16[4,128,512]{2,1,0:T(8,128)(2,1)} %get-tuple-element.52), channel_id=1, source_target_pairs={{0,4},{2,6},{4,0},{6,2},{1,5},{3,7},{5,1},{7,3},{8,12},{10,14},{12... | collective-permute-start | bytes 1572872 | tf_op jit(solution)/shard_map/move/ppermute | solution.py:17
  27.5 1.5 copy.12
  28.9 8.0 %collective-permute-done = bf16[4,128,512]{2,1,0:T(8,128)(2,1)S(1)} collective-permute-done((bf16[4,128,512]{2,1,0:T(8,128)(2,1)}, bf16[4,128,512]{2,1,0:T(8,128)(2,1)S(1)}, u32[]{:S(2)}, u32[]{:S(2)}) %collective-permute-start) | collective-permute-done | bytes 524320 | tf_op jit(solution)/shard_map/move/ppermute | solution.py:17
  37.0 13.5 %collective-permute-done.1 = bf16[4,128,512]{2,1,0:T(8,128)(2,1)} collective-permute-done((bf16[4,128,512]{2,1,0:T(8,128)(2,1)}, bf16[4,128,512]{2,1,0:T(8,128)(2,1)}, u32[]{:S(2)}, u32[]{:S(2)}) %collective-permute-start.1) | collective-permute-done | bytes 524320 | tf_op jit(solution)/shard_map/move/ppermute | solution.py:17
  50.5 2.6 collective-permute-done.2
  53.1 1.3 copy-done.2
  54.4 4.7 %all-to-all-start.1 = ((bf16[4,4,128,512]{3,2,1,0:T(8,128)(2,1)}), bf16[4,4,128,512]{3,2,1,0:T(8,128)(2,1)S(1)}, u32[]{:S(2)}, u32[]{:S(2)}) async-start(bf16[4,4,128,512]{3,2,1,0:T(8,128)(2,1)} %get-tuple-element.55), calls=%async_computation.1 | async-start | bytes 4194304 | tf_op jit(solution)/shard_map/move/all_to_all | solution.py:32
  59.2 1.7 collective-permute-start.3
  60.8 2.9 %collective-permute-start.4 = (bf16[448,256]{1,0:T(8,128)(2,1)S(1)}, bf16[448,256]{1,0:T(8,128)(2,1)S(1)}, u32[]{:S(2)}, u32[]{:S(2)}) collective-permute-start(bf16[448,256]{1,0:T(8,128)(2,1)S(1)} %get-tuple-element.102), channel_id=1, source_target_pairs={{0,64},{32,96},{64,0},{96,32},{1,65},{33,97},{65,1},{97,33},{2,66}... | collective-permute-start | bytes 688136 | tf_op jit(solution)/shard_map/move/ppermute | solution.py:17
  63.9 3.0 %pad_maximum_fusion = bf16[4,4,128,512]{3,2,0,1:T(8,128)(2,1)} fusion(bf16[4,1,128,512]{3,2,0,1:T(8,128)(2,1)} %bitcast.11, bf16[4,1,128,512]{3,2,0,1:T(8,128)(2,1)} %bitcast.10, bf16[4,1,128,512]{3,2,0,1:T(8,128)(2,1)S(1)} %bitcast.56, bf16[4,1,128,512]{3,2,0,1:T(8,128)(2,1)S(1)} %bitcast.55), kind=kLoop, calls=%fused_computation | loop fusion | flops 3145728 | bytes 4194304 | tf_op jit(solution)/shard_map/move/stack | solution.py:147
  66.9 9.2 %collective-permute-done.4 = bf16[448,256]{1,0:T(8,128)(2,1)S(1)} collective-permute-done((bf16[448,256]{1,0:T(8,128)(2,1)S(1)}, bf16[448,256]{1,0:T(8,128)(2,1)S(1)}, u32[]{:S(2)}, u32[]{:S(2)}) %collective-permute-start.4) | collective-permute-done | bytes 229408 | tf_op jit(solution)/shard_map/move/ppermute | solution.py:17
  76.1 2.4 collective-permute-done.5
  78.6 4.8 %all-to-all-done.1 = bf16[4,4,128,512]{3,2,1,0:T(8,128)(2,1)S(1)} async-done(((bf16[4,4,128,512]{3,2,1,0:T(8,128)(2,1)}), bf16[4,4,128,512]{3,2,1,0:T(8,128)(2,1)S(1)}, u32[]{:S(2)}, u32[]{:S(2)}) %all-to-all-start.1) | async-done | bytes 2097184 | tf_op jit(solution)/shard_map/move/all_to_all | solution.py:32
  83.4 3.9 %copy.13 = bf16[4,4,128,512]{3,2,1,0:T(8,128)(2,1)} copy(bf16[4,4,128,512]{3,2,0,1:T(8,128)(2,1)} %pad_maximum_fusion) | data formatting | bytes 4194304 | tf_op jit(solution)/shard_map/move/optimization_barrier | solution.py:135
  87.3 3.6 %all-to-all-start.2 = ((bf16[4,4,128,512]{3,2,1,0:T(8,128)(2,1)}), bf16[4,4,128,512]{3,2,1,0:T(8,128)(2,1)S(1)}, u32[]{:S(2)}, u32[]{:S(2)}) async-start(bf16[4,4,128,512]{3,2,1,0:T(8,128)(2,1)} %copy.13), calls=%async_computation.2 | async-start | bytes 4194304 | tf_op jit(solution)/shard_map/move/all_to_all | solution.py:32
  90.9 3.0 %dynamic-slice_bitcast_fusion = (bf16[4,128,512]{2,1,0:T(8,128)(2,1)}, bf16[4,128,512]{2,1,0:T(8,128)(2,1)}, bf16[4,128,512]{2,1,0:T(8,128)(2,1)}, bf16[4,128,512]{2,1,0:T(8,128)(2,1)}) fusion(bf16[4,4,128,512]{3,2,1,0:T(8,128)(2,1)} %copy-done.1, s32[]{:T(128)S(6)} %select_n.110, s32[]{:T(128)S(6)} %select_n.109, s32[]{:T(128)S(6)} %select_n.108, ...), kind=kLoop, calls=%fused_computation.3 | loop fusion | bytes 4194320 | tf_op jit(solution)/shard_map/move/jit(dynamic_index_in_dim)/squeeze | solution.py:28
  93.9 2.0 collective-permute-start.7
  96.0 2.7 %collective-permute-start.8 = (bf16[4,128,512]{2,1,0:T(8,128)(2,1)}, bf16[4,128,512]{2,1,0:T(8,128)(2,1)}, u32[]{:S(2)}, u32[]{:S(2)}) collective-permute-start(bf16[4,128,512]{2,1,0:T(8,128)(2,1)} %get-tuple-element.92), channel_id=1, source_target_pairs={{0,6},{2,4},{4,2},{6,0},{1,7},{3,5},{5,3},{7,1},{8,14},{10,12},{12... | collective-permute-start | bytes 1572872 | tf_op jit(solution)/shard_map/move/ppermute | solution.py:17
  98.6 1.7 bitcast_dynamic-update-slice_fusion
  100.3 8.7 %collective-permute-done.6.refs_1_ = bf16[4,128,512]{2,1,0:T(8,128)(2,1)S(1)} collective-permute-done((bf16[4,128,512]{2,1,0:T(8,128)(2,1)}, bf16[4,128,512]{2,1,0:T(8,128)(2,1)S(1)}, u32[]{:S(2)}, u32[]{:S(2)}) %collective-permute-start.6) | collective-permute-done | bytes 524320 | tf_op jit(solution)/shard_map/move/ppermute | solution.py:17
  109.0 0.8 dynamic-slice_dynamic-update-slice_fusion.2
  109.8 6.5 %collective-permute-done.7.refs_2_ = bf16[4,128,512]{2,1,0:T(8,128)(2,1)} collective-permute-done((bf16[4,128,512]{2,1,0:T(8,128)(2,1)}, bf16[4,128,512]{2,1,0:T(8,128)(2,1)}, u32[]{:S(2)}, u32[]{:S(2)}) %collective-permute-start.7) | collective-permute-done | bytes 524320 | tf_op jit(solution)/shard_map/move/ppermute | solution.py:17
  116.3 1.7 dynamic-slice_dynamic-update-slice_fusion.1
  118.0 0.9 collective-permute-done.8.refs_3_
  118.8 1.7 dynamic-slice_dynamic-update-slice_fusion
  120.6 1.1 constant_dynamic-update-slice_fusion
  122.2 1.7 collective-permute-start.13
  124.1 2.8 %collective-permute-start.14 = (bf16[4,448,256]{2,1,0:T(8,128)(2,1)S(1)}, bf16[4,448,256]{2,1,0:T(8,128)(2,1)}, u32[]{:S(2)}, u32[]{:S(2)}) collective-permute-start(bf16[4,448,256]{2,1,0:T(8,128)(2,1)S(1)} %pad_maximum_fusion.1.refs_0_), channel_id=1, source_target_pairs={{0,16},{8,24},{16,0},{24,8},{1,17},{9,25},{17,1},{25,9},{2,18},{10... | collective-permute-start | bytes 2752520 | tf_op jit(solution)/shard_map/ppermute | solution.py:17
  129.0 6.5 %gather_blocks.1 = (bf16[448,512]{1,0:T(8,128)(2,1)}, bf16[448,512]{1,0:T(8,128)(2,1)}, bf16[448,512]{1,0:T(8,128)(2,1)}, bf16[448,512]{1,0:T(8,128)(2,1)}) custom-call(s32[28]{0:T(128)} %compare_select_fusion.7.kind_ref, s32[28]{0:T(128)} %get-tuple-element.90.index_ref, s32[28]{0:T(128)} %get-tuple-element.88.half_ref, ...), custom_call_target="tpu_custom_call" | custom-call | tf_op jit(solution)/shard_map/weight/gather_blocks/pallas_call | solution.py:120
  135.5 3.7 %collective-permute-start.11 = (bf16[448,512]{1,0:T(8,128)(2,1)}, bf16[448,512]{1,0:T(8,128)(2,1)S(1)}, u32[]{:S(2)}, u32[]{:S(2)}) collective-permute-start(bf16[448,512]{1,0:T(8,128)(2,1)} %get-tuple-element.67), channel_id=1, source_target_pairs={{0,4},{2,6},{4,0},{6,2},{1,5},{3,7},{5,1},{7,3},{8,12},{10,14},{12... | collective-permute-start | bytes 1376264 | tf_op jit(solution)/shard_map/weight/ppermute | solution.py:17
  139.2 6.2 %collective-permute-done.13.refs_1_ = bf16[4,448,256]{2,1,0:T(8,128)(2,1)S(1)} collective-permute-done((bf16[4,448,256]{2,1,0:T(8,128)(2,1)S(1)}, bf16[4,448,256]{2,1,0:T(8,128)(2,1)S(1)}, u32[]{:S(2)}, u32[]{:S(2)}) %collective-permute-start.13) | collective-permute-done | bytes 917536 | tf_op jit(solution)/shard_map/ppermute | solution.py:17
  145.4 1.0 copy-done.8
  146.3 2.5 collective-permute-start.12
  148.8 0.7 pad_add_fusion
  149.5 17.7 %collective-permute-done.14.refs_2_ = bf16[4,448,256]{2,1,0:T(8,128)(2,1)} collective-permute-done((bf16[4,448,256]{2,1,0:T(8,128)(2,1)S(1)}, bf16[4,448,256]{2,1,0:T(8,128)(2,1)}, u32[]{:S(2)}, u32[]{:S(2)}) %collective-permute-start.14) | collective-permute-done | bytes 917536 | tf_op jit(solution)/shard_map/ppermute | solution.py:17
  167.2 2.9 %collective-permute-done.15.refs_3_ = bf16[4,448,256]{2,1,0:T(8,128)(2,1)} collective-permute-done((bf16[4,448,256]{2,1,0:T(8,128)(2,1)S(1)}, bf16[4,448,256]{2,1,0:T(8,128)(2,1)}, u32[]{:S(2)}, u32[]{:S(2)}) %collective-permute-start.15) | collective-permute-done | bytes 917536 | tf_op jit(solution)/shard_map/ppermute | solution.py:17
  170.1 0.7 copy-done.4
  171.2 9.2 %project.3 = (bf16[4,448,256]{2,1,0:T(8,128)(2,1)}, bf16[4,448,256]{2,1,0:T(8,128)(2,1)}) custom-call(s32[3]{0:T(128)} %get-tuple-element.105.place_ref, bf16[8,4,128,2048]{3,2,1,0:T(8,128)(2,1)} %bitcast.48, bf16[448,512]{1,0:T(8,128)(2,1)} %get-tuple-element.70.refs_0_, bf16[448,512]{1,0:T(8,128)(2,1)} %copy-done.4, bf16[448,512]{1,0:T(8,128)(2,1)} %copy-done.5, ...), custom_call_target="tpu_custom_call" | custom-call | tf_op jit(solution)/shard_map/projected/project/pallas_call | solution.py:217
  180.3 0.9 collective-permute-start.16
  181.2 1.1 collective-permute-start.17
  182.3 9.1 %project.2 = (bf16[4,448,256]{2,1,0:T(8,128)(2,1)}, bf16[4,448,256]{2,1,0:T(8,128)(2,1)}) custom-call(s32[3]{0:T(128)} %get-tuple-element.104.place_ref, bf16[8,4,128,2048]{3,2,1,0:T(8,128)(2,1)} %bitcast.49, bf16[448,512]{1,0:T(8,128)(2,1)} %get-tuple-element.70.refs_0_, bf16[448,512]{1,0:T(8,128)(2,1)} %copy-done.4, bf16[448,512]{1,0:T(8,128)(2,1)} %copy-done.5, ...), custom_call_target="tpu_custom_call" | custom-call | tf_op jit(solution)/shard_map/projected/project/pallas_call | solution.py:217
  191.5 2.1 collective-permute-start.18
  193.5 0.6 pad_add_fusion.2.place_ref
  194.2 15.7 %gradient.1 = (bf16[448,512]{1,0:T(8,128)(2,1)}, bf16[448,512]{1,0:T(8,128)(2,1)}, bf16[448,512]{1,0:T(8,128)(2,1)}, bf16[448,512]{1,0:T(8,128)(2,1)}) custom-call(s32[2]{0:T(128)} %pad_add_fusion.2.place_ref, bf16[8,4,128,2048]{3,2,1,0:T(8,128)(2,1)} %bitcast.50, bf16[4,448,256]{2,1,0:T(8,128)(2,1)} %copy-done.3, bf16[4,448,256]{2,1,0:T(8,128)(2,1)} %copy-done.8, ...), custom_call_target="tpu_custom_call" | custom-call | tf_op jit(solution)/shard_map/grad/gradient/pallas_call | solution.py:270
  209.9 1.5 collective-permute-start.23
  211.4 2.9 %collective-permute-start.24 = (bf16[448,512]{1,0:T(8,128)(2,1)}, bf16[448,512]{1,0:T(8,128)(2,1)S(1)}, u32[]{:S(2)}, u32[]{:S(2)}) collective-permute-start(bf16[448,512]{1,0:T(8,128)(2,1)} %get-tuple-element.84), channel_id=1, source_target_pairs={{0,64},{32,96},{64,0},{96,32},{1,65},{33,97},{65,1},{97,33},{2,66}... | collective-permute-start | bytes 1376264 | tf_op jit(solution)/shard_map/grad/ppermute | solution.py:17
  214.6 7.3 %collective-permute-done.17 = bf16[4,448,256]{2,1,0:T(8,128)(2,1)S(1)} collective-permute-done((bf16[4,448,256]{2,1,0:T(8,128)(2,1)}, bf16[4,448,256]{2,1,0:T(8,128)(2,1)S(1)}, u32[]{:S(2)}, u32[]{:S(2)}) %collective-permute-start.17) | collective-permute-done | bytes 917536 | tf_op jit(solution)/shard_map/projected/ppermute | solution.py:17
  221.9 1.1 collective-permute-done.18
  223.6 0.7 collective-permute-start.19
  224.2 2.8 %collective-permute-start.20 = (bf16[448,256]{1,0:T(8,128)(2,1)S(1)}, bf16[448,256]{1,0:T(8,128)(2,1)S(1)}, u32[]{:S(2)}, u32[]{:S(2)}) collective-permute-start(bf16[448,256]{1,0:T(8,128)(2,1)S(1)} %get-tuple-element.98), channel_id=1, source_target_pairs={{0,32},{2,0},{4,96},{6,64},{32,34},{34,2},{36,98},{38,66},{64,36},... | collective-permute-start | bytes 688136 | tf_op jit(solution)/shard_map/ppermute | solution.py:345
  227.1 3.5 %collective-permute-start.21 = (bf16[448,256]{1,0:T(8,128)(2,1)S(1)}, bf16[448,256]{1,0:T(8,128)(2,1)S(1)}, u32[]{:S(2)}, u32[]{:S(2)}) collective-permute-start(bf16[448,256]{1,0:T(8,128)(2,1)S(1)} %get-tuple-element.97), channel_id=1, source_target_pairs={{0,64},{2,96},{4,0},{6,32},{32,66},{34,98},{36,2},{38,34},{64,68},... | collective-permute-start | bytes 688136 | tf_op jit(solution)/shard_map/ppermute | solution.py:345
  230.6 4.9 %collective-permute-done.24.refs_2_ = bf16[448,512]{1,0:T(8,128)(2,1)S(1)} collective-permute-done((bf16[448,512]{1,0:T(8,128)(2,1)}, bf16[448,512]{1,0:T(8,128)(2,1)S(1)}, u32[]{:S(2)}, u32[]{:S(2)}) %collective-permute-start.24) | collective-permute-done | bytes 458784 | tf_op jit(solution)/shard_map/grad/ppermute | solution.py:17
  235.8 7.2 %collective-permute-done.25.refs_3_ = bf16[448,512]{1,0:T(8,128)(2,1)S(1)} collective-permute-done((bf16[448,512]{1,0:T(8,128)(2,1)}, bf16[448,512]{1,0:T(8,128)(2,1)S(1)}, u32[]{:S(2)}, u32[]{:S(2)}) %collective-permute-start.25) | collective-permute-done | bytes 458784 | tf_op jit(solution)/shard_map/grad/ppermute | solution.py:17
  243.0 0.8 copy-done.15
  243.7 4.8 %assemble.3 = f32[512,1792]{1,0:T(8,128)} custom-call(s32[1]{0:T(128)} %bitcast.place_ref, bf16[448,512]{1,0:T(8,128)(2,1)} %get-tuple-element.82.refs_0_, bf16[448,512]{1,0:T(8,128)(2,1)} %copy-done.13, bf16[448,512]{1,0:T(8,128)(2,1)} %copy-done.14, bf16[448,512]{1,0:T(8,128)(2,1)} %copy-done.15), custom_call_target="tpu_custom_call" | custom-call | tf_op jit(solution)/shard_map/assemble/pallas_call | solution.py:301
  248.6 0.6 copy-done.16
  249.4 0.7 copy-done.19
  250.1 2.4 assemble.2
  (71 shorter events, 5.1 us)
Async XLA Ops:
  17.6 35.5 %all-to-all-start = ((bf16[4,128,2048]{2,1,0:T(8,128)(2,1)}), bf16[4,128,2048]{2,1,0:T(8,128)(2,1)S(1)}, u32[]{:S(2)}, u32[]{:S(2)}) async-start(bf16[4,128,2048]{2,1,0:T(8,128)(2,1)} %cut_tokens.1), calls=%async_computation | async-start | bytes 4194304 | tf_op jit(solution)/shard_map/move/all_to_all | solution.py:32
  21.9 148.2 %all-gather.3.cloned.1.call-start = ((), (), s32[]{:S(2)}) async-start(), calls=%async_computation.3 | async-start | bytes 18874368 | tf_op jit(solution)/shard_map/move/all_gather | solution.py:152
  21.9 15.0 %collective-permute-start = (bf16[4,128,512]{2,1,0:T(8,128)(2,1)}, bf16[4,128,512]{2,1,0:T(8,128)(2,1)S(1)}, u32[]{:S(2)}, u32[]{:S(2)}) collective-permute-start(bf16[4,128,512]{2,1,0:T(8,128)(2,1)} %get-tuple-element.51), channel_id=1, source_target_pairs={{0,2},{2,0},{4,6},{6,4},{1,3},{3,1},{5,7},{7,5},{8,10},{10,8},{12,... | collective-permute-start | bytes 1572872 | tf_op jit(solution)/shard_map/move/ppermute | solution.py:17
  23.9 26.6 %collective-permute-start.1 = (bf16[4,128,512]{2,1,0:T(8,128)(2,1)}, bf16[4,128,512]{2,1,0:T(8,128)(2,1)}, u32[]{:S(2)}, u32[]{:S(2)}) collective-permute-start(bf16[4,128,512]{2,1,0:T(8,128)(2,1)} %get-tuple-element.52), channel_id=1, source_target_pairs={{0,4},{2,6},{4,0},{6,2},{1,5},{3,7},{5,1},{7,3},{8,12},{10,14},{12... | collective-permute-start | bytes 1572872 | tf_op jit(solution)/shard_map/move/ppermute | solution.py:17
  27.5 25.6 %collective-permute-start.2 = (bf16[4,128,512]{2,1,0:T(8,128)(2,1)}, bf16[4,128,512]{2,1,0:T(8,128)(2,1)}, u32[]{:S(2)}, u32[]{:S(2)}) collective-permute-start(bf16[4,128,512]{2,1,0:T(8,128)(2,1)} %get-tuple-element.53), channel_id=1, source_target_pairs={{0,6},{2,4},{4,2},{6,0},{1,7},{3,5},{5,3},{7,1},{8,14},{10,12},{12... | collective-permute-start | bytes 1572872 | tf_op jit(solution)/shard_map/move/ppermute | solution.py:17
  37.0 16.1 %copy-start.11 = (bf16[4,128,512]{2,1,0:T(8,128)(2,1)}, bf16[4,128,512]{2,1,0:T(8,128)(2,1)S(1)}, u32[]{:S(2)}) copy-start(bf16[4,128,512]{2,1,0:T(8,128)(2,1)S(1)} %collective-permute-done) | copy-start | bytes 1572868
  53.1 1.3 copy-start.2
  54.4 9.5 %copy-start.10 = (bf16[4,128,512]{2,1,0:T(8,128)(2,1)S(1)}, bf16[4,128,512]{2,1,0:T(8,128)(2,1)}, u32[]{:S(2)}) copy-start(bf16[4,128,512]{2,1,0:T(8,128)(2,1)} %get-tuple-element.56) | copy-start | bytes 1572868
  54.4 28.9 %all-to-all-start.1 = ((bf16[4,4,128,512]{3,2,1,0:T(8,128)(2,1)}), bf16[4,4,128,512]{3,2,1,0:T(8,128)(2,1)S(1)}, u32[]{:S(2)}, u32[]{:S(2)}) async-start(bf16[4,4,128,512]{3,2,1,0:T(8,128)(2,1)} %get-tuple-element.55), calls=%async_computation.1 | async-start | bytes 4194304 | tf_op jit(solution)/shard_map/move/all_to_all | solution.py:32
  59.1 4.8 %copy-start.12 = (bf16[4,128,512]{2,1,0:T(8,128)(2,1)S(1)}, bf16[4,128,512]{2,1,0:T(8,128)(2,1)}, u32[]{:S(2)}) copy-start(bf16[4,128,512]{2,1,0:T(8,128)(2,1)} %copy-done.11) | copy-start | bytes 1572868
  59.2 7.8 %collective-permute-start.3 = (bf16[448,256]{1,0:T(8,128)(2,1)S(1)}, bf16[448,256]{1,0:T(8,128)(2,1)S(1)}, u32[]{:S(2)}, u32[]{:S(2)}) collective-permute-start(bf16[448,256]{1,0:T(8,128)(2,1)S(1)} %get-tuple-element.103), channel_id=1, source_target_pairs={{0,32},{32,0},{64,96},{96,64},{1,33},{33,1},{65,97},{97,65},{2,34}... | collective-permute-start | bytes 688136 | tf_op jit(solution)/shard_map/move/ppermute | solution.py:17
  60.8 15.3 %collective-permute-start.4 = (bf16[448,256]{1,0:T(8,128)(2,1)S(1)}, bf16[448,256]{1,0:T(8,128)(2,1)S(1)}, u32[]{:S(2)}, u32[]{:S(2)}) collective-permute-start(bf16[448,256]{1,0:T(8,128)(2,1)S(1)} %get-tuple-element.102), channel_id=1, source_target_pairs={{0,64},{32,96},{64,0},{96,32},{1,65},{33,97},{65,1},{97,33},{2,66}... | collective-permute-start | bytes 688136 | tf_op jit(solution)/shard_map/move/ppermute | solution.py:17
  63.7 14.8 %collective-permute-start.5 = (bf16[448,256]{1,0:T(8,128)(2,1)S(1)}, bf16[448,256]{1,0:T(8,128)(2,1)S(1)}, u32[]{:S(2)}, u32[]{:S(2)}) collective-permute-start(bf16[448,256]{1,0:T(8,128)(2,1)S(1)} %get-tuple-element.101), channel_id=1, source_target_pairs={{0,96},{32,64},{64,32},{96,0},{1,97},{33,65},{65,33},{97,1},{2,98}... | collective-permute-start | bytes 688136 | tf_op jit(solution)/shard_map/move/ppermute | solution.py:17
  78.6 48.3 %copy-start.3 = (bf16[4,448,256]{2,1,0:T(8,128)(2,1)}, bf16[4,448,256]{2,1,0:T(8,128)(2,1)S(1)}, u32[]{:S(2)}) copy-start(bf16[4,448,256]{2,1,0:T(8,128)(2,1)S(1)} %pad_maximum_fusion.1.refs_0_) | copy-start | bytes 2752516
  83.4 3.9 %copy-start.1 = (bf16[4,4,128,512]{3,2,1,0:T(8,128)(2,1)}, bf16[4,4,128,512]{3,2,1,0:T(8,128)(2,1)S(1)}, u32[]{:S(2)}) copy-start(bf16[4,4,128,512]{3,2,1,0:T(8,128)(2,1)S(1)} %all-to-all-done.1) | copy-start | bytes 6291460
  87.3 33.3 %all-to-all-start.2 = ((bf16[4,4,128,512]{3,2,1,0:T(8,128)(2,1)}), bf16[4,4,128,512]{3,2,1,0:T(8,128)(2,1)S(1)}, u32[]{:S(2)}, u32[]{:S(2)}) async-start(bf16[4,4,128,512]{3,2,1,0:T(8,128)(2,1)} %copy.13), calls=%async_computation.2 | async-start | bytes 4194304 | tf_op jit(solution)/shard_map/move/all_to_all | solution.py:32
  93.9 15.1 %collective-permute-start.6 = (bf16[4,128,512]{2,1,0:T(8,128)(2,1)}, bf16[4,128,512]{2,1,0:T(8,128)(2,1)S(1)}, u32[]{:S(2)}, u32[]{:S(2)}) collective-permute-start(bf16[4,128,512]{2,1,0:T(8,128)(2,1)} %get-tuple-element.94), channel_id=1, source_target_pairs={{0,2},{2,0},{4,6},{6,4},{1,3},{3,1},{5,7},{7,5},{8,10},{10,8},{12,... | collective-permute-start | bytes 1572872 | tf_op jit(solution)/shard_map/move/ppermute | solution.py:17
  93.9 22.3 %collective-permute-start.7 = (bf16[4,128,512]{2,1,0:T(8,128)(2,1)}, bf16[4,128,512]{2,1,0:T(8,128)(2,1)}, u32[]{:S(2)}, u32[]{:S(2)}) collective-permute-start(bf16[4,128,512]{2,1,0:T(8,128)(2,1)} %get-tuple-element.93), channel_id=1, source_target_pairs={{0,4},{2,6},{4,0},{6,2},{1,5},{3,7},{5,1},{7,3},{8,12},{10,14},{12... | collective-permute-start | bytes 1572872 | tf_op jit(solution)/shard_map/move/ppermute | solution.py:17
  96.0 22.9 %collective-permute-start.8 = (bf16[4,128,512]{2,1,0:T(8,128)(2,1)}, bf16[4,128,512]{2,1,0:T(8,128)(2,1)}, u32[]{:S(2)}, u32[]{:S(2)}) collective-permute-start(bf16[4,128,512]{2,1,0:T(8,128)(2,1)} %get-tuple-element.92), channel_id=1, source_target_pairs={{0,6},{2,4},{4,2},{6,0},{1,7},{3,5},{5,3},{7,1},{8,14},{10,12},{12... | collective-permute-start | bytes 1572872 | tf_op jit(solution)/shard_map/move/ppermute | solution.py:17
  109.0 12.7 %copy-start.7 = (bf16[4,128,512]{2,1,0:T(8,128)(2,1)}, bf16[4,128,512]{2,1,0:T(8,128)(2,1)S(1)}, u32[]{:S(2)}) copy-start(bf16[4,128,512]{2,1,0:T(8,128)(2,1)S(1)} %collective-permute-done.6.refs_1_) | copy-start | bytes 1572868
  120.5 3.4 %slice-start = ((s32[129]{0:T(256)}), s32[128]{0:T(128)S(1)}, s32[]{:S(2)}) async-start(s32[129]{0:T(256)} %param.7), calls=%async_computation.4 | async-start | bytes 1024 | tf_op jit(solution)/shard_map/weight/slice | solution.py:171
  120.5 1.7 copy-start
  122.2 6.8 %collective-permute-start.9 = (bf16[16,128,512]{2,1,0:T(8,128)(2,1)}, bf16[16,128,512]{2,1,0:T(8,128)(2,1)}, u32[]{:S(2)}, u32[]{:S(2)}) collective-permute-start(bf16[16,128,512]{2,1,0:T(8,128)(2,1)} %constant_dynamic-update-slice_fusion), channel_id=1, source_target_pairs={{0,1},{1,0},{2,3},{3,2},{4,5},{5,4},{6,7},{7,6},{8,9},{9,8},{10,11... | collective-permute-start | bytes 6291464 | tf_op jit(solution)/shard_map/weight/ppermute | solution.py:164
  122.2 23.1 %collective-permute-start.13 = (bf16[4,448,256]{2,1,0:T(8,128)(2,1)S(1)}, bf16[4,448,256]{2,1,0:T(8,128)(2,1)S(1)}, u32[]{:S(2)}, u32[]{:S(2)}) collective-permute-start(bf16[4,448,256]{2,1,0:T(8,128)(2,1)S(1)} %pad_maximum_fusion.1.refs_0_), channel_id=1, source_target_pairs={{0,8},{8,0},{16,24},{24,16},{1,9},{9,1},{17,25},{25,17},{2,10},{10... | collective-permute-start | bytes 2752520 | tf_op jit(solution)/shard_map/ppermute | solution.py:17
  124.1 43.1 %collective-permute-start.14 = (bf16[4,448,256]{2,1,0:T(8,128)(2,1)S(1)}, bf16[4,448,256]{2,1,0:T(8,128)(2,1)}, u32[]{:S(2)}, u32[]{:S(2)}) collective-permute-start(bf16[4,448,256]{2,1,0:T(8,128)(2,1)S(1)} %pad_maximum_fusion.1.refs_0_), channel_id=1, source_target_pairs={{0,16},{8,24},{16,0},{24,8},{1,17},{9,25},{17,1},{25,9},{2,18},{10... | collective-permute-start | bytes 2752520 | tf_op jit(solution)/shard_map/ppermute | solution.py:17
  126.9 43.2 %collective-permute-start.15 = (bf16[4,448,256]{2,1,0:T(8,128)(2,1)S(1)}, bf16[4,448,256]{2,1,0:T(8,128)(2,1)}, u32[]{:S(2)}, u32[]{:S(2)}) collective-permute-start(bf16[4,448,256]{2,1,0:T(8,128)(2,1)S(1)} %pad_maximum_fusion.1.refs_0_), channel_id=1, source_target_pairs={{0,24},{8,16},{16,8},{24,0},{1,25},{9,17},{17,9},{25,1},{2,26},{10... | collective-permute-start | bytes 2752520 | tf_op jit(solution)/shard_map/ppermute | solution.py:17
  135.5 34.6 %collective-permute-start.10 = (bf16[448,512]{1,0:T(8,128)(2,1)}, bf16[448,512]{1,0:T(8,128)(2,1)S(1)}, u32[]{:S(2)}, u32[]{:S(2)}) collective-permute-start(bf16[448,512]{1,0:T(8,128)(2,1)} %get-tuple-element.66), channel_id=1, source_target_pairs={{0,2},{2,0},{4,6},{6,4},{1,3},{3,1},{5,7},{7,5},{8,10},{10,8},{12,... | collective-permute-start | bytes 1376264 | tf_op jit(solution)/shard_map/weight/ppermute | solution.py:17
  135.5 34.6 %collective-permute-start.11 = (bf16[448,512]{1,0:T(8,128)(2,1)}, bf16[448,512]{1,0:T(8,128)(2,1)S(1)}, u32[]{:S(2)}, u32[]{:S(2)}) collective-permute-start(bf16[448,512]{1,0:T(8,128)(2,1)} %get-tuple-element.67), channel_id=1, source_target_pairs={{0,4},{2,6},{4,0},{6,2},{1,5},{3,7},{5,1},{7,3},{8,12},{10,14},{12... | collective-permute-start | bytes 1376264 | tf_op jit(solution)/shard_map/weight/ppermute | solution.py:17
  145.4 1.0 copy-start.8
  146.3 23.7 %collective-permute-start.12 = (bf16[448,512]{1,0:T(8,128)(2,1)}, bf16[448,512]{1,0:T(8,128)(2,1)S(1)}, u32[]{:S(2)}, u32[]{:S(2)}) collective-permute-start(bf16[448,512]{1,0:T(8,128)(2,1)} %get-tuple-element.68), channel_id=1, source_target_pairs={{0,6},{2,4},{4,2},{6,0},{1,7},{3,5},{5,3},{7,1},{8,14},{10,12},{12... | collective-permute-start | bytes 1376264 | tf_op jit(solution)/shard_map/weight/ppermute | solution.py:17
  170.0 0.8 copy-start.4
  170.1 0.9 copy-start.5
  170.1 1.1 copy-start.6
  180.3 33.9 %collective-permute-start.16 = (bf16[4,448,256]{2,1,0:T(8,128)(2,1)}, bf16[4,448,256]{2,1,0:T(8,128)(2,1)S(1)}, u32[]{:S(2)}, u32[]{:S(2)}) collective-permute-start(bf16[4,448,256]{2,1,0:T(8,128)(2,1)} %get-tuple-element.75), channel_id=1, source_target_pairs={{0,16},{8,24},{16,0},{24,8},{1,17},{9,25},{17,1},{25,9},{2,18},{10... | collective-permute-start | bytes 2752520 | tf_op jit(solution)/shard_map/projected/ppermute | solution.py:17
  181.2 40.7 %collective-permute-start.17 = (bf16[4,448,256]{2,1,0:T(8,128)(2,1)}, bf16[4,448,256]{2,1,0:T(8,128)(2,1)S(1)}, u32[]{:S(2)}, u32[]{:S(2)}) collective-permute-start(bf16[4,448,256]{2,1,0:T(8,128)(2,1)} %get-tuple-element.76), channel_id=1, source_target_pairs={{0,8},{8,0},{16,24},{24,16},{1,9},{9,1},{17,25},{25,17},{2,10},{10... | collective-permute-start | bytes 2752520 | tf_op jit(solution)/shard_map/projected/ppermute | solution.py:17
  191.5 31.6 %collective-permute-start.18 = (bf16[4,448,256]{2,1,0:T(8,128)(2,1)}, bf16[4,448,256]{2,1,0:T(8,128)(2,1)S(1)}, u32[]{:S(2)}, u32[]{:S(2)}) collective-permute-start(bf16[4,448,256]{2,1,0:T(8,128)(2,1)} %get-tuple-element.77), channel_id=1, source_target_pairs={{0,24},{8,16},{16,8},{24,0},{1,25},{9,17},{17,9},{25,1},{2,26},{10... | collective-permute-start | bytes 2752520 | tf_op jit(solution)/shard_map/projected/ppermute | solution.py:17
  194.2 28.9 %copy-start.9 = (bf16[4,448,256]{2,1,0:T(8,128)(2,1)S(1)}, bf16[4,448,256]{2,1,0:T(8,128)(2,1)}, u32[]{:S(2)}) copy-start(bf16[4,448,256]{2,1,0:T(8,128)(2,1)} %get-tuple-element.74) | copy-start | bytes 2752516
  209.9 17.2 %collective-permute-start.23 = (bf16[448,512]{1,0:T(8,128)(2,1)}, bf16[448,512]{1,0:T(8,128)(2,1)S(1)}, u32[]{:S(2)}, u32[]{:S(2)}) collective-permute-start(bf16[448,512]{1,0:T(8,128)(2,1)} %get-tuple-element.83), channel_id=1, source_target_pairs={{0,32},{32,0},{64,96},{96,64},{1,33},{33,1},{65,97},{97,65},{2,34}... | collective-permute-start | bytes 1376264 | tf_op jit(solution)/shard_map/grad/ppermute | solution.py:17
  211.4 24.1 %collective-permute-start.24 = (bf16[448,512]{1,0:T(8,128)(2,1)}, bf16[448,512]{1,0:T(8,128)(2,1)S(1)}, u32[]{:S(2)}, u32[]{:S(2)}) collective-permute-start(bf16[448,512]{1,0:T(8,128)(2,1)} %get-tuple-element.84), channel_id=1, source_target_pairs={{0,64},{32,96},{64,0},{96,32},{1,65},{33,97},{65,1},{97,33},{2,66}... | collective-permute-start | bytes 1376264 | tf_op jit(solution)/shard_map/grad/ppermute | solution.py:17
  214.2 28.7 %collective-permute-start.25 = (bf16[448,512]{1,0:T(8,128)(2,1)}, bf16[448,512]{1,0:T(8,128)(2,1)S(1)}, u32[]{:S(2)}, u32[]{:S(2)}) collective-permute-start(bf16[448,512]{1,0:T(8,128)(2,1)} %get-tuple-element.85), channel_id=1, source_target_pairs={{0,96},{32,64},{64,32},{96,0},{1,97},{33,65},{65,33},{97,1},{2,98}... | collective-permute-start | bytes 1376264 | tf_op jit(solution)/shard_map/grad/ppermute | solution.py:17
  223.6 25.0 %collective-permute-start.19 = (bf16[448,256]{1,0:T(8,128)(2,1)S(1)}, bf16[448,256]{1,0:T(8,128)(2,1)S(1)}, u32[]{:S(2)}, u32[]{:S(2)}) collective-permute-start(bf16[448,256]{1,0:T(8,128)(2,1)S(1)} %get-tuple-element.99), channel_id=1, source_target_pairs={{0,0},{2,32},{4,64},{6,96},{32,2},{34,34},{36,66},{38,98},{64,4},{... | collective-permute-start | bytes 688136 | tf_op jit(solution)/shard_map/ppermute | solution.py:345
  224.2 24.3 %collective-permute-start.20 = (bf16[448,256]{1,0:T(8,128)(2,1)S(1)}, bf16[448,256]{1,0:T(8,128)(2,1)S(1)}, u32[]{:S(2)}, u32[]{:S(2)}) collective-permute-start(bf16[448,256]{1,0:T(8,128)(2,1)S(1)} %get-tuple-element.98), channel_id=1, source_target_pairs={{0,32},{2,0},{4,96},{6,64},{32,34},{34,2},{36,98},{38,66},{64,36},... | collective-permute-start | bytes 688136 | tf_op jit(solution)/shard_map/ppermute | solution.py:345
  227.1 15.9 %copy-start.13 = (bf16[448,512]{1,0:T(8,128)(2,1)}, bf16[448,512]{1,0:T(8,128)(2,1)S(1)}, u32[]{:S(2)}) copy-start(bf16[448,512]{1,0:T(8,128)(2,1)S(1)} %collective-permute-done.23.refs_1_) | copy-start | bytes 1376260
  227.1 21.5 %collective-permute-start.21 = (bf16[448,256]{1,0:T(8,128)(2,1)S(1)}, bf16[448,256]{1,0:T(8,128)(2,1)S(1)}, u32[]{:S(2)}, u32[]{:S(2)}) collective-permute-start(bf16[448,256]{1,0:T(8,128)(2,1)S(1)} %get-tuple-element.97), channel_id=1, source_target_pairs={{0,64},{2,96},{4,0},{6,32},{32,66},{34,98},{36,2},{38,34},{64,68},... | collective-permute-start | bytes 688136 | tf_op jit(solution)/shard_map/ppermute | solution.py:345
  235.5 7.5 %copy-start.14 = (bf16[448,512]{1,0:T(8,128)(2,1)}, bf16[448,512]{1,0:T(8,128)(2,1)S(1)}, u32[]{:S(2)}) copy-start(bf16[448,512]{1,0:T(8,128)(2,1)S(1)} %collective-permute-done.24.refs_2_) | copy-start | bytes 1376260
  235.5 13.1 %collective-permute-start.22 = (bf16[448,256]{1,0:T(8,128)(2,1)S(1)}, bf16[448,256]{1,0:T(8,128)(2,1)S(1)}, u32[]{:S(2)}, u32[]{:S(2)}) collective-permute-start(bf16[448,256]{1,0:T(8,128)(2,1)S(1)} %get-tuple-element.96), channel_id=1, source_target_pairs={{0,96},{2,64},{4,32},{6,0},{32,98},{34,66},{36,34},{38,2},{64,100}... | collective-permute-start | bytes 688136 | tf_op jit(solution)/shard_map/ppermute | solution.py:345
  243.0 0.8 copy-start.15
  248.5 0.7 copy-start.16
  248.6 0.8 copy-start.17
  248.6 0.8 copy-start.18
  249.4 0.7 copy-start.19
Sparse Core Ops, SparseCore 0:
  54.5 89.1 all-gather.2

commit v3 on v2

--- a/solution.py
+++ b/solution.py
@@ -135,6 +135,24 @@
     return lax.optimization_barrier(values)
 
 
+def stack_kernel(*refs):
+    for s, ref in enumerate(refs[:-1]):
+        refs[-1][0, s] = ref[0]
+
+
+def stack(parts):
+    count, rows, cols = parts[0].shape
+    return pl.pallas_call(
+        stack_kernel,
+        grid=(count,),
+        in_specs=[pl.BlockSpec((1, rows, cols), lambda i: (i, 0, 0))] * len(parts),
+        out_specs=pl.BlockSpec((1, len(parts), rows, cols), lambda i: (i, 0, 0, 0)),
+        out_shape=jax.ShapeDtypeStruct((count, len(parts), rows, cols), parts[0].dtype),
+        compiler_params=PARAMS,
+        name="stack",
+    )(*parts)
+
+
 def move(old_codes, old_scales, tokens, cotangent):
     y, x, z, c = (lax.axis_index(a) for a in AXES)
     first, *second = dequantize(old_codes, old_scales, z)
@@ -144,8 +162,7 @@
     first, tokens, cotangent, *second = together(first, tokens, cotangent, *second)
     first = all_to_all(first, "x")
     cot = jnp.stack(exchange([pick(cotangent, y ^ s) for s in range(RING)], "y"))
-    second = jnp.stack(second, axis=1)
-    first, second, cot = together(first, second, cot)
+    first, second, cot = together(first, stack(second), cot)
     firsts = exchange([pick(first, z ^ s, 1) for s in range(RING)], "z")
     second = all_to_all(second, "x")
     second, cot = together(second, cot)

time: 260 us -> 258 us (level)
  Pallas kernels: 56.7 us -> 60.8 us
  local copies, waits for them, and re-layouts: 22.4 us -> 18.9 us
  other arithmetic: 7.44 us -> 4.46 us
    pallas_call x0 -> x1, Pallas kernels: none -> 4.11 us  [stack(): pl.pallas_call(stack_kernel, grid=(count,), in_specs=[pl.BlockSpec((1, ro...]
    optimization_barrier x1 -> x0, local copies, waits for them, and re-layouts: 3.88 us -> none  [together(): return lax.optimization_barrier(values)]
    another operation x1 -> x0, other arithmetic: 2.98 us -> none  [move(): second = jnp.stack(second, axis=1)]
    unnamed x46 -> x42, local copies, waits for them, and re-layouts: 12.7 us -> 13.1 us
  transfers between devices with their start and end apart: 30 -> 30, of which waited for: 16 -> 17; matrix products, arithmetic and copies ran while one was open for 9% -> 6% of each run, Pallas kernels for 14% -> 16%
where the time goes in v3:
time: 258 us; the launch traced here: 257 us
  waiting for transfers between devices  105 us (41%)
  Pallas kernels  60.8 us (24%)
  starting transfers between devices  53.7 us (21%)
  local copies, waits for them, and re-layouts  18.9 us (7%)
  between operations  14.2 us (6%)
  other arithmetic  4.46 us (2%)
    ppermute x21, waiting for transfers between devices, swap(): return lax.ppermute(array, axis, [(i, i ^ s) for i in range(RING)])  98.8 us
    ppermute x21, starting transfers between devices, swap(): return lax.ppermute(array, axis, [(i, i ^ s) for i in range(RING)])  34.1 us
    pallas_call x2, Pallas kernels, project(): pl.pallas_call(project_kernel, grid_spec=pltpu.PrefetchScalarGridSpec(num...  18.3 us
    pallas_call x1, Pallas kernels, gradient(): pl.pallas_call(grad_kernel, grid_spec=pltpu.PrefetchScalarGridSpec(num_sc...  15.7 us
    unnamed x42, local copies, waits for them, and re-layouts  13.1 us
    all_to_all x3, starting transfers between devices, all_to_all(): return lax.all_to_all(array, axis, 0, 0, tiled=True)  12.5 us
    pallas_call x2, Pallas kernels, assemble(): pl.pallas_call(assemble_kernel, grid_spec=pltpu.PrefetchScalarGridSpec(nu...  7.21 us
    ppermute x4, starting transfers between devices, on_device(): done.append(lax.ppermute(pick(total, z ^ s), ('y', 'z'), pairs))  7.09 us
  transfers between devices with their start and end apart: 30, of which 17 were waited for; matrix products, arithmetic and copies ran while one was open for 6% of the time, Pallas kernels for 16%

profile of v3, /device:TPU:0, one launch (start us, length us, event | category | flops | bytes accessed | tf_op | source)
XLA Modules:
  0.0 256.8 jit_solution(15426443476598264776)
XLA Ops:
  7.2 0.7 convert_element_type.21
  7.9 0.7 copy.12
  8.6 5.2 %dequantize.1 = (bf16[4,4,128,512]{3,2,1,0:T(8,128)(2,1)}, bf16[4,128,512]{2,1,0:T(8,128)(2,1)}, bf16[4,128,512]{2,1,0:T(8,128)(2,1)}, bf16[4,128,512]{2,1,0:T(8,128)(2,1)}, bf16[4,128,512]{2,1,0:T(8,128)(2,1)}) custom-call(s32[1]{0:T(128)} %bitcast.1.place_ref, bf16[256,8192]{1,0:T(8,128)(2,1)} %codes_ref.1, f32[2,8192]{1,0:T(2,128)} %bitcast.51), custom_call_target="tpu_custom_call" | custom-call | tf_op jit(solution)/shard_map/move/dequantize/pallas_call | solution.py:85
  13.8 3.8 %cut_tokens.1 = bf16[4,128,2048]{2,1,0:T(8,128)(2,1)} custom-call(s32[1]{0:T(128)} %bitcast.4.place_ref, bf16[256,8192]{1,0:T(8,128)(2,1)} %tokens_ref), custom_call_target="tpu_custom_call" | custom-call | tf_op jit(solution)/shard_map/move/cut_tokens/pallas_call | solution.py:45
  17.6 4.4 %all-to-all-start = ((bf16[4,128,2048]{2,1,0:T(8,128)(2,1)}), bf16[4,128,2048]{2,1,0:T(8,128)(2,1)S(1)}, u32[]{:S(2)}, u32[]{:S(2)}) async-start(bf16[4,128,2048]{2,1,0:T(8,128)(2,1)} %cut_tokens.1), calls=%async_computation | async-start | bytes 4194304 | tf_op jit(solution)/shard_map/move/all_to_all | solution.py:32
  22.0 1.9 collective-permute-start
  23.9 3.6 %collective-permute-start.1 = (bf16[4,128,512]{2,1,0:T(8,128)(2,1)}, bf16[4,128,512]{2,1,0:T(8,128)(2,1)}, u32[]{:S(2)}, u32[]{:S(2)}) collective-permute-start(bf16[4,128,512]{2,1,0:T(8,128)(2,1)} %get-tuple-element.52), channel_id=1, source_target_pairs={{0,4},{2,6},{4,0},{6,2},{1,5},{3,7},{5,1},{7,3},{8,12},{10,14},{12... | collective-permute-start | bytes 1572872 | tf_op jit(solution)/shard_map/move/ppermute | solution.py:17
  27.5 1.5 copy.9
  29.0 8.0 %collective-permute-done.refs_1_ = bf16[4,128,512]{2,1,0:T(8,128)(2,1)S(1)} collective-permute-done((bf16[4,128,512]{2,1,0:T(8,128)(2,1)}, bf16[4,128,512]{2,1,0:T(8,128)(2,1)S(1)}, u32[]{:S(2)}, u32[]{:S(2)}) %collective-permute-start) | collective-permute-done | bytes 524320 | tf_op jit(solution)/shard_map/move/ppermute | solution.py:17
  37.0 13.5 %collective-permute-done.1.refs_2_ = bf16[4,128,512]{2,1,0:T(8,128)(2,1)} collective-permute-done((bf16[4,128,512]{2,1,0:T(8,128)(2,1)}, bf16[4,128,512]{2,1,0:T(8,128)(2,1)}, u32[]{:S(2)}, u32[]{:S(2)}) %collective-permute-start.1) | collective-permute-done | bytes 524320 | tf_op jit(solution)/shard_map/move/ppermute | solution.py:17
  50.5 2.6 %collective-permute-done.2.refs_3_ = bf16[4,128,512]{2,1,0:T(8,128)(2,1)} collective-permute-done((bf16[4,128,512]{2,1,0:T(8,128)(2,1)}, bf16[4,128,512]{2,1,0:T(8,128)(2,1)}, u32[]{:S(2)}, u32[]{:S(2)}) %collective-permute-start.2) | collective-permute-done | bytes 524320 | tf_op jit(solution)/shard_map/move/ppermute | solution.py:17
  53.1 1.3 copy-done.2
  54.4 4.5 %all-to-all-start.1 = ((bf16[4,4,128,512]{3,2,1,0:T(8,128)(2,1)}), bf16[4,4,128,512]{3,2,1,0:T(8,128)(2,1)S(1)}, u32[]{:S(2)}, u32[]{:S(2)}) async-start(bf16[4,4,128,512]{3,2,1,0:T(8,128)(2,1)} %get-tuple-element.55), calls=%async_computation.1 | async-start | bytes 4194304 | tf_op jit(solution)/shard_map/move/all_to_all | solution.py:32
  59.0 3.3 %collective-permute-start.4 = (bf16[448,256]{1,0:T(8,128)(2,1)S(1)}, bf16[448,256]{1,0:T(8,128)(2,1)S(1)}, u32[]{:S(2)}, u32[]{:S(2)}) collective-permute-start(bf16[448,256]{1,0:T(8,128)(2,1)S(1)} %get-tuple-element.102), channel_id=1, source_target_pairs={{0,64},{32,96},{64,0},{96,32},{1,65},{33,97},{65,1},{97,33},{2,66}... | collective-permute-start | bytes 688136 | tf_op jit(solution)/shard_map/move/ppermute | solution.py:17
  62.3 1.1 collective-permute-start.5
  63.4 4.1 %stack.53 = bf16[4,4,128,512]{3,2,1,0:T(8,128)(2,1)} custom-call(bf16[4,128,512]{2,1,0:T(8,128)(2,1)} %get-tuple-element.56.refs_0_, bf16[4,128,512]{2,1,0:T(8,128)(2,1)} %copy-done.10, bf16[4,128,512]{2,1,0:T(8,128)(2,1)} %collective-permute-done.1.refs_2_, bf16[4,128,512]{2,1,0:T(8,128)(2,1)} %collective-permute-done.2.refs_3_), custom_call_target="tpu_custom_call" | custom-call | tf_op jit(solution)/shard_map/move/stack/pallas_call | solution.py:145
  67.5 2.5 collective-permute-done.4
  69.9 3.9 %collective-permute-done.5 = bf16[448,256]{1,0:T(8,128)(2,1)S(1)} collective-permute-done((bf16[448,256]{1,0:T(8,128)(2,1)S(1)}, bf16[448,256]{1,0:T(8,128)(2,1)S(1)}, u32[]{:S(2)}, u32[]{:S(2)}) %collective-permute-start.5) | collective-permute-done | bytes 229408 | tf_op jit(solution)/shard_map/move/ppermute | solution.py:17
  73.8 3.5 %collective-permute-done.3 = bf16[448,256]{1,0:T(8,128)(2,1)S(1)} collective-permute-done((bf16[448,256]{1,0:T(8,128)(2,1)S(1)}, bf16[448,256]{1,0:T(8,128)(2,1)S(1)}, u32[]{:S(2)}, u32[]{:S(2)}) %collective-permute-start.3) | collective-permute-done | bytes 229408 | tf_op jit(solution)/shard_map/move/ppermute | solution.py:17
  77.4 5.8 %all-to-all-done.1 = bf16[4,4,128,512]{3,2,1,0:T(8,128)(2,1)S(1)} async-done(((bf16[4,4,128,512]{3,2,1,0:T(8,128)(2,1)}), bf16[4,4,128,512]{3,2,1,0:T(8,128)(2,1)S(1)}, u32[]{:S(2)}, u32[]{:S(2)}) %all-to-all-start.1) | async-done | bytes 2097184 | tf_op jit(solution)/shard_map/move/all_to_all | solution.py:32
  83.2 1.4 copy-done.1
  84.6 3.6 %all-to-all-start.2 = ((bf16[4,4,128,512]{3,2,1,0:T(8,128)(2,1)}), bf16[4,4,128,512]{3,2,1,0:T(8,128)(2,1)S(1)}, u32[]{:S(2)}, u32[]{:S(2)}) async-start(bf16[4,4,128,512]{3,2,1,0:T(8,128)(2,1)} %stack.53), calls=%async_computation.2 | async-start | bytes 4194304 | tf_op jit(solution)/shard_map/move/all_to_all | solution.py:32
  88.2 3.0 %dynamic-slice_bitcast_fusion = (bf16[4,128,512]{2,1,0:T(8,128)(2,1)}, bf16[4,128,512]{2,1,0:T(8,128)(2,1)}, bf16[4,128,512]{2,1,0:T(8,128)(2,1)}, bf16[4,128,512]{2,1,0:T(8,128)(2,1)}) fusion(bf16[4,4,128,512]{3,2,1,0:T(8,128)(2,1)} %copy-done.1, s32[]{:T(128)S(6)} %select_n.110, s32[]{:T(128)S(6)} %select_n.109, s32[]{:T(128)S(6)} %select_n.108, ...), kind=kLoop, calls=%fused_computation.2 | loop fusion | bytes 4194320 | tf_op jit(solution)/shard_map/move/jit(dynamic_index_in_dim)/squeeze | solution.py:28
  91.2 1.9 collective-permute-start.7
  93.1 2.8 %collective-permute-start.8 = (bf16[4,128,512]{2,1,0:T(8,128)(2,1)}, bf16[4,128,512]{2,1,0:T(8,128)(2,1)}, u32[]{:S(2)}, u32[]{:S(2)}) collective-permute-start(bf16[4,128,512]{2,1,0:T(8,128)(2,1)} %get-tuple-element.92), channel_id=1, source_target_pairs={{0,6},{2,4},{4,2},{6,0},{1,7},{3,5},{5,3},{7,1},{8,14},{10,12},{12... | collective-permute-start | bytes 1572872 | tf_op jit(solution)/shard_map/move/ppermute | solution.py:17
  95.9 1.7 bitcast_dynamic-update-slice_fusion
  97.6 8.7 %collective-permute-done.6.refs_1_ = bf16[4,128,512]{2,1,0:T(8,128)(2,1)S(1)} collective-permute-done((bf16[4,128,512]{2,1,0:T(8,128)(2,1)}, bf16[4,128,512]{2,1,0:T(8,128)(2,1)S(1)}, u32[]{:S(2)}, u32[]{:S(2)}) %collective-permute-start.6) | collective-permute-done | bytes 524320 | tf_op jit(solution)/shard_map/move/ppermute | solution.py:17
  106.3 0.8 dynamic-slice_dynamic-update-slice_fusion.2
  107.1 6.4 %collective-permute-done.7.refs_2_ = bf16[4,128,512]{2,1,0:T(8,128)(2,1)} collective-permute-done((bf16[4,128,512]{2,1,0:T(8,128)(2,1)}, bf16[4,128,512]{2,1,0:T(8,128)(2,1)}, u32[]{:S(2)}, u32[]{:S(2)}) %collective-permute-start.7) | collective-permute-done | bytes 524320 | tf_op jit(solution)/shard_map/move/ppermute | solution.py:17
  113.5 1.7 dynamic-slice_dynamic-update-slice_fusion.1
  115.2 0.9 collective-permute-done.8.refs_3_
  116.1 1.7 dynamic-slice_dynamic-update-slice_fusion
  117.9 1.1 constant_dynamic-update-slice_fusion
  119.5 1.6 collective-permute-start.13
  121.3 2.8 %collective-permute-start.14 = (bf16[4,448,256]{2,1,0:T(8,128)(2,1)S(1)}, bf16[4,448,256]{2,1,0:T(8,128)(2,1)}, u32[]{:S(2)}, u32[]{:S(2)}) collective-permute-start(bf16[4,448,256]{2,1,0:T(8,128)(2,1)S(1)} %pad_maximum_fusion.refs_0_), channel_id=1, source_target_pairs={{0,16},{8,24},{16,0},{24,8},{1,17},{9,25},{17,1},{25,9},{2,18},{10... | collective-permute-start | bytes 2752520 | tf_op jit(solution)/shard_map/ppermute | solution.py:17
  125.0 0.6 compare_select_fusion.6
  126.2 6.5 %gather_blocks.1 = (bf16[448,512]{1,0:T(8,128)(2,1)}, bf16[448,512]{1,0:T(8,128)(2,1)}, bf16[448,512]{1,0:T(8,128)(2,1)}, bf16[448,512]{1,0:T(8,128)(2,1)}) custom-call(s32[28]{0:T(128)} %compare_select_fusion.7.kind_ref, s32[28]{0:T(128)} %get-tuple-element.90.index_ref, s32[28]{0:T(128)} %get-tuple-element.88.half_ref, ...), custom_call_target="tpu_custom_call" | custom-call | tf_op jit(solution)/shard_map/weight/gather_blocks/pallas_call | solution.py:120
  132.7 3.6 %collective-permute-start.11 = (bf16[448,512]{1,0:T(8,128)(2,1)}, bf16[448,512]{1,0:T(8,128)(2,1)S(1)}, u32[]{:S(2)}, u32[]{:S(2)}) collective-permute-start(bf16[448,512]{1,0:T(8,128)(2,1)} %get-tuple-element.67), channel_id=1, source_target_pairs={{0,4},{2,6},{4,0},{6,2},{1,5},{3,7},{5,1},{7,3},{8,12},{10,14},{12... | collective-permute-start | bytes 1376264 | tf_op jit(solution)/shard_map/weight/ppermute | solution.py:17
  136.3 6.3 %collective-permute-done.13.refs_1_ = bf16[4,448,256]{2,1,0:T(8,128)(2,1)S(1)} collective-permute-done((bf16[4,448,256]{2,1,0:T(8,128)(2,1)S(1)}, bf16[4,448,256]{2,1,0:T(8,128)(2,1)S(1)}, u32[]{:S(2)}, u32[]{:S(2)}) %collective-permute-start.13) | collective-permute-done | bytes 917536 | tf_op jit(solution)/shard_map/ppermute | solution.py:17
  142.6 2.4 collective-permute-start.12
  145.0 0.6 pad_add_fusion
  145.6 18.8 %collective-permute-done.14.refs_2_ = bf16[4,448,256]{2,1,0:T(8,128)(2,1)} collective-permute-done((bf16[4,448,256]{2,1,0:T(8,128)(2,1)S(1)}, bf16[4,448,256]{2,1,0:T(8,128)(2,1)}, u32[]{:S(2)}, u32[]{:S(2)}) %collective-permute-start.14) | collective-permute-done | bytes 917536 | tf_op jit(solution)/shard_map/ppermute | solution.py:17
  164.4 2.9 %collective-permute-done.15.refs_3_ = bf16[4,448,256]{2,1,0:T(8,128)(2,1)} collective-permute-done((bf16[4,448,256]{2,1,0:T(8,128)(2,1)S(1)}, bf16[4,448,256]{2,1,0:T(8,128)(2,1)}, u32[]{:S(2)}, u32[]{:S(2)}) %collective-permute-start.15) | collective-permute-done | bytes 917536 | tf_op jit(solution)/shard_map/ppermute | solution.py:17
  167.3 0.7 copy-done.4
  168.4 9.2 %project.3 = (bf16[4,448,256]{2,1,0:T(8,128)(2,1)}, bf16[4,448,256]{2,1,0:T(8,128)(2,1)}) custom-call(s32[3]{0:T(128)} %get-tuple-element.105.place_ref, bf16[8,4,128,2048]{3,2,1,0:T(8,128)(2,1)} %bitcast.44, bf16[448,512]{1,0:T(8,128)(2,1)} %get-tuple-element.70.refs_0_, bf16[448,512]{1,0:T(8,128)(2,1)} %copy-done.4, bf16[448,512]{1,0:T(8,128)(2,1)} %copy-done.5, ...), custom_call_target="tpu_custom_call" | custom-call | tf_op jit(solution)/shard_map/projected/project/pallas_call | solution.py:234
  178.0 1.1 collective-permute-start.17
  179.1 9.1 %project.2 = (bf16[4,448,256]{2,1,0:T(8,128)(2,1)}, bf16[4,448,256]{2,1,0:T(8,128)(2,1)}) custom-call(s32[3]{0:T(128)} %get-tuple-element.104.place_ref, bf16[8,4,128,2048]{3,2,1,0:T(8,128)(2,1)} %bitcast.45, bf16[448,512]{1,0:T(8,128)(2,1)} %get-tuple-element.70.refs_0_, bf16[448,512]{1,0:T(8,128)(2,1)} %copy-done.4, bf16[448,512]{1,0:T(8,128)(2,1)} %copy-done.5, ...), custom_call_target="tpu_custom_call" | custom-call | tf_op jit(solution)/shard_map/projected/project/pallas_call | solution.py:234
  188.2 2.6 %collective-permute-start.18 = (bf16[4,448,256]{2,1,0:T(8,128)(2,1)}, bf16[4,448,256]{2,1,0:T(8,128)(2,1)S(1)}, u32[]{:S(2)}, u32[]{:S(2)}) collective-permute-start(bf16[4,448,256]{2,1,0:T(8,128)(2,1)} %get-tuple-element.77), channel_id=1, source_target_pairs={{0,24},{8,16},{16,8},{24,0},{1,25},{9,17},{17,9},{25,1},{2,26},{10... | collective-permute-start | bytes 2752520 | tf_op jit(solution)/shard_map/projected/ppermute | solution.py:17
  190.8 0.6 pad_add_fusion.2.place_ref
  191.4 15.7 %gradient.1 = (bf16[448,512]{1,0:T(8,128)(2,1)}, bf16[448,512]{1,0:T(8,128)(2,1)}, bf16[448,512]{1,0:T(8,128)(2,1)}, bf16[448,512]{1,0:T(8,128)(2,1)}) custom-call(s32[2]{0:T(128)} %pad_add_fusion.2.place_ref, bf16[8,4,128,2048]{3,2,1,0:T(8,128)(2,1)} %bitcast.46, bf16[4,448,256]{2,1,0:T(8,128)(2,1)} %copy-done.3, bf16[4,448,256]{2,1,0:T(8,128)(2,1)} %copy-done.8, ...), custom_call_target="tpu_custom_call" | custom-call | tf_op jit(solution)/shard_map/grad/gradient/pallas_call | solution.py:287
  207.1 1.6 collective-permute-start.23
  208.7 2.9 %collective-permute-start.24 = (bf16[448,512]{1,0:T(8,128)(2,1)}, bf16[448,512]{1,0:T(8,128)(2,1)S(1)}, u32[]{:S(2)}, u32[]{:S(2)}) collective-permute-start(bf16[448,512]{1,0:T(8,128)(2,1)} %get-tuple-element.84), channel_id=1, source_target_pairs={{0,64},{32,96},{64,0},{96,32},{1,65},{33,97},{65,1},{97,33},{2,66}... | collective-permute-start | bytes 1376264 | tf_op jit(solution)/shard_map/grad/ppermute | solution.py:17
  211.8 6.8 %collective-permute-done.17 = bf16[4,448,256]{2,1,0:T(8,128)(2,1)S(1)} collective-permute-done((bf16[4,448,256]{2,1,0:T(8,128)(2,1)}, bf16[4,448,256]{2,1,0:T(8,128)(2,1)S(1)}, u32[]{:S(2)}, u32[]{:S(2)}) %collective-permute-start.17) | collective-permute-done | bytes 917536 | tf_op jit(solution)/shard_map/projected/ppermute | solution.py:17
  218.6 1.7 collective-permute-done.18
  220.8 0.7 collective-permute-start.19
  221.5 2.9 %collective-permute-start.20 = (bf16[448,256]{1,0:T(8,128)(2,1)S(1)}, bf16[448,256]{1,0:T(8,128)(2,1)S(1)}, u32[]{:S(2)}, u32[]{:S(2)}) collective-permute-start(bf16[448,256]{1,0:T(8,128)(2,1)S(1)} %get-tuple-element.98), channel_id=1, source_target_pairs={{0,32},{2,0},{4,96},{6,64},{32,34},{34,2},{36,98},{38,66},{64,36},... | collective-permute-start | bytes 688136 | tf_op jit(solution)/shard_map/ppermute | solution.py:362
  224.4 3.4 %collective-permute-start.21 = (bf16[448,256]{1,0:T(8,128)(2,1)S(1)}, bf16[448,256]{1,0:T(8,128)(2,1)S(1)}, u32[]{:S(2)}, u32[]{:S(2)}) collective-permute-start(bf16[448,256]{1,0:T(8,128)(2,1)S(1)} %get-tuple-element.97), channel_id=1, source_target_pairs={{0,64},{2,96},{4,0},{6,32},{32,66},{34,98},{36,2},{38,34},{64,68},... | collective-permute-start | bytes 688136 | tf_op jit(solution)/shard_map/ppermute | solution.py:362
  227.7 5.1 %collective-permute-done.24.refs_2_ = bf16[448,512]{1,0:T(8,128)(2,1)S(1)} collective-permute-done((bf16[448,512]{1,0:T(8,128)(2,1)}, bf16[448,512]{1,0:T(8,128)(2,1)S(1)}, u32[]{:S(2)}, u32[]{:S(2)}) %collective-permute-start.24) | collective-permute-done | bytes 458784 | tf_op jit(solution)/shard_map/grad/ppermute | solution.py:17
  233.1 7.3 %collective-permute-done.25.refs_3_ = bf16[448,512]{1,0:T(8,128)(2,1)S(1)} collective-permute-done((bf16[448,512]{1,0:T(8,128)(2,1)}, bf16[448,512]{1,0:T(8,128)(2,1)S(1)}, u32[]{:S(2)}, u32[]{:S(2)}) %collective-permute-start.25) | collective-permute-done | bytes 458784 | tf_op jit(solution)/shard_map/grad/ppermute | solution.py:17
  240.4 0.8 copy-done.13
  241.1 4.8 %assemble.3 = f32[512,1792]{1,0:T(8,128)} custom-call(s32[1]{0:T(128)} %bitcast.place_ref, bf16[448,512]{1,0:T(8,128)(2,1)} %get-tuple-element.82.refs_0_, bf16[448,512]{1,0:T(8,128)(2,1)} %copy-done.11, bf16[448,512]{1,0:T(8,128)(2,1)} %copy-done.12, bf16[448,512]{1,0:T(8,128)(2,1)} %copy-done.13), custom_call_target="tpu_custom_call" | custom-call | tf_op jit(solution)/shard_map/assemble/pallas_call | solution.py:318
  246.0 0.6 copy-done.14
  246.8 0.7 copy-done.17
  247.5 2.4 assemble.2
  (66 shorter events, 4.5 us)
Async XLA Ops:
  17.6 35.5 %all-to-all-start = ((bf16[4,128,2048]{2,1,0:T(8,128)(2,1)}), bf16[4,128,2048]{2,1,0:T(8,128)(2,1)S(1)}, u32[]{:S(2)}, u32[]{:S(2)}) async-start(bf16[4,128,2048]{2,1,0:T(8,128)(2,1)} %cut_tokens.1), calls=%async_computation | async-start | bytes 4194304 | tf_op jit(solution)/shard_map/move/all_to_all | solution.py:32
  22.0 145.4 %all-gather.3.cloned.1.call-start = ((), (), s32[]{:S(2)}) async-start(), calls=%async_computation.3 | async-start | bytes 18874368 | tf_op jit(solution)/shard_map/move/all_gather | solution.py:169
  22.0 15.0 %collective-permute-start = (bf16[4,128,512]{2,1,0:T(8,128)(2,1)}, bf16[4,128,512]{2,1,0:T(8,128)(2,1)S(1)}, u32[]{:S(2)}, u32[]{:S(2)}) collective-permute-start(bf16[4,128,512]{2,1,0:T(8,128)(2,1)} %get-tuple-element.51), channel_id=1, source_target_pairs={{0,2},{2,0},{4,6},{6,4},{1,3},{3,1},{5,7},{7,5},{8,10},{10,8},{12,... | collective-permute-start | bytes 1572872 | tf_op jit(solution)/shard_map/move/ppermute | solution.py:17
  23.9 26.6 %collective-permute-start.1 = (bf16[4,128,512]{2,1,0:T(8,128)(2,1)}, bf16[4,128,512]{2,1,0:T(8,128)(2,1)}, u32[]{:S(2)}, u32[]{:S(2)}) collective-permute-start(bf16[4,128,512]{2,1,0:T(8,128)(2,1)} %get-tuple-element.52), channel_id=1, source_target_pairs={{0,4},{2,6},{4,0},{6,2},{1,5},{3,7},{5,1},{7,3},{8,12},{10,14},{12... | collective-permute-start | bytes 1572872 | tf_op jit(solution)/shard_map/move/ppermute | solution.py:17
  27.5 25.6 %collective-permute-start.2 = (bf16[4,128,512]{2,1,0:T(8,128)(2,1)}, bf16[4,128,512]{2,1,0:T(8,128)(2,1)}, u32[]{:S(2)}, u32[]{:S(2)}) collective-permute-start(bf16[4,128,512]{2,1,0:T(8,128)(2,1)} %get-tuple-element.53), channel_id=1, source_target_pairs={{0,6},{2,4},{4,2},{6,0},{1,7},{3,5},{5,3},{7,1},{8,14},{10,12},{12... | collective-permute-start | bytes 1572872 | tf_op jit(solution)/shard_map/move/ppermute | solution.py:17
  37.0 26.3 %copy-start.10 = (bf16[4,128,512]{2,1,0:T(8,128)(2,1)}, bf16[4,128,512]{2,1,0:T(8,128)(2,1)S(1)}, u32[]{:S(2)}) copy-start(bf16[4,128,512]{2,1,0:T(8,128)(2,1)S(1)} %collective-permute-done.refs_1_) | copy-start | bytes 1572868
  53.1 1.3 copy-start.2
  54.4 28.8 %all-to-all-start.1 = ((bf16[4,4,128,512]{3,2,1,0:T(8,128)(2,1)}), bf16[4,4,128,512]{3,2,1,0:T(8,128)(2,1)S(1)}, u32[]{:S(2)}, u32[]{:S(2)}) async-start(bf16[4,4,128,512]{3,2,1,0:T(8,128)(2,1)} %get-tuple-element.55), calls=%async_computation.1 | async-start | bytes 4194304 | tf_op jit(solution)/shard_map/move/all_to_all | solution.py:32
  59.0 10.9 %collective-permute-start.4 = (bf16[448,256]{1,0:T(8,128)(2,1)S(1)}, bf16[448,256]{1,0:T(8,128)(2,1)S(1)}, u32[]{:S(2)}, u32[]{:S(2)}) collective-permute-start(bf16[448,256]{1,0:T(8,128)(2,1)S(1)} %get-tuple-element.102), channel_id=1, source_target_pairs={{0,64},{32,96},{64,0},{96,32},{1,65},{33,97},{65,1},{97,33},{2,66}... | collective-permute-start | bytes 688136 | tf_op jit(solution)/shard_map/move/ppermute | solution.py:17
  62.3 11.6 %collective-permute-start.5 = (bf16[448,256]{1,0:T(8,128)(2,1)S(1)}, bf16[448,256]{1,0:T(8,128)(2,1)S(1)}, u32[]{:S(2)}, u32[]{:S(2)}) collective-permute-start(bf16[448,256]{1,0:T(8,128)(2,1)S(1)} %get-tuple-element.101), channel_id=1, source_target_pairs={{0,96},{32,64},{64,32},{96,0},{1,97},{33,65},{65,33},{97,1},{2,98}... | collective-permute-start | bytes 688136 | tf_op jit(solution)/shard_map/move/ppermute | solution.py:17
  63.3 14.0 %collective-permute-start.3 = (bf16[448,256]{1,0:T(8,128)(2,1)S(1)}, bf16[448,256]{1,0:T(8,128)(2,1)S(1)}, u32[]{:S(2)}, u32[]{:S(2)}) collective-permute-start(bf16[448,256]{1,0:T(8,128)(2,1)S(1)} %get-tuple-element.103), channel_id=1, source_target_pairs={{0,32},{32,0},{64,96},{96,64},{1,33},{33,1},{65,97},{97,65},{2,34}... | collective-permute-start | bytes 688136 | tf_op jit(solution)/shard_map/move/ppermute | solution.py:17
  77.4 46.7 %copy-start.3 = (bf16[4,448,256]{2,1,0:T(8,128)(2,1)}, bf16[4,448,256]{2,1,0:T(8,128)(2,1)S(1)}, u32[]{:S(2)}) copy-start(bf16[4,448,256]{2,1,0:T(8,128)(2,1)S(1)} %pad_maximum_fusion.refs_0_) | copy-start | bytes 2752516
  83.2 1.4 copy-start.1
  84.6 33.2 %all-to-all-start.2 = ((bf16[4,4,128,512]{3,2,1,0:T(8,128)(2,1)}), bf16[4,4,128,512]{3,2,1,0:T(8,128)(2,1)S(1)}, u32[]{:S(2)}, u32[]{:S(2)}) async-start(bf16[4,4,128,512]{3,2,1,0:T(8,128)(2,1)} %stack.53), calls=%async_computation.2 | async-start | bytes 4194304 | tf_op jit(solution)/shard_map/move/all_to_all | solution.py:32
  91.2 15.1 %collective-permute-start.6 = (bf16[4,128,512]{2,1,0:T(8,128)(2,1)}, bf16[4,128,512]{2,1,0:T(8,128)(2,1)S(1)}, u32[]{:S(2)}, u32[]{:S(2)}) collective-permute-start(bf16[4,128,512]{2,1,0:T(8,128)(2,1)} %get-tuple-element.94), channel_id=1, source_target_pairs={{0,2},{2,0},{4,6},{6,4},{1,3},{3,1},{5,7},{7,5},{8,10},{10,8},{12,... | collective-permute-start | bytes 1572872 | tf_op jit(solution)/shard_map/move/ppermute | solution.py:17
  91.2 22.2 %collective-permute-start.7 = (bf16[4,128,512]{2,1,0:T(8,128)(2,1)}, bf16[4,128,512]{2,1,0:T(8,128)(2,1)}, u32[]{:S(2)}, u32[]{:S(2)}) collective-permute-start(bf16[4,128,512]{2,1,0:T(8,128)(2,1)} %get-tuple-element.93), channel_id=1, source_target_pairs={{0,4},{2,6},{4,0},{6,2},{1,5},{3,7},{5,1},{7,3},{8,12},{10,14},{12... | collective-permute-start | bytes 1572872 | tf_op jit(solution)/shard_map/move/ppermute | solution.py:17
  93.1 22.9 %collective-permute-start.8 = (bf16[4,128,512]{2,1,0:T(8,128)(2,1)}, bf16[4,128,512]{2,1,0:T(8,128)(2,1)}, u32[]{:S(2)}, u32[]{:S(2)}) collective-permute-start(bf16[4,128,512]{2,1,0:T(8,128)(2,1)} %get-tuple-element.92), channel_id=1, source_target_pairs={{0,6},{2,4},{4,2},{6,0},{1,7},{3,5},{5,3},{7,1},{8,14},{10,12},{12... | collective-permute-start | bytes 1572872 | tf_op jit(solution)/shard_map/move/ppermute | solution.py:17
  106.3 12.7 %copy-start.7 = (bf16[4,128,512]{2,1,0:T(8,128)(2,1)}, bf16[4,128,512]{2,1,0:T(8,128)(2,1)S(1)}, u32[]{:S(2)}) copy-start(bf16[4,128,512]{2,1,0:T(8,128)(2,1)S(1)} %collective-permute-done.6.refs_1_) | copy-start | bytes 1572868
  117.8 3.4 %slice-start = ((s32[129]{0:T(256)}), s32[128]{0:T(128)S(1)}, s32[]{:S(2)}) async-start(s32[129]{0:T(256)} %param.7), calls=%async_computation.4 | async-start | bytes 1024 | tf_op jit(solution)/shard_map/weight/slice | solution.py:188
  117.8 1.7 copy-start
  119.5 6.8 %collective-permute-start.9 = (bf16[16,128,512]{2,1,0:T(8,128)(2,1)}, bf16[16,128,512]{2,1,0:T(8,128)(2,1)}, u32[]{:S(2)}, u32[]{:S(2)}) collective-permute-start(bf16[16,128,512]{2,1,0:T(8,128)(2,1)} %constant_dynamic-update-slice_fusion), channel_id=1, source_target_pairs={{0,1},{1,0},{2,3},{3,2},{4,5},{5,4},{6,7},{7,6},{8,9},{9,8},{10,11... | collective-permute-start | bytes 6291464 | tf_op jit(solution)/shard_map/weight/ppermute | solution.py:181
  119.5 23.1 %collective-permute-start.13 = (bf16[4,448,256]{2,1,0:T(8,128)(2,1)S(1)}, bf16[4,448,256]{2,1,0:T(8,128)(2,1)S(1)}, u32[]{:S(2)}, u32[]{:S(2)}) collective-permute-start(bf16[4,448,256]{2,1,0:T(8,128)(2,1)S(1)} %pad_maximum_fusion.refs_0_), channel_id=1, source_target_pairs={{0,8},{8,0},{16,24},{24,16},{1,9},{9,1},{17,25},{25,17},{2,10},{10... | collective-permute-start | bytes 2752520 | tf_op jit(solution)/shard_map/ppermute | solution.py:17
  121.3 43.1 %collective-permute-start.14 = (bf16[4,448,256]{2,1,0:T(8,128)(2,1)S(1)}, bf16[4,448,256]{2,1,0:T(8,128)(2,1)}, u32[]{:S(2)}, u32[]{:S(2)}) collective-permute-start(bf16[4,448,256]{2,1,0:T(8,128)(2,1)S(1)} %pad_maximum_fusion.refs_0_), channel_id=1, source_target_pairs={{0,16},{8,24},{16,0},{24,8},{1,17},{9,25},{17,1},{25,9},{2,18},{10... | collective-permute-start | bytes 2752520 | tf_op jit(solution)/shard_map/ppermute | solution.py:17
  124.1 43.2 %collective-permute-start.15 = (bf16[4,448,256]{2,1,0:T(8,128)(2,1)S(1)}, bf16[4,448,256]{2,1,0:T(8,128)(2,1)}, u32[]{:S(2)}, u32[]{:S(2)}) collective-permute-start(bf16[4,448,256]{2,1,0:T(8,128)(2,1)S(1)} %pad_maximum_fusion.refs_0_), channel_id=1, source_target_pairs={{0,24},{8,16},{16,8},{24,0},{1,25},{9,17},{17,9},{25,1},{2,26},{10... | collective-permute-start | bytes 2752520 | tf_op jit(solution)/shard_map/ppermute | solution.py:17
  132.7 34.5 %collective-permute-start.10 = (bf16[448,512]{1,0:T(8,128)(2,1)}, bf16[448,512]{1,0:T(8,128)(2,1)S(1)}, u32[]{:S(2)}, u32[]{:S(2)}) collective-permute-start(bf16[448,512]{1,0:T(8,128)(2,1)} %get-tuple-element.66), channel_id=1, source_target_pairs={{0,2},{2,0},{4,6},{6,4},{1,3},{3,1},{5,7},{7,5},{8,10},{10,8},{12,... | collective-permute-start | bytes 1376264 | tf_op jit(solution)/shard_map/weight/ppermute | solution.py:17
  132.7 34.5 %collective-permute-start.11 = (bf16[448,512]{1,0:T(8,128)(2,1)}, bf16[448,512]{1,0:T(8,128)(2,1)S(1)}, u32[]{:S(2)}, u32[]{:S(2)}) collective-permute-start(bf16[448,512]{1,0:T(8,128)(2,1)} %get-tuple-element.67), channel_id=1, source_target_pairs={{0,4},{2,6},{4,0},{6,2},{1,5},{3,7},{5,1},{7,3},{8,12},{10,14},{12... | collective-permute-start | bytes 1376264 | tf_op jit(solution)/shard_map/weight/ppermute | solution.py:17
  142.6 34.9 %copy-start.8 = (bf16[4,448,256]{2,1,0:T(8,128)(2,1)}, bf16[4,448,256]{2,1,0:T(8,128)(2,1)S(1)}, u32[]{:S(2)}) copy-start(bf16[4,448,256]{2,1,0:T(8,128)(2,1)S(1)} %collective-permute-done.13.refs_1_) | copy-start | bytes 2752516
  142.6 24.7 %collective-permute-start.12 = (bf16[448,512]{1,0:T(8,128)(2,1)}, bf16[448,512]{1,0:T(8,128)(2,1)S(1)}, u32[]{:S(2)}, u32[]{:S(2)}) collective-permute-start(bf16[448,512]{1,0:T(8,128)(2,1)} %get-tuple-element.68), channel_id=1, source_target_pairs={{0,6},{2,4},{4,2},{6,0},{1,7},{3,5},{5,3},{7,1},{8,14},{10,12},{12... | collective-permute-start | bytes 1376264 | tf_op jit(solution)/shard_map/weight/ppermute | solution.py:17
  167.3 0.8 copy-start.4
  167.3 1.0 copy-start.5
  167.3 1.1 copy-start.6
  177.5 34.1 %collective-permute-start.16 = (bf16[4,448,256]{2,1,0:T(8,128)(2,1)}, bf16[4,448,256]{2,1,0:T(8,128)(2,1)S(1)}, u32[]{:S(2)}, u32[]{:S(2)}) collective-permute-start(bf16[4,448,256]{2,1,0:T(8,128)(2,1)} %get-tuple-element.75), channel_id=1, source_target_pairs={{0,16},{8,24},{16,0},{24,8},{1,17},{9,25},{17,1},{25,9},{2,18},{10... | collective-permute-start | bytes 2752520 | tf_op jit(solution)/shard_map/projected/ppermute | solution.py:17
  178.0 40.6 %collective-permute-start.17 = (bf16[4,448,256]{2,1,0:T(8,128)(2,1)}, bf16[4,448,256]{2,1,0:T(8,128)(2,1)S(1)}, u32[]{:S(2)}, u32[]{:S(2)}) collective-permute-start(bf16[4,448,256]{2,1,0:T(8,128)(2,1)} %get-tuple-element.76), channel_id=1, source_target_pairs={{0,8},{8,0},{16,24},{24,16},{1,9},{9,1},{17,25},{25,17},{2,10},{10... | collective-permute-start | bytes 2752520 | tf_op jit(solution)/shard_map/projected/ppermute | solution.py:17
  188.2 32.1 %collective-permute-start.18 = (bf16[4,448,256]{2,1,0:T(8,128)(2,1)}, bf16[4,448,256]{2,1,0:T(8,128)(2,1)S(1)}, u32[]{:S(2)}, u32[]{:S(2)}) collective-permute-start(bf16[4,448,256]{2,1,0:T(8,128)(2,1)} %get-tuple-element.77), channel_id=1, source_target_pairs={{0,24},{8,16},{16,8},{24,0},{1,25},{9,17},{17,9},{25,1},{2,26},{10... | collective-permute-start | bytes 2752520 | tf_op jit(solution)/shard_map/projected/ppermute | solution.py:17
  191.4 28.8 %copy-start.9 = (bf16[4,448,256]{2,1,0:T(8,128)(2,1)S(1)}, bf16[4,448,256]{2,1,0:T(8,128)(2,1)}, u32[]{:S(2)}) copy-start(bf16[4,448,256]{2,1,0:T(8,128)(2,1)} %get-tuple-element.74) | copy-start | bytes 2752516
  207.1 17.2 %collective-permute-start.23 = (bf16[448,512]{1,0:T(8,128)(2,1)}, bf16[448,512]{1,0:T(8,128)(2,1)S(1)}, u32[]{:S(2)}, u32[]{:S(2)}) collective-permute-start(bf16[448,512]{1,0:T(8,128)(2,1)} %get-tuple-element.83), channel_id=1, source_target_pairs={{0,32},{32,0},{64,96},{96,64},{1,33},{33,1},{65,97},{97,65},{2,34}... | collective-permute-start | bytes 1376264 | tf_op jit(solution)/shard_map/grad/ppermute | solution.py:17
  208.7 24.2 %collective-permute-start.24 = (bf16[448,512]{1,0:T(8,128)(2,1)}, bf16[448,512]{1,0:T(8,128)(2,1)S(1)}, u32[]{:S(2)}, u32[]{:S(2)}) collective-permute-start(bf16[448,512]{1,0:T(8,128)(2,1)} %get-tuple-element.84), channel_id=1, source_target_pairs={{0,64},{32,96},{64,0},{96,32},{1,65},{33,97},{65,1},{97,33},{2,66}... | collective-permute-start | bytes 1376264 | tf_op jit(solution)/shard_map/grad/ppermute | solution.py:17
  211.6 28.7 %collective-permute-start.25 = (bf16[448,512]{1,0:T(8,128)(2,1)}, bf16[448,512]{1,0:T(8,128)(2,1)S(1)}, u32[]{:S(2)}, u32[]{:S(2)}) collective-permute-start(bf16[448,512]{1,0:T(8,128)(2,1)} %get-tuple-element.85), channel_id=1, source_target_pairs={{0,96},{32,64},{64,32},{96,0},{1,97},{33,65},{65,33},{97,1},{2,98}... | collective-permute-start | bytes 1376264 | tf_op jit(solution)/shard_map/grad/ppermute | solution.py:17
  220.8 25.1 %collective-permute-start.19 = (bf16[448,256]{1,0:T(8,128)(2,1)S(1)}, bf16[448,256]{1,0:T(8,128)(2,1)S(1)}, u32[]{:S(2)}, u32[]{:S(2)}) collective-permute-start(bf16[448,256]{1,0:T(8,128)(2,1)S(1)} %get-tuple-element.99), channel_id=1, source_target_pairs={{0,0},{2,32},{4,64},{6,96},{32,2},{34,34},{36,66},{38,98},{64,4},{... | collective-permute-start | bytes 688136 | tf_op jit(solution)/shard_map/ppermute | solution.py:362
  221.5 24.5 %collective-permute-start.20 = (bf16[448,256]{1,0:T(8,128)(2,1)S(1)}, bf16[448,256]{1,0:T(8,128)(2,1)S(1)}, u32[]{:S(2)}, u32[]{:S(2)}) collective-permute-start(bf16[448,256]{1,0:T(8,128)(2,1)S(1)} %get-tuple-element.98), channel_id=1, source_target_pairs={{0,32},{2,0},{4,96},{6,64},{32,34},{34,2},{36,98},{38,66},{64,36},... | collective-permute-start | bytes 688136 | tf_op jit(solution)/shard_map/ppermute | solution.py:362
  224.4 16.0 %copy-start.11 = (bf16[448,512]{1,0:T(8,128)(2,1)}, bf16[448,512]{1,0:T(8,128)(2,1)S(1)}, u32[]{:S(2)}) copy-start(bf16[448,512]{1,0:T(8,128)(2,1)S(1)} %collective-permute-done.23.refs_1_) | copy-start | bytes 1376260
  224.4 21.6 %collective-permute-start.21 = (bf16[448,256]{1,0:T(8,128)(2,1)S(1)}, bf16[448,256]{1,0:T(8,128)(2,1)S(1)}, u32[]{:S(2)}, u32[]{:S(2)}) collective-permute-start(bf16[448,256]{1,0:T(8,128)(2,1)S(1)} %get-tuple-element.97), channel_id=1, source_target_pairs={{0,64},{2,96},{4,0},{6,32},{32,66},{34,98},{36,2},{38,34},{64,68},... | collective-permute-start | bytes 688136 | tf_op jit(solution)/shard_map/ppermute | solution.py:362
  232.9 7.5 %copy-start.12 = (bf16[448,512]{1,0:T(8,128)(2,1)}, bf16[448,512]{1,0:T(8,128)(2,1)S(1)}, u32[]{:S(2)}) copy-start(bf16[448,512]{1,0:T(8,128)(2,1)S(1)} %collective-permute-done.24.refs_2_) | copy-start | bytes 1376260
  232.9 13.1 %collective-permute-start.22 = (bf16[448,256]{1,0:T(8,128)(2,1)S(1)}, bf16[448,256]{1,0:T(8,128)(2,1)S(1)}, u32[]{:S(2)}, u32[]{:S(2)}) collective-permute-start(bf16[448,256]{1,0:T(8,128)(2,1)S(1)} %get-tuple-element.96), channel_id=1, source_target_pairs={{0,96},{2,64},{4,32},{6,0},{32,98},{34,66},{36,34},{38,2},{64,100}... | collective-permute-start | bytes 688136 | tf_op jit(solution)/shard_map/ppermute | solution.py:362
  240.4 0.8 copy-start.13
  245.9 0.7 copy-start.14
  246.0 0.8 copy-start.15
  246.0 0.8 copy-start.16
  246.8 0.7 copy-start.17
Sparse Core Ops, SparseCore 0:
  54.5 85.7 all-gather.2

commit v4 on v3

--- a/solution.py
+++ b/solution.py
@@ -201,7 +201,7 @@
         jnp.where(slot == 0, 2 * c + low, (2 * c + low) * RING + s),
     )
     sources = firsts + [second.reshape(owners, block, part), other]
-    return gather(kind, index, half, sources, hidden)
+    return list(gather(kind, index, half, sources, hidden))
 
 
 def project_kernel(place_ref, tokens_ref, *refs):
@@ -341,11 +341,13 @@
         every, firsts, second, cot = move(old_codes, old_scales, tokens, cut)
 
     with jax.named_scope("weight"):
-        weights = exchange(weight_rows(firsts, second, old_offsets, local_hidden), "z")
-
-    cots = exchange([cot] * RING, "x")
-    sides = together(*weights, *cots)
-    weights, cots = sides[:RING], sides[RING:]
+        rows = weight_rows(firsts, second, old_offsets, local_hidden)
+        rows[0], last = together(rows[0], cot)
+        weights = exchange(rows, "z")
+
+    cots = [cot, swap(cot, "x", 1), swap(cot, "x", 2), swap(last, "x", 3)]
+    sides = together(*weights, *cots[1:3])
+    weights, cots[1:3] = sides[:RING], sides[RING:]
 
     with jax.named_scope("projected"):
         far, right = project(every, weights, [x ^ 2, x ^ 1], z)

time: 258 us -> 271 us (1.050)
  waiting for transfers between devices: 105 us -> 118 us
    ppermute x21, waiting for transfers between devices: 98.8 us -> 112 us  [swap(): return lax.ppermute(array, axis, [(i, i ^ s) for i in range(RING)])]
  transfers between devices with their start and end apart: 30 -> 30, of which waited for: 17 -> 16; matrix products, arithmetic and copies ran while one was open for 6% -> 6% of each run, Pallas kernels for 16% -> 18%
where the time goes in v4:
time: 271 us; the launch traced here: 270 us
  waiting for transfers between devices  118 us (44%)
  Pallas kernels  60.6 us (22%)
  starting transfers between devices  53.9 us (20%)
  local copies, waits for them, and re-layouts  19 us (7%)
  between operations  14.2 us (5%)
  other arithmetic  4.26 us (2%)
    ppermute x21, waiting for transfers between devices, swap(): return lax.ppermute(array, axis, [(i, i ^ s) for i in range(RING)])  112 us
    ppermute x21, starting transfers between devices, swap(): return lax.ppermute(array, axis, [(i, i ^ s) for i in range(RING)])  35.3 us
    pallas_call x2, Pallas kernels, project(): pl.pallas_call(project_kernel, grid_spec=pltpu.PrefetchScalarGridSpec(num...  18.3 us
    pallas_call x1, Pallas kernels, gradient(): pl.pallas_call(grad_kernel, grid_spec=pltpu.PrefetchScalarGridSpec(num_sc...  15.5 us
    unnamed x42, local copies, waits for them, and re-layouts  13.2 us
    all_to_all x3, starting transfers between devices, all_to_all(): return lax.all_to_all(array, axis, 0, 0, tiled=True)  12.5 us
    pallas_call x2, Pallas kernels, assemble(): pl.pallas_call(assemble_kernel, grid_spec=pltpu.PrefetchScalarGridSpec(nu...  7.21 us
    pallas_call x1, Pallas kernels, gather(): pl.pallas_call(gather_kernel, grid_spec=pltpu.PrefetchScalarGridSpec(num_...  6.5 us
  transfers between devices with their start and end apart: 30, of which 16 were waited for; matrix products, arithmetic and copies ran while one was open for 6% of the time, Pallas kernels for 18%

profile of v4, /device:TPU:0, one launch (start us, length us, event | category | flops | bytes accessed | tf_op | source)
XLA Modules:
  0.0 270.1 jit_solution(4819015904383693054)
XLA Ops:
  7.2 0.7 convert_element_type.21
  7.9 0.7 copy.12
  8.6 5.2 %dequantize.1 = (bf16[4,4,128,512]{3,2,1,0:T(8,128)(2,1)}, bf16[4,128,512]{2,1,0:T(8,128)(2,1)}, bf16[4,128,512]{2,1,0:T(8,128)(2,1)}, bf16[4,128,512]{2,1,0:T(8,128)(2,1)}, bf16[4,128,512]{2,1,0:T(8,128)(2,1)}) custom-call(s32[1]{0:T(128)} %bitcast.1.place_ref, bf16[256,8192]{1,0:T(8,128)(2,1)} %codes_ref.1, f32[2,8192]{1,0:T(2,128)} %bitcast.51), custom_call_target="tpu_custom_call" | custom-call | tf_op jit(solution)/shard_map/move/dequantize/pallas_call | solution.py:85
  13.8 3.8 %cut_tokens.1 = bf16[4,128,2048]{2,1,0:T(8,128)(2,1)} custom-call(s32[1]{0:T(128)} %bitcast.4.place_ref, bf16[256,8192]{1,0:T(8,128)(2,1)} %tokens_ref), custom_call_target="tpu_custom_call" | custom-call | tf_op jit(solution)/shard_map/move/cut_tokens/pallas_call | solution.py:45
  17.6 4.4 %all-to-all-start = ((bf16[4,128,2048]{2,1,0:T(8,128)(2,1)}), bf16[4,128,2048]{2,1,0:T(8,128)(2,1)S(1)}, u32[]{:S(2)}, u32[]{:S(2)}) async-start(bf16[4,128,2048]{2,1,0:T(8,128)(2,1)} %cut_tokens.1), calls=%async_computation | async-start | bytes 4194304 | tf_op jit(solution)/shard_map/move/all_to_all | solution.py:32
  22.0 1.9 collective-permute-start
  23.9 3.6 %collective-permute-start.1 = (bf16[4,128,512]{2,1,0:T(8,128)(2,1)}, bf16[4,128,512]{2,1,0:T(8,128)(2,1)}, u32[]{:S(2)}, u32[]{:S(2)}) collective-permute-start(bf16[4,128,512]{2,1,0:T(8,128)(2,1)} %get-tuple-element.52), channel_id=1, source_target_pairs={{0,4},{2,6},{4,0},{6,2},{1,5},{3,7},{5,1},{7,3},{8,12},{10,14},{12... | collective-permute-start | bytes 1572872 | tf_op jit(solution)/shard_map/move/ppermute | solution.py:17
  27.5 1.5 copy.9
  29.0 8.0 %collective-permute-done.refs_1_ = bf16[4,128,512]{2,1,0:T(8,128)(2,1)S(1)} collective-permute-done((bf16[4,128,512]{2,1,0:T(8,128)(2,1)}, bf16[4,128,512]{2,1,0:T(8,128)(2,1)S(1)}, u32[]{:S(2)}, u32[]{:S(2)}) %collective-permute-start) | collective-permute-done | bytes 524320 | tf_op jit(solution)/shard_map/move/ppermute | solution.py:17
  37.0 13.5 %collective-permute-done.1.refs_2_ = bf16[4,128,512]{2,1,0:T(8,128)(2,1)} collective-permute-done((bf16[4,128,512]{2,1,0:T(8,128)(2,1)}, bf16[4,128,512]{2,1,0:T(8,128)(2,1)}, u32[]{:S(2)}, u32[]{:S(2)}) %collective-permute-start.1) | collective-permute-done | bytes 524320 | tf_op jit(solution)/shard_map/move/ppermute | solution.py:17
  50.5 2.6 collective-permute-done.2.refs_3_
  53.1 1.3 copy-done.2
  54.4 4.5 %all-to-all-start.1 = ((bf16[4,4,128,512]{3,2,1,0:T(8,128)(2,1)}), bf16[4,4,128,512]{3,2,1,0:T(8,128)(2,1)S(1)}, u32[]{:S(2)}, u32[]{:S(2)}) async-start(bf16[4,4,128,512]{3,2,1,0:T(8,128)(2,1)} %get-tuple-element.55), calls=%async_computation.1 | async-start | bytes 4194304 | tf_op jit(solution)/shard_map/move/all_to_all | solution.py:32
  59.0 3.3 %collective-permute-start.4 = (bf16[448,256]{1,0:T(8,128)(2,1)S(1)}, bf16[448,256]{1,0:T(8,128)(2,1)S(1)}, u32[]{:S(2)}, u32[]{:S(2)}) collective-permute-start(bf16[448,256]{1,0:T(8,128)(2,1)S(1)} %get-tuple-element.102), channel_id=1, source_target_pairs={{0,64},{32,96},{64,0},{96,32},{1,65},{33,97},{65,1},{97,33},{2,66}... | collective-permute-start | bytes 688136 | tf_op jit(solution)/shard_map/move/ppermute | solution.py:17
  62.3 1.1 collective-permute-start.5
  63.4 4.1 %stack.53 = bf16[4,4,128,512]{3,2,1,0:T(8,128)(2,1)} custom-call(bf16[4,128,512]{2,1,0:T(8,128)(2,1)} %get-tuple-element.56.refs_0_, bf16[4,128,512]{2,1,0:T(8,128)(2,1)} %copy-done.10, bf16[4,128,512]{2,1,0:T(8,128)(2,1)} %collective-permute-done.1.refs_2_, bf16[4,128,512]{2,1,0:T(8,128)(2,1)} %collective-permute-done.2.refs_3_), custom_call_target="tpu_custom_call" | custom-call | tf_op jit(solution)/shard_map/move/stack/pallas_call | solution.py:145
  67.5 2.5 collective-permute-done.4
  69.9 3.9 %collective-permute-done.5 = bf16[448,256]{1,0:T(8,128)(2,1)S(1)} collective-permute-done((bf16[448,256]{1,0:T(8,128)(2,1)S(1)}, bf16[448,256]{1,0:T(8,128)(2,1)S(1)}, u32[]{:S(2)}, u32[]{:S(2)}) %collective-permute-start.5) | collective-permute-done | bytes 229408 | tf_op jit(solution)/shard_map/move/ppermute | solution.py:17
  73.8 3.5 %collective-permute-done.3 = bf16[448,256]{1,0:T(8,128)(2,1)S(1)} collective-permute-done((bf16[448,256]{1,0:T(8,128)(2,1)S(1)}, bf16[448,256]{1,0:T(8,128)(2,1)S(1)}, u32[]{:S(2)}, u32[]{:S(2)}) %collective-permute-start.3) | collective-permute-done | bytes 229408 | tf_op jit(solution)/shard_map/move/ppermute | solution.py:17
  77.4 5.8 %all-to-all-done.1 = bf16[4,4,128,512]{3,2,1,0:T(8,128)(2,1)S(1)} async-done(((bf16[4,4,128,512]{3,2,1,0:T(8,128)(2,1)}), bf16[4,4,128,512]{3,2,1,0:T(8,128)(2,1)S(1)}, u32[]{:S(2)}, u32[]{:S(2)}) %all-to-all-start.1) | async-done | bytes 2097184 | tf_op jit(solution)/shard_map/move/all_to_all | solution.py:32
  83.2 1.4 copy-done.1
  84.6 3.6 %all-to-all-start.2 = ((bf16[4,4,128,512]{3,2,1,0:T(8,128)(2,1)}), bf16[4,4,128,512]{3,2,1,0:T(8,128)(2,1)S(1)}, u32[]{:S(2)}, u32[]{:S(2)}) async-start(bf16[4,4,128,512]{3,2,1,0:T(8,128)(2,1)} %stack.53), calls=%async_computation.2 | async-start | bytes 4194304 | tf_op jit(solution)/shard_map/move/all_to_all | solution.py:32
  88.2 3.1 %dynamic-slice_bitcast_fusion = (bf16[4,128,512]{2,1,0:T(8,128)(2,1)}, bf16[4,128,512]{2,1,0:T(8,128)(2,1)}, bf16[4,128,512]{2,1,0:T(8,128)(2,1)}, bf16[4,128,512]{2,1,0:T(8,128)(2,1)}) fusion(bf16[4,4,128,512]{3,2,1,0:T(8,128)(2,1)} %copy-done.1, s32[]{:T(128)S(6)} %select_n.110, s32[]{:T(128)S(6)} %select_n.109, s32[]{:T(128)S(6)} %select_n.108, ...), kind=kLoop, calls=%fused_computation.2 | loop fusion | bytes 4194320 | tf_op jit(solution)/shard_map/move/jit(dynamic_index_in_dim)/squeeze | solution.py:28
  91.3 1.9 collective-permute-start.7
  93.2 2.8 %collective-permute-start.8 = (bf16[4,128,512]{2,1,0:T(8,128)(2,1)}, bf16[4,128,512]{2,1,0:T(8,128)(2,1)}, u32[]{:S(2)}, u32[]{:S(2)}) collective-permute-start(bf16[4,128,512]{2,1,0:T(8,128)(2,1)} %get-tuple-element.92), channel_id=1, source_target_pairs={{0,6},{2,4},{4,2},{6,0},{1,7},{3,5},{5,3},{7,1},{8,14},{10,12},{12... | collective-permute-start | bytes 1572872 | tf_op jit(solution)/shard_map/move/ppermute | solution.py:17
  96.0 1.7 bitcast_dynamic-update-slice_fusion
  97.7 8.7 %collective-permute-done.6.refs_1_ = bf16[4,128,512]{2,1,0:T(8,128)(2,1)S(1)} collective-permute-done((bf16[4,128,512]{2,1,0:T(8,128)(2,1)}, bf16[4,128,512]{2,1,0:T(8,128)(2,1)S(1)}, u32[]{:S(2)}, u32[]{:S(2)}) %collective-permute-start.6) | collective-permute-done | bytes 524320 | tf_op jit(solution)/shard_map/move/ppermute | solution.py:17
  106.4 0.8 dynamic-slice_dynamic-update-slice_fusion.2
  107.2 6.4 %collective-permute-done.7.refs_2_ = bf16[4,128,512]{2,1,0:T(8,128)(2,1)} collective-permute-done((bf16[4,128,512]{2,1,0:T(8,128)(2,1)}, bf16[4,128,512]{2,1,0:T(8,128)(2,1)}, u32[]{:S(2)}, u32[]{:S(2)}) %collective-permute-start.7) | collective-permute-done | bytes 524320 | tf_op jit(solution)/shard_map/move/ppermute | solution.py:17
  113.6 1.7 dynamic-slice_dynamic-update-slice_fusion.1
  115.2 0.9 collective-permute-done.8.refs_3_
  116.1 1.7 dynamic-slice_dynamic-update-slice_fusion
  117.9 1.1 constant_dynamic-update-slice_fusion
  119.8 1.7 collective-permute-start.13
  121.5 2.7 collective-permute-start.14
  124.1 0.6 and_select_fusion
  125.8 6.5 %gather_blocks.1 = (bf16[448,512]{1,0:T(8,128)(2,1)}, bf16[448,512]{1,0:T(8,128)(2,1)}, bf16[448,512]{1,0:T(8,128)(2,1)}, bf16[448,512]{1,0:T(8,128)(2,1)}) custom-call(s32[28]{0:T(128)} %compare_select_fusion.7.kind_ref, s32[28]{0:T(128)} %get-tuple-element.90.index_ref, s32[28]{0:T(128)} %get-tuple-element.88.half_ref, ...), custom_call_target="tpu_custom_call" | custom-call | tf_op jit(solution)/shard_map/weight/gather_blocks/pallas_call | solution.py:120
  132.3 3.8 %collective-permute-start.11 = (bf16[448,512]{1,0:T(8,128)(2,1)}, bf16[448,512]{1,0:T(8,128)(2,1)S(1)}, u32[]{:S(2)}, u32[]{:S(2)}) collective-permute-start(bf16[448,512]{1,0:T(8,128)(2,1)} %get-tuple-element.69), channel_id=1, source_target_pairs={{0,4},{2,6},{4,0},{6,2},{1,5},{3,7},{5,1},{7,3},{8,12},{10,14},{12... | collective-permute-start | bytes 1376264 | tf_op jit(solution)/shard_map/weight/ppermute | solution.py:17
  136.1 0.9 collective-permute-start.12
  137.0 0.7 pad_add_fusion
  137.6 5.4 %collective-permute-done.13.refs_1_ = bf16[4,448,256]{2,1,0:T(8,128)(2,1)S(1)} collective-permute-done((bf16[4,448,256]{2,1,0:T(8,128)(2,1)S(1)}, bf16[4,448,256]{2,1,0:T(8,128)(2,1)S(1)}, u32[]{:S(2)}, u32[]{:S(2)}) %collective-permute-start.13) | collective-permute-done | bytes 917536 | tf_op jit(solution)/shard_map/ppermute | solution.py:17
  143.0 2.8 %collective-permute-start.22 = (bf16[4,448,256]{2,1,0:T(8,128)(2,1)S(1)}, bf16[4,448,256]{2,1,0:T(8,128)(2,1)}, u32[]{:S(2)}, u32[]{:S(2)}) collective-permute-start(bf16[4,448,256]{2,1,0:T(8,128)(2,1)S(1)} %pad_maximum_fusion.refs_0_), channel_id=1, source_target_pairs={{0,24},{8,16},{16,8},{24,0},{1,25},{9,17},{17,9},{25,1},{2,26},{10... | collective-permute-start | bytes 2752520 | tf_op jit(solution)/shard_map/ppermute | solution.py:17
  145.8 18.9 %collective-permute-done.14.refs_2_ = bf16[4,448,256]{2,1,0:T(8,128)(2,1)} collective-permute-done((bf16[4,448,256]{2,1,0:T(8,128)(2,1)S(1)}, bf16[4,448,256]{2,1,0:T(8,128)(2,1)}, u32[]{:S(2)}, u32[]{:S(2)}) %collective-permute-start.14) | collective-permute-done | bytes 917536 | tf_op jit(solution)/shard_map/ppermute | solution.py:17
  164.8 0.7 copy-done.4
  165.9 9.1 %project.3 = (bf16[4,448,256]{2,1,0:T(8,128)(2,1)}, bf16[4,448,256]{2,1,0:T(8,128)(2,1)}) custom-call(s32[3]{0:T(128)} %get-tuple-element.105.place_ref, bf16[8,4,128,2048]{3,2,1,0:T(8,128)(2,1)} %bitcast.44, bf16[448,512]{1,0:T(8,128)(2,1)} %get-tuple-element.71.refs_0_, bf16[448,512]{1,0:T(8,128)(2,1)} %copy-done.4, bf16[448,512]{1,0:T(8,128)(2,1)} %copy-done.5, ...), custom_call_target="tpu_custom_call" | custom-call | tf_op jit(solution)/shard_map/projected/project/pallas_call | solution.py:234
  175.0 0.9 collective-permute-start.15
  176.3 9.1 %project.2 = (bf16[4,448,256]{2,1,0:T(8,128)(2,1)}, bf16[4,448,256]{2,1,0:T(8,128)(2,1)}) custom-call(s32[3]{0:T(128)} %get-tuple-element.104.place_ref, bf16[8,4,128,2048]{3,2,1,0:T(8,128)(2,1)} %bitcast.45, bf16[448,512]{1,0:T(8,128)(2,1)} %get-tuple-element.71.refs_0_, bf16[448,512]{1,0:T(8,128)(2,1)} %copy-done.4, bf16[448,512]{1,0:T(8,128)(2,1)} %copy-done.5, ...), custom_call_target="tpu_custom_call" | custom-call | tf_op jit(solution)/shard_map/projected/project/pallas_call | solution.py:234
  185.4 2.8 %collective-permute-start.17 = (bf16[4,448,256]{2,1,0:T(8,128)(2,1)}, bf16[4,448,256]{2,1,0:T(8,128)(2,1)S(1)}, u32[]{:S(2)}, u32[]{:S(2)}) collective-permute-start(bf16[4,448,256]{2,1,0:T(8,128)(2,1)} %get-tuple-element.78), channel_id=1, source_target_pairs={{0,24},{8,16},{16,8},{24,0},{1,25},{9,17},{17,9},{25,1},{2,26},{10... | collective-permute-start | bytes 2752520 | tf_op jit(solution)/shard_map/projected/ppermute | solution.py:17
  188.3 0.6 pad_add_fusion.2.place_ref
  188.8 15.3 %collective-permute-done.22.refs_3_ = bf16[4,448,256]{2,1,0:T(8,128)(2,1)} collective-permute-done((bf16[4,448,256]{2,1,0:T(8,128)(2,1)S(1)}, bf16[4,448,256]{2,1,0:T(8,128)(2,1)}, u32[]{:S(2)}, u32[]{:S(2)}) %collective-permute-start.22) | collective-permute-done | bytes 917536 | tf_op jit(solution)/shard_map/ppermute | solution.py:17
  204.1 15.5 %gradient.1 = (bf16[448,512]{1,0:T(8,128)(2,1)}, bf16[448,512]{1,0:T(8,128)(2,1)}, bf16[448,512]{1,0:T(8,128)(2,1)}, bf16[448,512]{1,0:T(8,128)(2,1)}) custom-call(s32[2]{0:T(128)} %pad_add_fusion.2.place_ref, bf16[8,4,128,2048]{3,2,1,0:T(8,128)(2,1)} %bitcast.46, bf16[4,448,256]{2,1,0:T(8,128)(2,1)} %copy-done.3, bf16[4,448,256]{2,1,0:T(8,128)(2,1)} %copy-done.8, ...), custom_call_target="tpu_custom_call" | custom-call | tf_op jit(solution)/shard_map/grad/gradient/pallas_call | solution.py:287
  219.6 1.6 collective-permute-start.23
  221.2 2.9 %collective-permute-start.24 = (bf16[448,512]{1,0:T(8,128)(2,1)}, bf16[448,512]{1,0:T(8,128)(2,1)S(1)}, u32[]{:S(2)}, u32[]{:S(2)}) collective-permute-start(bf16[448,512]{1,0:T(8,128)(2,1)} %get-tuple-element.84), channel_id=1, source_target_pairs={{0,64},{32,96},{64,0},{96,32},{1,65},{33,97},{65,1},{97,33},{2,66}... | collective-permute-start | bytes 1376264 | tf_op jit(solution)/shard_map/grad/ppermute | solution.py:17
  224.9 0.7 collective-permute-start.18
  225.5 2.1 collective-permute-start.19
  227.7 5.6 %collective-permute-done.23.refs_1_ = bf16[448,512]{1,0:T(8,128)(2,1)S(1)} collective-permute-done((bf16[448,512]{1,0:T(8,128)(2,1)}, bf16[448,512]{1,0:T(8,128)(2,1)S(1)}, u32[]{:S(2)}, u32[]{:S(2)}) %collective-permute-start.23) | collective-permute-done | bytes 458784 | tf_op jit(solution)/shard_map/grad/ppermute | solution.py:17
  233.2 3.2 %collective-permute-start.20 = (bf16[448,256]{1,0:T(8,128)(2,1)S(1)}, bf16[448,256]{1,0:T(8,128)(2,1)S(1)}, u32[]{:S(2)}, u32[]{:S(2)}) collective-permute-start(bf16[448,256]{1,0:T(8,128)(2,1)S(1)} %get-tuple-element.97), channel_id=1, source_target_pairs={{0,64},{2,96},{4,0},{6,32},{32,66},{34,98},{36,2},{38,34},{64,68},... | collective-permute-start | bytes 688136 | tf_op jit(solution)/shard_map/ppermute | solution.py:364
  236.4 9.2 %collective-permute-done.24.refs_2_ = bf16[448,512]{1,0:T(8,128)(2,1)S(1)} collective-permute-done((bf16[448,512]{1,0:T(8,128)(2,1)}, bf16[448,512]{1,0:T(8,128)(2,1)S(1)}, u32[]{:S(2)}, u32[]{:S(2)}) %collective-permute-start.24) | collective-permute-done | bytes 458784 | tf_op jit(solution)/shard_map/grad/ppermute | solution.py:17
  245.8 8.0 %collective-permute-done.25.refs_3_ = bf16[448,512]{1,0:T(8,128)(2,1)S(1)} collective-permute-done((bf16[448,512]{1,0:T(8,128)(2,1)}, bf16[448,512]{1,0:T(8,128)(2,1)S(1)}, u32[]{:S(2)}, u32[]{:S(2)}) %collective-permute-start.25) | collective-permute-done | bytes 458784 | tf_op jit(solution)/shard_map/grad/ppermute | solution.py:17
  253.7 0.8 copy-done.13
  254.5 4.8 %assemble.3 = f32[512,1792]{1,0:T(8,128)} custom-call(s32[1]{0:T(128)} %bitcast.place_ref, bf16[448,512]{1,0:T(8,128)(2,1)} %get-tuple-element.82.refs_0_, bf16[448,512]{1,0:T(8,128)(2,1)} %copy-done.11, bf16[448,512]{1,0:T(8,128)(2,1)} %copy-done.12, bf16[448,512]{1,0:T(8,128)(2,1)} %copy-done.13), custom_call_target="tpu_custom_call" | custom-call | tf_op jit(solution)/shard_map/assemble/pallas_call | solution.py:318
  259.4 0.6 copy-done.14
  260.2 0.7 copy-done.17
  260.9 2.4 assemble.2
  (66 shorter events, 4.0 us)
Async XLA Ops:
  17.6 35.5 %all-to-all-start = ((bf16[4,128,2048]{2,1,0:T(8,128)(2,1)}), bf16[4,128,2048]{2,1,0:T(8,128)(2,1)S(1)}, u32[]{:S(2)}, u32[]{:S(2)}) async-start(bf16[4,128,2048]{2,1,0:T(8,128)(2,1)} %cut_tokens.1), calls=%async_computation | async-start | bytes 4194304 | tf_op jit(solution)/shard_map/move/all_to_all | solution.py:32
  22.0 142.9 %all-gather.3.cloned.1.call-start = ((), (), s32[]{:S(2)}) async-start(), calls=%async_computation.3 | async-start | bytes 18874368 | tf_op jit(solution)/shard_map/move/all_gather | solution.py:169
  22.0 15.0 %collective-permute-start = (bf16[4,128,512]{2,1,0:T(8,128)(2,1)}, bf16[4,128,512]{2,1,0:T(8,128)(2,1)S(1)}, u32[]{:S(2)}, u32[]{:S(2)}) collective-permute-start(bf16[4,128,512]{2,1,0:T(8,128)(2,1)} %get-tuple-element.51), channel_id=1, source_target_pairs={{0,2},{2,0},{4,6},{6,4},{1,3},{3,1},{5,7},{7,5},{8,10},{10,8},{12,... | collective-permute-start | bytes 1572872 | tf_op jit(solution)/shard_map/move/ppermute | solution.py:17
  23.9 26.6 %collective-permute-start.1 = (bf16[4,128,512]{2,1,0:T(8,128)(2,1)}, bf16[4,128,512]{2,1,0:T(8,128)(2,1)}, u32[]{:S(2)}, u32[]{:S(2)}) collective-permute-start(bf16[4,128,512]{2,1,0:T(8,128)(2,1)} %get-tuple-element.52), channel_id=1, source_target_pairs={{0,4},{2,6},{4,0},{6,2},{1,5},{3,7},{5,1},{7,3},{8,12},{10,14},{12... | collective-permute-start | bytes 1572872 | tf_op jit(solution)/shard_map/move/ppermute | solution.py:17
  27.5 25.6 %collective-permute-start.2 = (bf16[4,128,512]{2,1,0:T(8,128)(2,1)}, bf16[4,128,512]{2,1,0:T(8,128)(2,1)}, u32[]{:S(2)}, u32[]{:S(2)}) collective-permute-start(bf16[4,128,512]{2,1,0:T(8,128)(2,1)} %get-tuple-element.53), channel_id=1, source_target_pairs={{0,6},{2,4},{4,2},{6,0},{1,7},{3,5},{5,3},{7,1},{8,14},{10,12},{12... | collective-permute-start | bytes 1572872 | tf_op jit(solution)/shard_map/move/ppermute | solution.py:17
  37.0 26.3 %copy-start.10 = (bf16[4,128,512]{2,1,0:T(8,128)(2,1)}, bf16[4,128,512]{2,1,0:T(8,128)(2,1)S(1)}, u32[]{:S(2)}) copy-start(bf16[4,128,512]{2,1,0:T(8,128)(2,1)S(1)} %collective-permute-done.refs_1_) | copy-start | bytes 1572868
  53.1 1.3 copy-start.2
  54.4 28.8 %all-to-all-start.1 = ((bf16[4,4,128,512]{3,2,1,0:T(8,128)(2,1)}), bf16[4,4,128,512]{3,2,1,0:T(8,128)(2,1)S(1)}, u32[]{:S(2)}, u32[]{:S(2)}) async-start(bf16[4,4,128,512]{3,2,1,0:T(8,128)(2,1)} %get-tuple-element.55), calls=%async_computation.1 | async-start | bytes 4194304 | tf_op jit(solution)/shard_map/move/all_to_all | solution.py:32
  59.0 10.9 %collective-permute-start.4 = (bf16[448,256]{1,0:T(8,128)(2,1)S(1)}, bf16[448,256]{1,0:T(8,128)(2,1)S(1)}, u32[]{:S(2)}, u32[]{:S(2)}) collective-permute-start(bf16[448,256]{1,0:T(8,128)(2,1)S(1)} %get-tuple-element.102), channel_id=1, source_target_pairs={{0,64},{32,96},{64,0},{96,32},{1,65},{33,97},{65,1},{97,33},{2,66}... | collective-permute-start | bytes 688136 | tf_op jit(solution)/shard_map/move/ppermute | solution.py:17
  62.3 11.6 %collective-permute-start.5 = (bf16[448,256]{1,0:T(8,128)(2,1)S(1)}, bf16[448,256]{1,0:T(8,128)(2,1)S(1)}, u32[]{:S(2)}, u32[]{:S(2)}) collective-permute-start(bf16[448,256]{1,0:T(8,128)(2,1)S(1)} %get-tuple-element.101), channel_id=1, source_target_pairs={{0,96},{32,64},{64,32},{96,0},{1,97},{33,65},{65,33},{97,1},{2,98}... | collective-permute-start | bytes 688136 | tf_op jit(solution)/shard_map/move/ppermute | solution.py:17
  63.3 14.0 %collective-permute-start.3 = (bf16[448,256]{1,0:T(8,128)(2,1)S(1)}, bf16[448,256]{1,0:T(8,128)(2,1)S(1)}, u32[]{:S(2)}, u32[]{:S(2)}) collective-permute-start(bf16[448,256]{1,0:T(8,128)(2,1)S(1)} %get-tuple-element.103), channel_id=1, source_target_pairs={{0,32},{32,0},{64,96},{96,64},{1,33},{33,1},{65,97},{97,65},{2,34}... | collective-permute-start | bytes 688136 | tf_op jit(solution)/shard_map/move/ppermute | solution.py:17
  77.4 65.6 %copy-start.3 = (bf16[4,448,256]{2,1,0:T(8,128)(2,1)}, bf16[4,448,256]{2,1,0:T(8,128)(2,1)S(1)}, u32[]{:S(2)}) copy-start(bf16[4,448,256]{2,1,0:T(8,128)(2,1)S(1)} %pad_maximum_fusion.refs_0_) | copy-start | bytes 2752516
  83.2 1.4 copy-start.1
  84.6 33.2 %all-to-all-start.2 = ((bf16[4,4,128,512]{3,2,1,0:T(8,128)(2,1)}), bf16[4,4,128,512]{3,2,1,0:T(8,128)(2,1)S(1)}, u32[]{:S(2)}, u32[]{:S(2)}) async-start(bf16[4,4,128,512]{3,2,1,0:T(8,128)(2,1)} %stack.53), calls=%async_computation.2 | async-start | bytes 4194304 | tf_op jit(solution)/shard_map/move/all_to_all | solution.py:32
  91.3 15.1 %collective-permute-start.6 = (bf16[4,128,512]{2,1,0:T(8,128)(2,1)}, bf16[4,128,512]{2,1,0:T(8,128)(2,1)S(1)}, u32[]{:S(2)}, u32[]{:S(2)}) collective-permute-start(bf16[4,128,512]{2,1,0:T(8,128)(2,1)} %get-tuple-element.94), channel_id=1, source_target_pairs={{0,2},{2,0},{4,6},{6,4},{1,3},{3,1},{5,7},{7,5},{8,10},{10,8},{12,... | collective-permute-start | bytes 1572872 | tf_op jit(solution)/shard_map/move/ppermute | solution.py:17
  91.3 22.2 %collective-permute-start.7 = (bf16[4,128,512]{2,1,0:T(8,128)(2,1)}, bf16[4,128,512]{2,1,0:T(8,128)(2,1)}, u32[]{:S(2)}, u32[]{:S(2)}) collective-permute-start(bf16[4,128,512]{2,1,0:T(8,128)(2,1)} %get-tuple-element.93), channel_id=1, source_target_pairs={{0,4},{2,6},{4,0},{6,2},{1,5},{3,7},{5,1},{7,3},{8,12},{10,14},{12... | collective-permute-start | bytes 1572872 | tf_op jit(solution)/shard_map/move/ppermute | solution.py:17
  93.2 22.9 %collective-permute-start.8 = (bf16[4,128,512]{2,1,0:T(8,128)(2,1)}, bf16[4,128,512]{2,1,0:T(8,128)(2,1)}, u32[]{:S(2)}, u32[]{:S(2)}) collective-permute-start(bf16[4,128,512]{2,1,0:T(8,128)(2,1)} %get-tuple-element.92), channel_id=1, source_target_pairs={{0,6},{2,4},{4,2},{6,0},{1,7},{3,5},{5,3},{7,1},{8,14},{10,12},{12... | collective-permute-start | bytes 1572872 | tf_op jit(solution)/shard_map/move/ppermute | solution.py:17
  106.4 12.7 %copy-start.7 = (bf16[4,128,512]{2,1,0:T(8,128)(2,1)}, bf16[4,128,512]{2,1,0:T(8,128)(2,1)S(1)}, u32[]{:S(2)}) copy-start(bf16[4,128,512]{2,1,0:T(8,128)(2,1)S(1)} %collective-permute-done.6.refs_1_) | copy-start | bytes 1572868
  117.8 1.7 slice-start
  117.8 1.7 copy-start
  119.5 6.2 %collective-permute-start.9 = (bf16[16,128,512]{2,1,0:T(8,128)(2,1)}, bf16[16,128,512]{2,1,0:T(8,128)(2,1)}, u32[]{:S(2)}, u32[]{:S(2)}) collective-permute-start(bf16[16,128,512]{2,1,0:T(8,128)(2,1)} %constant_dynamic-update-slice_fusion), channel_id=1, source_target_pairs={{0,1},{1,0},{2,3},{3,2},{4,5},{5,4},{6,7},{7,6},{8,9},{9,8},{10,11... | collective-permute-start | bytes 6291464 | tf_op jit(solution)/shard_map/weight/ppermute | solution.py:181
  119.8 23.2 %collective-permute-start.13 = (bf16[4,448,256]{2,1,0:T(8,128)(2,1)S(1)}, bf16[4,448,256]{2,1,0:T(8,128)(2,1)S(1)}, u32[]{:S(2)}, u32[]{:S(2)}) collective-permute-start(bf16[4,448,256]{2,1,0:T(8,128)(2,1)S(1)} %pad_maximum_fusion.refs_0_), channel_id=1, source_target_pairs={{0,8},{8,0},{16,24},{24,16},{1,9},{9,1},{17,25},{25,17},{2,10},{10... | collective-permute-start | bytes 2752520 | tf_op jit(solution)/shard_map/ppermute | solution.py:17
  121.5 43.3 %collective-permute-start.14 = (bf16[4,448,256]{2,1,0:T(8,128)(2,1)S(1)}, bf16[4,448,256]{2,1,0:T(8,128)(2,1)}, u32[]{:S(2)}, u32[]{:S(2)}) collective-permute-start(bf16[4,448,256]{2,1,0:T(8,128)(2,1)S(1)} %pad_maximum_fusion.refs_0_), channel_id=1, source_target_pairs={{0,16},{8,24},{16,0},{24,8},{1,17},{9,25},{17,1},{25,9},{2,18},{10... | collective-permute-start | bytes 2752520 | tf_op jit(solution)/shard_map/ppermute | solution.py:17
  132.3 32.5 %collective-permute-start.10 = (bf16[448,512]{1,0:T(8,128)(2,1)}, bf16[448,512]{1,0:T(8,128)(2,1)S(1)}, u32[]{:S(2)}, u32[]{:S(2)}) collective-permute-start(bf16[448,512]{1,0:T(8,128)(2,1)} %get-tuple-element.68), channel_id=1, source_target_pairs={{0,2},{2,0},{4,6},{6,4},{1,3},{3,1},{5,7},{7,5},{8,10},{10,8},{12,... | collective-permute-start | bytes 1376264 | tf_op jit(solution)/shard_map/weight/ppermute | solution.py:17
  132.3 32.5 %collective-permute-start.11 = (bf16[448,512]{1,0:T(8,128)(2,1)}, bf16[448,512]{1,0:T(8,128)(2,1)S(1)}, u32[]{:S(2)}, u32[]{:S(2)}) collective-permute-start(bf16[448,512]{1,0:T(8,128)(2,1)} %get-tuple-element.69), channel_id=1, source_target_pairs={{0,4},{2,6},{4,0},{6,2},{1,5},{3,7},{5,1},{7,3},{8,12},{10,14},{12... | collective-permute-start | bytes 1376264 | tf_op jit(solution)/shard_map/weight/ppermute | solution.py:17
  136.1 28.7 %collective-permute-start.12 = (bf16[448,512]{1,0:T(8,128)(2,1)}, bf16[448,512]{1,0:T(8,128)(2,1)S(1)}, u32[]{:S(2)}, u32[]{:S(2)}) collective-permute-start(bf16[448,512]{1,0:T(8,128)(2,1)} %get-tuple-element.70), channel_id=1, source_target_pairs={{0,6},{2,4},{4,2},{6,0},{1,7},{3,5},{5,3},{7,1},{8,14},{10,12},{12... | collective-permute-start | bytes 1376264 | tf_op jit(solution)/shard_map/weight/ppermute | solution.py:17
  143.0 32.0 %copy-start.8 = (bf16[4,448,256]{2,1,0:T(8,128)(2,1)}, bf16[4,448,256]{2,1,0:T(8,128)(2,1)S(1)}, u32[]{:S(2)}) copy-start(bf16[4,448,256]{2,1,0:T(8,128)(2,1)S(1)} %collective-permute-done.13.refs_1_) | copy-start | bytes 2752516
  143.0 61.1 %collective-permute-start.22 = (bf16[4,448,256]{2,1,0:T(8,128)(2,1)S(1)}, bf16[4,448,256]{2,1,0:T(8,128)(2,1)}, u32[]{:S(2)}, u32[]{:S(2)}) collective-permute-start(bf16[4,448,256]{2,1,0:T(8,128)(2,1)S(1)} %pad_maximum_fusion.refs_0_), channel_id=1, source_target_pairs={{0,24},{8,16},{16,8},{24,0},{1,25},{9,17},{17,9},{25,1},{2,26},{10... | collective-permute-start | bytes 2752520 | tf_op jit(solution)/shard_map/ppermute | solution.py:17
  164.8 0.8 copy-start.4
  164.8 0.9 copy-start.5
  164.8 1.1 copy-start.6
  175.0 49.1 %collective-permute-start.15 = (bf16[4,448,256]{2,1,0:T(8,128)(2,1)}, bf16[4,448,256]{2,1,0:T(8,128)(2,1)S(1)}, u32[]{:S(2)}, u32[]{:S(2)}) collective-permute-start(bf16[4,448,256]{2,1,0:T(8,128)(2,1)} %get-tuple-element.76), channel_id=1, source_target_pairs={{0,16},{8,24},{16,0},{24,8},{1,17},{9,25},{17,1},{25,9},{2,18},{10... | collective-permute-start | bytes 2752520 | tf_op jit(solution)/shard_map/projected/ppermute | solution.py:17
  175.9 48.4 %collective-permute-start.16 = (bf16[4,448,256]{2,1,0:T(8,128)(2,1)}, bf16[4,448,256]{2,1,0:T(8,128)(2,1)S(1)}, u32[]{:S(2)}, u32[]{:S(2)}) collective-permute-start(bf16[4,448,256]{2,1,0:T(8,128)(2,1)} %get-tuple-element.77), channel_id=1, source_target_pairs={{0,8},{8,0},{16,24},{24,16},{1,9},{9,1},{17,25},{25,17},{2,10},{10... | collective-permute-start | bytes 2752520 | tf_op jit(solution)/shard_map/projected/ppermute | solution.py:17
  185.4 38.9 %collective-permute-start.17 = (bf16[4,448,256]{2,1,0:T(8,128)(2,1)}, bf16[4,448,256]{2,1,0:T(8,128)(2,1)S(1)}, u32[]{:S(2)}, u32[]{:S(2)}) collective-permute-start(bf16[4,448,256]{2,1,0:T(8,128)(2,1)} %get-tuple-element.78), channel_id=1, source_target_pairs={{0,24},{8,16},{16,8},{24,0},{1,25},{9,17},{17,9},{25,1},{2,26},{10... | collective-permute-start | bytes 2752520 | tf_op jit(solution)/shard_map/projected/ppermute | solution.py:17
  188.8 35.5 %copy-start.9 = (bf16[4,448,256]{2,1,0:T(8,128)(2,1)S(1)}, bf16[4,448,256]{2,1,0:T(8,128)(2,1)}, u32[]{:S(2)}) copy-start(bf16[4,448,256]{2,1,0:T(8,128)(2,1)} %get-tuple-element.75) | copy-start | bytes 2752516
  219.6 13.6 %collective-permute-start.23 = (bf16[448,512]{1,0:T(8,128)(2,1)}, bf16[448,512]{1,0:T(8,128)(2,1)S(1)}, u32[]{:S(2)}, u32[]{:S(2)}) collective-permute-start(bf16[448,512]{1,0:T(8,128)(2,1)} %get-tuple-element.83), channel_id=1, source_target_pairs={{0,32},{32,0},{64,96},{96,64},{1,33},{33,1},{65,97},{97,65},{2,34}... | collective-permute-start | bytes 1376264 | tf_op jit(solution)/shard_map/grad/ppermute | solution.py:17
  221.2 24.4 %collective-permute-start.24 = (bf16[448,512]{1,0:T(8,128)(2,1)}, bf16[448,512]{1,0:T(8,128)(2,1)S(1)}, u32[]{:S(2)}, u32[]{:S(2)}) collective-permute-start(bf16[448,512]{1,0:T(8,128)(2,1)} %get-tuple-element.84), channel_id=1, source_target_pairs={{0,64},{32,96},{64,0},{96,32},{1,65},{33,97},{65,1},{97,33},{2,66}... | collective-permute-start | bytes 1376264 | tf_op jit(solution)/shard_map/grad/ppermute | solution.py:17
  224.1 29.6 %collective-permute-start.25 = (bf16[448,512]{1,0:T(8,128)(2,1)}, bf16[448,512]{1,0:T(8,128)(2,1)S(1)}, u32[]{:S(2)}, u32[]{:S(2)}) collective-permute-start(bf16[448,512]{1,0:T(8,128)(2,1)} %get-tuple-element.85), channel_id=1, source_target_pairs={{0,96},{32,64},{64,32},{96,0},{1,97},{33,65},{65,33},{97,1},{2,98}... | collective-permute-start | bytes 1376264 | tf_op jit(solution)/shard_map/grad/ppermute | solution.py:17
  224.9 34.4 %collective-permute-start.18 = (bf16[448,256]{1,0:T(8,128)(2,1)S(1)}, bf16[448,256]{1,0:T(8,128)(2,1)S(1)}, u32[]{:S(2)}, u32[]{:S(2)}) collective-permute-start(bf16[448,256]{1,0:T(8,128)(2,1)S(1)} %get-tuple-element.99), channel_id=1, source_target_pairs={{0,0},{2,32},{4,64},{6,96},{32,2},{34,34},{36,66},{38,98},{64,4},{... | collective-permute-start | bytes 688136 | tf_op jit(solution)/shard_map/ppermute | solution.py:364
  225.5 33.8 %collective-permute-start.19 = (bf16[448,256]{1,0:T(8,128)(2,1)S(1)}, bf16[448,256]{1,0:T(8,128)(2,1)S(1)}, u32[]{:S(2)}, u32[]{:S(2)}) collective-permute-start(bf16[448,256]{1,0:T(8,128)(2,1)S(1)} %get-tuple-element.98), channel_id=1, source_target_pairs={{0,32},{2,0},{4,96},{6,64},{32,34},{34,2},{36,98},{38,66},{64,36},... | collective-permute-start | bytes 688136 | tf_op jit(solution)/shard_map/ppermute | solution.py:364
  233.2 20.5 %copy-start.11 = (bf16[448,512]{1,0:T(8,128)(2,1)}, bf16[448,512]{1,0:T(8,128)(2,1)S(1)}, u32[]{:S(2)}) copy-start(bf16[448,512]{1,0:T(8,128)(2,1)S(1)} %collective-permute-done.23.refs_1_) | copy-start | bytes 1376260
  233.2 26.1 %collective-permute-start.20 = (bf16[448,256]{1,0:T(8,128)(2,1)S(1)}, bf16[448,256]{1,0:T(8,128)(2,1)S(1)}, u32[]{:S(2)}, u32[]{:S(2)}) collective-permute-start(bf16[448,256]{1,0:T(8,128)(2,1)S(1)} %get-tuple-element.97), channel_id=1, source_target_pairs={{0,64},{2,96},{4,0},{6,32},{32,66},{34,98},{36,2},{38,34},{64,68},... | collective-permute-start | bytes 688136 | tf_op jit(solution)/shard_map/ppermute | solution.py:364
  245.6 8.1 %copy-start.12 = (bf16[448,512]{1,0:T(8,128)(2,1)}, bf16[448,512]{1,0:T(8,128)(2,1)S(1)}, u32[]{:S(2)}) copy-start(bf16[448,512]{1,0:T(8,128)(2,1)S(1)} %collective-permute-done.24.refs_2_) | copy-start | bytes 1376260
  245.6 13.7 %collective-permute-start.21 = (bf16[448,256]{1,0:T(8,128)(2,1)S(1)}, bf16[448,256]{1,0:T(8,128)(2,1)S(1)}, u32[]{:S(2)}, u32[]{:S(2)}) collective-permute-start(bf16[448,256]{1,0:T(8,128)(2,1)S(1)} %get-tuple-element.96), channel_id=1, source_target_pairs={{0,96},{2,64},{4,32},{6,0},{32,98},{34,66},{36,34},{38,2},{64,100}... | collective-permute-start | bytes 688136 | tf_op jit(solution)/shard_map/ppermute | solution.py:364
  253.7 0.8 copy-start.13
  259.3 0.7 copy-start.14
  259.3 0.8 copy-start.15
  259.3 0.8 copy-start.16
  260.2 0.7 copy-start.17
Sparse Core Ops, SparseCore 0:
  54.5 85.7 all-gather.2
